TPU v7x, 256 devices: a whole 4x4x8 slice. The times are simulated.
256 devices in a mesh: wide: 32 (over y, z), narrow: 8 (over x, core).
Axes of the slice: x: 4, y: 4, z: 8, core: 2. Of those that a mesh axis runs over, the one named last changes fastest.
Arguments:
- targets: float32 [262144, 64], P(('wide', 'narrow')), may hold values from -6 to 6
- train_features: bfloat16 [262144, 128], P(('wide', 'narrow')), may hold values from -6 to 6
- test_features: bfloat16 [8192, 128], P(('wide', 'narrow')), may hold values from -6 to 6
- left_factors: float32 [262144, 4, 128], P(('wide', 'narrow')), may hold values from -0.5 to 0.5
- right_factors: float32 [262144, 4, 128], P(('wide', 'narrow')), may hold values from -0.01171875 to 0.01171875
- capacitance: float32 [15, 256, 256], replicated, may hold values from -0.375 to 0.375
- pivots: int32 [15, 256], replicated, may hold values from 0 to 255, each once within a row
Outputs:
- solved_targets: float32 [262144, 64], P(('wide', 'narrow'))
- predictions: float32 [8192, 64], P(('wide', 'narrow'))
Inputs may be any that keep to these rules, and one draw needn't show every extreme that they name: `pivots`: each row is a permutation of 0 .. 255.
All inputs are finite; a program needn't handle non-finite values.
Results may differ from a plain program's by a relative error of at most 0.0049.
Values may be sent and summed in bfloat16 or wider, within the bound.
No kernel may reach another device: no remote copies, remote signals or barrier semaphores. Data moves between devices by JAX's collectives and lax.ppermute only.
A program may use at most 128 MiB of HBM per device.

v0:
```python
import jax
import jax.numpy as jnp
from jax import lax
from jax.sharding import PartitionSpec as P

LEVELS = 4


spread_coef = 3.0


def partner_2(value, axis, stride):
    mask = 2**stride
    pairs = [(source, source ^ mask) for source in range(lax.axis_size(axis))]
    return lax.ppermute(value, axis, pairs)


def split_up(shard, dim, count):
    lengths = shard.shape
    pieces = shard.reshape(*lengths[:dim], count, lengths[dim] // count, *lengths[dim + 1 :])
    return jnp.moveaxis(pieces, dim, 0)


def sum_at_owner(shard, axis, dim):
    count = lax.axis_size(axis)
    pieces = lax.all_to_all(split_up(shard, dim, count), axis, 0, 0, tiled=True)
    return jnp.sum(pieces.astype(jnp.float32), axis=0)


def summed_on_arrival(shard, axis, dim):
    pieces = split_up(shard, dim, lax.axis_size(axis))
    arrived = lax.all_to_all(pieces, axis, split_axis=0, concat_axis=0, tiled=True)
    return arrived.sum(axis=0)


def kernel_block(rows_in, train_features, train_sq):
    rows_float = rows_in.astype(jnp.float32)
    row_sq = jnp.sum(rows_float * rows_float, axis=1)
    inner = lax.dot_general(
        rows_in, train_features, (((1,), (1,)), ((), ())), preferred_element_type=jnp.float32
    )
    dist = row_sq[:, None] + train_sq[None, :] - 2.0 * inner
    return jnp.exp(-(spread_coef / rows_in.shape[1]) * dist).astype(jnp.bfloat16)


def blockwise(piece, handler):
    row_count = piece.shape[0]
    blocks = piece.reshape(row_count // 2048, 2048, piece.shape[1])
    result = lax.map(handler, blocks)
    return result.reshape((row_count,) + result.shape[2:])


def add_partner(values, bit_index):
    return values + partner_2(values, ("wide", "narrow"), bit_index)


def split_sums(projected, span_bits):
    for bit_index in range(0, span_bits):
        projected = add_partner(projected, bit_index)
    partner = partner_2(projected, ("wide", "narrow"), span_bits)
    return (projected, partner)


def body(targets, train_features, test_features, left_factors, right_factors, capacitance, pivots):
    position = lax.axis_index(("wide", "narrow"))
    total_dev = lax.axis_size(("wide", "narrow"))
    rank = left_factors.shape[2]
    train_float = train_features.astype(jnp.float32)
    train_sq = jnp.sum(train_float * train_float, axis=1)

    def make_kernel(rows_in):
        return kernel_block(rows_in, train_features, train_sq)

    gathered = lax.all_gather(test_features, ("wide", "narrow"), axis=0, tiled=True)
    stored = blockwise(gathered, make_kernel)
    current = targets
    for tree_level in range(1, LEVELS + 1):
        span = total_dev >> tree_level
        span_bits = span.bit_length() - 1
        child = jnp.right_shift(position, span_bits)
        first = jnp.bitwise_and(child, 1) == 0
        heap = (1 << tree_level - 1) - 1 + jnp.right_shift(child, 1)
        projected = jnp.dot(
            right_factors[:, tree_level - 1, :].T,
            current,
            precision=lax.Precision.HIGHEST,
            preferred_element_type=jnp.float32,
        )
        own, partner = split_sums(projected, span_bits)
        stacked = jnp.where(
            first, jnp.concatenate([partner, own], axis=0), jnp.concatenate([own, partner], axis=0)
        )
        permuted = jnp.take(stacked, pivots[heap], axis=0)
        solved = jnp.dot(
            capacitance[heap],
            permuted,
            precision=lax.Precision.HIGHEST,
            preferred_element_type=jnp.float32,
        )
        share = jnp.where(first, solved[:rank], solved[rank:])
        current = current - jnp.dot(
            left_factors[:, tree_level - 1, :],
            share,
            precision=lax.Precision.HIGHEST,
            preferred_element_type=jnp.float32,
        )
    weights_bf = current.astype(jnp.bfloat16)
    terms = jnp.dot(stored, weights_bf, preferred_element_type=jnp.float32)
    partial_rows = sum_at_owner(terms.astype(jnp.bfloat16), "wide", 0)
    predictions = summed_on_arrival(partial_rows, "narrow", 0)
    return (current, predictions)


def solution(mesh):
    placed = (
        P(("wide", "narrow"), None),
        P(("wide", "narrow"), None),
        P(("wide", "narrow"), None),
        P(("wide", "narrow"), None, None),
        P(("wide", "narrow"), None, None),
        P(),
        P(),
    )
    return jax.shard_map(
        body,
        mesh=mesh,
        in_specs=placed,
        out_specs=(P(("wide", "narrow"), None), P(("wide", "narrow"), None)),
        check_vma=False,
    )
```

profile of v0, /device:TPU:1, one launch (start us, length us, event | category | flops | bytes accessed | tf_op | source)
XLA Modules:
  0.0 240.4 jit_solution(12396946927468767755)
XLA Ops:
  7.2 5.9 %fusion.48 = (f32[1024,1,128]{2,1,0:T(1,128)S(1)}, f32[1024,1,128]{2,1,0:T(1,128)S(1)}, f32[1024,1,128]{2,1,0:T(1,128)S(1)}, f32[1024,1,128]{2,1,0:T(1,128)S(1)}) fusion(f32[1024,4,128]{2,1,0:T(4,128)} %param.15), kind=kLoop, calls=%fused_computation.90 | loop fusion | bytes 4194304 | tf_op jit(solution)/shard_map/slice | solution.py:84
  13.1 1.4 fusion.50
  14.5 3.3 %collective-permute-start = (f32[128,64]{0,1:T(8,128)S(1)}, f32[128,64]{0,1:T(8,128)S(1)}, u32[]{:S(2)}, u32[]{:S(2)}) collective-permute-start(f32[128,64]{0,1:T(8,128)S(1)} %fusion.50), channel_id=1, source_target_pairs={{0,1},{1,0},{2,3},{3,2},{4,5},{5,4},{6,7},{7,6},{8,9},{9,8},{10,11... | collective-permute-start | bytes 98312 | tf_op jit(solution)/shard_map/ppermute | solution.py:15
  17.8 0.9 collective-permute-done
  18.7 2.8 %collective-permute-done.1 = f32[128,64]{0,1:T(8,128)S(1)} collective-permute-done((f32[128,64]{0,1:T(8,128)S(1)}, f32[128,64]{0,1:T(8,128)S(1)}, u32[]{:S(2)}, u32[]{:S(2)}) %collective-permute-start.1) | collective-permute-done | bytes 32800 | tf_op jit(solution)/shard_map/ppermute | solution.py:15
  21.5 1.0 collective-permute-start.2
  22.5 3.2 %collective-permute-done.2 = f32[128,64]{0,1:T(8,128)S(1)} collective-permute-done((f32[128,64]{0,1:T(8,128)S(1)}, f32[128,64]{0,1:T(8,128)S(1)}, u32[]{:S(2)}, u32[]{:S(2)}) %collective-permute-start.2) | collective-permute-done | bytes 32800 | tf_op jit(solution)/shard_map/ppermute | solution.py:15
  25.7 6.6 %fusion.49 = (f32[1024,1,128]{2,1,0:T(1,128)S(1)}, f32[1024,1,128]{2,1,0:T(1,128)S(1)}, f32[1024,1,128]{2,1,0:T(1,128)}, f32[1024,1,128]{2,1,0:T(1,128)S(1)}) fusion(f32[1024,4,128]{2,1,0:T(4,128)} %param.14), kind=kLoop, calls=%fused_computation.91 | loop fusion | bytes 4194304 | tf_op jit(solution)/shard_map/slice | solution.py:102
  32.4 3.0 %collective-permute-start.4 = (f32[128,64]{0,1:T(8,128)S(1)}, f32[128,64]{0,1:T(8,128)S(1)}, u32[]{:S(2)}, u32[]{:S(2)}) collective-permute-start(f32[128,64]{0,1:T(8,128)S(1)} %add.124), channel_id=1, source_target_pairs={{0,16},{1,17},{2,18},{3,19},{4,20},{5,21},{6,22},{7,23},{8,24},{9,... | collective-permute-start | bytes 98312 | tf_op jit(solution)/shard_map/ppermute | solution.py:15
  36.7 5.4 %collective-permute-start.5 = (f32[128,64]{0,1:T(8,128)S(1)}, f32[128,64]{0,1:T(8,128)S(1)}, u32[]{:S(2)}, u32[]{:S(2)}) collective-permute-start(f32[128,64]{0,1:T(8,128)S(1)} %add.125), channel_id=1, source_target_pairs={{0,32},{1,33},{2,34},{3,35},{4,36},{5,37},{6,38},{7,39},{8,40},{9,... | collective-permute-start | bytes 98312 | tf_op jit(solution)/shard_map/ppermute | solution.py:15
  42.1 1.3 collective-permute-done.5
  43.4 1.3 collective-permute-start.6
  44.7 1.8 collective-permute-done.6
  46.6 2.5 %collective-permute-start.7 = (f32[128,64]{0,1:T(8,128)S(1)}, f32[128,64]{0,1:T(8,128)S(1)}, u32[]{:S(2)}, u32[]{:S(2)}) collective-permute-start(f32[128,64]{0,1:T(8,128)S(1)} %add.127), channel_id=1, source_target_pairs={{0,128},{1,129},{2,130},{3,131},{4,132},{5,133},{6,134},{7,135},{8... | collective-permute-start | bytes 98312 | tf_op jit(solution)/shard_map/ppermute | solution.py:15
  49.1 1.7 collective-permute-done.7
  51.7 1.4 fusion.13
  53.1 1.8 fusion.6
  55.3 7.7 %collective-permute-start.8 = (f32[128,64]{0,1:T(8,128)S(1)}, f32[128,64]{0,1:T(8,128)S(1)}, u32[]{:S(2)}, u32[]{:S(2)}) collective-permute-start(f32[128,64]{0,1:T(8,128)S(1)} %convolution_bitcast_fusion.6), channel_id=1, source_target_pairs={{0,1},{1,0},{2,3},{3,2},{4,5},{5,4},{6,7},{7,6},{8,9},{9,8},{10,11... | collective-permute-start | bytes 98312 | tf_op jit(solution)/shard_map/ppermute | solution.py:15
  63.0 0.9 collective-permute-done.8
  63.9 1.2 collective-permute-start.9
  65.1 1.6 collective-permute-done.9
  66.7 2.7 %collective-permute-start.10 = (f32[128,64]{0,1:T(8,128)S(1)}, f32[128,64]{0,1:T(8,128)S(1)}, u32[]{:S(2)}, u32[]{:S(2)}) collective-permute-start(f32[128,64]{0,1:T(8,128)S(1)} %add.131), channel_id=1, source_target_pairs={{0,4},{1,5},{2,6},{3,7},{4,0},{5,1},{6,2},{7,3},{8,12},{9,13},{10,... | collective-permute-start | bytes 98312 | tf_op jit(solution)/shard_map/ppermute | solution.py:15
  69.4 1.5 collective-permute-done.10
  71.3 2.8 %collective-permute-done.11 = f32[128,64]{0,1:T(8,128)S(1)} collective-permute-done((f32[128,64]{0,1:T(8,128)S(1)}, f32[128,64]{0,1:T(8,128)S(1)}, u32[]{:S(2)}, u32[]{:S(2)}) %collective-permute-start.11) | collective-permute-done | bytes 32800 | tf_op jit(solution)/shard_map/ppermute | solution.py:15
  74.1 2.2 collective-permute-start.12
  76.3 1.8 collective-permute-done.12
  78.1 5.4 %collective-permute-start.13 = (f32[128,64]{0,1:T(8,128)S(1)}, f32[128,64]{0,1:T(8,128)S(1)}, u32[]{:S(2)}, u32[]{:S(2)}) collective-permute-start(f32[128,64]{0,1:T(8,128)S(1)} %add.134), channel_id=1, source_target_pairs={{0,32},{1,33},{2,34},{3,35},{4,36},{5,37},{6,38},{7,39},{8,40},{9,... | collective-permute-start | bytes 98312 | tf_op jit(solution)/shard_map/ppermute | solution.py:15
  83.5 1.4 collective-permute-done.13
  84.9 1.3 collective-permute-start.14
  86.3 1.4 collective-permute-done.14
  88.5 1.4 fusion.11
  91.1 7.0 %collective-permute-start.15 = (f32[128,64]{0,1:T(8,128)S(1)}, f32[128,64]{0,1:T(8,128)S(1)}, u32[]{:S(2)}, u32[]{:S(2)}) collective-permute-start(f32[128,64]{0,1:T(8,128)S(1)} %convolution_bitcast_fusion.5), channel_id=1, source_target_pairs={{0,1},{1,0},{2,3},{3,2},{4,5},{5,4},{6,7},{7,6},{8,9},{9,8},{10,11... | collective-permute-start | bytes 98312 | tf_op jit(solution)/shard_map/ppermute | solution.py:15
  98.1 0.9 collective-permute-done.15
  98.9 0.9 collective-permute-start.16
  99.8 1.9 collective-permute-done.16
  101.7 2.5 %collective-permute-start.17 = (f32[128,64]{0,1:T(8,128)S(1)}, f32[128,64]{0,1:T(8,128)S(1)}, u32[]{:S(2)}, u32[]{:S(2)}) collective-permute-start(f32[128,64]{0,1:T(8,128)S(1)} %add.138), channel_id=1, source_target_pairs={{0,4},{1,5},{2,6},{3,7},{4,0},{5,1},{6,2},{7,3},{8,12},{9,13},{10,... | collective-permute-start | bytes 98312 | tf_op jit(solution)/shard_map/ppermute | solution.py:15
  104.2 1.8 collective-permute-done.17
  106.0 2.7 %collective-permute-done.18 = f32[128,64]{0,1:T(8,128)S(1)} collective-permute-done((f32[128,64]{0,1:T(8,128)S(1)}, f32[128,64]{0,1:T(8,128)S(1)}, u32[]{:S(2)}, u32[]{:S(2)}) %collective-permute-start.18) | collective-permute-done | bytes 32800 | tf_op jit(solution)/shard_map/ppermute | solution.py:15
  108.8 1.8 collective-permute-start.19
  110.6 2.2 collective-permute-done.19
  112.8 5.6 %collective-permute-start.20 = (f32[128,64]{0,1:T(8,128)S(1)}, f32[128,64]{0,1:T(8,128)S(1)}, u32[]{:S(2)}, u32[]{:S(2)}) collective-permute-start(f32[128,64]{0,1:T(8,128)S(1)} %add.141), channel_id=1, source_target_pairs={{0,32},{1,33},{2,34},{3,35},{4,36},{5,37},{6,38},{7,39},{8,40},{9,... | collective-permute-start | bytes 98312 | tf_op jit(solution)/shard_map/ppermute | solution.py:15
  118.4 1.6 collective-permute-done.20
  120.9 1.4 fusion.9
  123.4 5.7 %collective-permute-start.21 = (f32[128,64]{0,1:T(8,128)S(1)}, f32[128,64]{0,1:T(8,128)S(1)}, u32[]{:S(2)}, u32[]{:S(2)}) collective-permute-start(f32[128,64]{0,1:T(8,128)S(1)} %convolution_bitcast_fusion.4), channel_id=1, source_target_pairs={{0,1},{1,0},{2,3},{3,2},{4,5},{5,4},{6,7},{7,6},{8,9},{9,8},{10,11... | collective-permute-start | bytes 98312 | tf_op jit(solution)/shard_map/ppermute | solution.py:15
  129.1 0.9 collective-permute-done.21
  130.8 1.9 collective-permute-done.22
  132.7 2.7 %collective-permute-start.23 = (f32[128,64]{0,1:T(8,128)S(1)}, f32[128,64]{0,1:T(8,128)S(1)}, u32[]{:S(2)}, u32[]{:S(2)}) collective-permute-start(f32[128,64]{0,1:T(8,128)S(1)} %add.145), channel_id=1, source_target_pairs={{0,4},{1,5},{2,6},{3,7},{4,0},{5,1},{6,2},{7,3},{8,12},{9,13},{10,... | collective-permute-start | bytes 98312 | tf_op jit(solution)/shard_map/ppermute | solution.py:15
  135.5 1.5 collective-permute-done.23
  137.6 2.1 collective-permute-done.24
  139.7 2.2 collective-permute-start.25
  142.0 1.8 collective-permute-done.25
  144.6 1.4 fusion.7
  146.7 25.4 %while.10 = (s32[]{:T(128)}, bf16[4,2048,1024]{2,1,0:T(8,128)(2,1)}, bf16[4,2048,128]{2,1,0:T(8,128)(2,1)}, f32[1024]{0:T(1024)S(1)}, bf16[1024,128]{1,0:T(8,128)(2,1)S(1)}, /*index=5*/s32[]{:T(128)}) while((s32[]{:T(128)}, bf16[4,2048,1024]{2,1,0:T(8,128)(2,1)}, bf16[4,2048,128]{2,1,0:T(8,128)(2,1)}, f32[1024]{0:T(1024)S(1)}, ...), condition=%wide.region_3.5_spmd, body=%wide.region_1.4_spmd.sunk | while | flops 548141056 | bytes 5526601 | solution.py:49
  146.7 1.4 multiply_reduce_fusion.3
  148.2 4.9 %bitcast_dynamic-update-slice_fusion.2 = bf16[4,2048,1024]{2,1,0:T(8,128)(2,1)} fusion(bf16[4,2048,1024]{2,1,0:T(8,128)(2,1)} %get-tuple-element.95, s32[]{:T(128)} %get-tuple-element.94, bf16[1024,128]{1,0:T(8,128)(2,1)S(1)} %get-tuple-element.104, f32[1024]{0:T(1024)S(1)} %get-tuple-element.103, f32[2048]{0:T(1024)S(1)} %multiply_reduce_fusion.3, ...), kind=kOutput, calls=%fused_computation.5.clone.1 | convolution fusion | flops 547356672 | bytes 4994048 | tf_op jit(solution)/shard_map/while/body/eval_jaxpr/dot_general | solution.py:39
  153.1 1.4 multiply_reduce_fusion.3
  154.5 5.0 %bitcast_dynamic-update-slice_fusion.2 = bf16[4,2048,1024]{2,1,0:T(8,128)(2,1)} fusion(bf16[4,2048,1024]{2,1,0:T(8,128)(2,1)} %get-tuple-element.95, s32[]{:T(128)} %get-tuple-element.94, bf16[1024,128]{1,0:T(8,128)(2,1)S(1)} %get-tuple-element.104, f32[1024]{0:T(1024)S(1)} %get-tuple-element.103, f32[2048]{0:T(1024)S(1)} %multiply_reduce_fusion.3, ...), kind=kOutput, calls=%fused_computation.5.clone.1 | convolution fusion | flops 547356672 | bytes 4994048 | tf_op jit(solution)/shard_map/while/body/eval_jaxpr/dot_general | solution.py:39
  159.5 1.4 multiply_reduce_fusion.3
  160.9 5.0 %bitcast_dynamic-update-slice_fusion.2 = bf16[4,2048,1024]{2,1,0:T(8,128)(2,1)} fusion(bf16[4,2048,1024]{2,1,0:T(8,128)(2,1)} %get-tuple-element.95, s32[]{:T(128)} %get-tuple-element.94, bf16[1024,128]{1,0:T(8,128)(2,1)S(1)} %get-tuple-element.104, f32[1024]{0:T(1024)S(1)} %get-tuple-element.103, f32[2048]{0:T(1024)S(1)} %multiply_reduce_fusion.3, ...), kind=kOutput, calls=%fused_computation.5.clone.1 | convolution fusion | flops 547356672 | bytes 4994048 | tf_op jit(solution)/shard_map/while/body/eval_jaxpr/dot_general | solution.py:39
  165.8 1.4 multiply_reduce_fusion.3
  167.2 4.9 %bitcast_dynamic-update-slice_fusion.2 = bf16[4,2048,1024]{2,1,0:T(8,128)(2,1)} fusion(bf16[4,2048,1024]{2,1,0:T(8,128)(2,1)} %get-tuple-element.95, s32[]{:T(128)} %get-tuple-element.94, bf16[1024,128]{1,0:T(8,128)(2,1)S(1)} %get-tuple-element.104, f32[1024]{0:T(1024)S(1)} %get-tuple-element.103, f32[2048]{0:T(1024)S(1)} %multiply_reduce_fusion.3, ...), kind=kOutput, calls=%fused_computation.5.clone.1 | convolution fusion | flops 547356672 | bytes 4994048 | tf_op jit(solution)/shard_map/while/body/eval_jaxpr/dot_general | solution.py:39
  172.1 11.0 %convolution_convert_fusion = bf16[8192,64]{0,1:T(8,128)(2,1)S(1)} fusion(bf16[8192,1024]{1,0:T(8,128)(2,1)} %bitcast.81, f32[1024,64]{0,1:T(8,128)S(1)} %fusion.3), kind=kOutput, calls=%fused_computation.10 | convolution fusion | flops 1074331648 | bytes 18087936 | tf_op jit(solution)/shard_map/dot_general | solution.py:108
  183.2 28.7 %all_to_all.10 = bf16[32,256,64]{1,2,0:T(8,128)(2,1)S(1)} all-to-all(bf16[32,256,64]{1,2,0:T(8,128)(2,1)S(1)} %bitcast.83), channel_id=1, replica_groups=mesh['wide'=32,'narrow'=8] {'wide'}, dimensions={0} | all-to-all | bytes 2097152 | tf_op jit(solution)/shard_map/all_to_all | solution.py:26
  212.3 19.3 %all_to_all.11 = f32[8,1,2048]{2,1,0:T(1,128)S(1)} all-to-all(f32[8,1,2048]{2,1,0:T(1,128)S(1)} %reshape.71), channel_id=1, replica_groups=mesh['wide'=32,'narrow'=8] {'narrow'}, dimensions={0} | all-to-all | bytes 131072 | tf_op jit(solution)/shard_map/all_to_all | solution.py:32
  (76 shorter events, 12.6 us)
Async XLA Ops:
  7.2 139.6 %all-gather.2.cloned.1.call-start = ((), (), s32[]{:S(2)}) async-start(), calls=%async_computation.2 | async-start | bytes 2105344 | tf_op jit(solution)/shard_map/all_gather | solution.py:74
  14.5 4.2 %collective-permute-start = (f32[128,64]{0,1:T(8,128)S(1)}, f32[128,64]{0,1:T(8,128)S(1)}, u32[]{:S(2)}, u32[]{:S(2)}) collective-permute-start(f32[128,64]{0,1:T(8,128)S(1)} %fusion.50), channel_id=1, source_target_pairs={{0,1},{1,0},{2,3},{3,2},{4,5},{5,4},{6,7},{7,6},{8,9},{9,8},{10,11... | collective-permute-start | bytes 98312 | tf_op jit(solution)/shard_map/ppermute | solution.py:15
  18.7 2.8 %collective-permute-start.1 = (f32[128,64]{0,1:T(8,128)S(1)}, f32[128,64]{0,1:T(8,128)S(1)}, u32[]{:S(2)}, u32[]{:S(2)}) collective-permute-start(f32[128,64]{0,1:T(8,128)S(1)} %add.121), channel_id=1, source_target_pairs={{0,2},{1,3},{2,0},{3,1},{4,6},{5,7},{6,4},{7,5},{8,10},{9,11},{10,... | collective-permute-start | bytes 98312 | tf_op jit(solution)/shard_map/ppermute | solution.py:15
  21.5 4.3 %collective-permute-start.2 = (f32[128,64]{0,1:T(8,128)S(1)}, f32[128,64]{0,1:T(8,128)S(1)}, u32[]{:S(2)}, u32[]{:S(2)}) collective-permute-start(f32[128,64]{0,1:T(8,128)S(1)} %add.122), channel_id=1, source_target_pairs={{0,4},{1,5},{2,6},{3,7},{4,0},{5,1},{6,2},{7,3},{8,12},{9,13},{10,... | collective-permute-start | bytes 98312 | tf_op jit(solution)/shard_map/ppermute | solution.py:15
  25.7 6.7 %collective-permute-start.3 = (f32[128,64]{0,1:T(8,128)S(1)}, f32[128,64]{0,1:T(8,128)S(1)}, u32[]{:S(2)}, u32[]{:S(2)}) collective-permute-start(f32[128,64]{0,1:T(8,128)S(1)} %add.123), channel_id=1, source_target_pairs={{0,8},{1,9},{2,10},{3,11},{4,12},{5,13},{6,14},{7,15},{8,0},{9,1},... | collective-permute-start | bytes 98312 | tf_op jit(solution)/shard_map/ppermute | solution.py:15
  32.4 4.3 %collective-permute-start.4 = (f32[128,64]{0,1:T(8,128)S(1)}, f32[128,64]{0,1:T(8,128)S(1)}, u32[]{:S(2)}, u32[]{:S(2)}) collective-permute-start(f32[128,64]{0,1:T(8,128)S(1)} %add.124), channel_id=1, source_target_pairs={{0,16},{1,17},{2,18},{3,19},{4,20},{5,21},{6,22},{7,23},{8,24},{9,... | collective-permute-start | bytes 98312 | tf_op jit(solution)/shard_map/ppermute | solution.py:15
  36.7 6.7 %collective-permute-start.5 = (f32[128,64]{0,1:T(8,128)S(1)}, f32[128,64]{0,1:T(8,128)S(1)}, u32[]{:S(2)}, u32[]{:S(2)}) collective-permute-start(f32[128,64]{0,1:T(8,128)S(1)} %add.125), channel_id=1, source_target_pairs={{0,32},{1,33},{2,34},{3,35},{4,36},{5,37},{6,38},{7,39},{8,40},{9,... | collective-permute-start | bytes 98312 | tf_op jit(solution)/shard_map/ppermute | solution.py:15
  43.4 3.2 %collective-permute-start.6 = (f32[128,64]{0,1:T(8,128)S(1)}, f32[128,64]{0,1:T(8,128)S(1)}, u32[]{:S(2)}, u32[]{:S(2)}) collective-permute-start(f32[128,64]{0,1:T(8,128)S(1)} %add.126), channel_id=1, source_target_pairs={{0,64},{1,65},{2,66},{3,67},{4,68},{5,69},{6,70},{7,71},{8,72},{9,... | collective-permute-start | bytes 98312 | tf_op jit(solution)/shard_map/ppermute | solution.py:15
  46.6 4.3 %collective-permute-start.7 = (f32[128,64]{0,1:T(8,128)S(1)}, f32[128,64]{0,1:T(8,128)S(1)}, u32[]{:S(2)}, u32[]{:S(2)}) collective-permute-start(f32[128,64]{0,1:T(8,128)S(1)} %add.127), channel_id=1, source_target_pairs={{0,128},{1,129},{2,130},{3,131},{4,132},{5,133},{6,134},{7,135},{8... | collective-permute-start | bytes 98312 | tf_op jit(solution)/shard_map/ppermute | solution.py:15
  55.3 82.1 %copy-start.1 = (bf16[1024,128]{1,0:T(8,128)(2,1)S(1)}, bf16[1024,128]{1,0:T(8,128)(2,1)}, u32[]{:S(2)}) copy-start(bf16[1024,128]{1,0:T(8,128)(2,1)} %param.12) | copy-start | bytes 786436
  55.3 8.6 %collective-permute-start.8 = (f32[128,64]{0,1:T(8,128)S(1)}, f32[128,64]{0,1:T(8,128)S(1)}, u32[]{:S(2)}, u32[]{:S(2)}) collective-permute-start(f32[128,64]{0,1:T(8,128)S(1)} %convolution_bitcast_fusion.6), channel_id=1, source_target_pairs={{0,1},{1,0},{2,3},{3,2},{4,5},{5,4},{6,7},{7,6},{8,9},{9,8},{10,11... | collective-permute-start | bytes 98312 | tf_op jit(solution)/shard_map/ppermute | solution.py:15
  63.9 2.8 %collective-permute-start.9 = (f32[128,64]{0,1:T(8,128)S(1)}, f32[128,64]{0,1:T(8,128)S(1)}, u32[]{:S(2)}, u32[]{:S(2)}) collective-permute-start(f32[128,64]{0,1:T(8,128)S(1)} %add.130), channel_id=1, source_target_pairs={{0,2},{1,3},{2,0},{3,1},{4,6},{5,7},{6,4},{7,5},{8,10},{9,11},{10,... | collective-permute-start | bytes 98312 | tf_op jit(solution)/shard_map/ppermute | solution.py:15
  66.7 4.3 %collective-permute-start.10 = (f32[128,64]{0,1:T(8,128)S(1)}, f32[128,64]{0,1:T(8,128)S(1)}, u32[]{:S(2)}, u32[]{:S(2)}) collective-permute-start(f32[128,64]{0,1:T(8,128)S(1)} %add.131), channel_id=1, source_target_pairs={{0,4},{1,5},{2,6},{3,7},{4,0},{5,1},{6,2},{7,3},{8,12},{9,13},{10,... | collective-permute-start | bytes 98312 | tf_op jit(solution)/shard_map/ppermute | solution.py:15
  71.0 3.2 %collective-permute-start.11 = (f32[128,64]{0,1:T(8,128)S(1)}, f32[128,64]{0,1:T(8,128)S(1)}, u32[]{:S(2)}, u32[]{:S(2)}) collective-permute-start(f32[128,64]{0,1:T(8,128)S(1)} %add.132), channel_id=1, source_target_pairs={{0,8},{1,9},{2,10},{3,11},{4,12},{5,13},{6,14},{7,15},{8,0},{9,1},... | collective-permute-start | bytes 98312 | tf_op jit(solution)/shard_map/ppermute | solution.py:15
  74.1 3.9 %collective-permute-start.12 = (f32[128,64]{0,1:T(8,128)S(1)}, f32[128,64]{0,1:T(8,128)S(1)}, u32[]{:S(2)}, u32[]{:S(2)}) collective-permute-start(f32[128,64]{0,1:T(8,128)S(1)} %add.133), channel_id=1, source_target_pairs={{0,16},{1,17},{2,18},{3,19},{4,20},{5,21},{6,22},{7,23},{8,24},{9,... | collective-permute-start | bytes 98312 | tf_op jit(solution)/shard_map/ppermute | solution.py:15
  78.1 6.8 %collective-permute-start.13 = (f32[128,64]{0,1:T(8,128)S(1)}, f32[128,64]{0,1:T(8,128)S(1)}, u32[]{:S(2)}, u32[]{:S(2)}) collective-permute-start(f32[128,64]{0,1:T(8,128)S(1)} %add.134), channel_id=1, source_target_pairs={{0,32},{1,33},{2,34},{3,35},{4,36},{5,37},{6,38},{7,39},{8,40},{9,... | collective-permute-start | bytes 98312 | tf_op jit(solution)/shard_map/ppermute | solution.py:15
  84.9 2.8 %collective-permute-start.14 = (f32[128,64]{0,1:T(8,128)S(1)}, f32[128,64]{0,1:T(8,128)S(1)}, u32[]{:S(2)}, u32[]{:S(2)}) collective-permute-start(f32[128,64]{0,1:T(8,128)S(1)} %add.135), channel_id=1, source_target_pairs={{0,64},{1,65},{2,66},{3,67},{4,68},{5,69},{6,70},{7,71},{8,72},{9,... | collective-permute-start | bytes 98312 | tf_op jit(solution)/shard_map/ppermute | solution.py:15
  91.1 7.9 %collective-permute-start.15 = (f32[128,64]{0,1:T(8,128)S(1)}, f32[128,64]{0,1:T(8,128)S(1)}, u32[]{:S(2)}, u32[]{:S(2)}) collective-permute-start(f32[128,64]{0,1:T(8,128)S(1)} %convolution_bitcast_fusion.5), channel_id=1, source_target_pairs={{0,1},{1,0},{2,3},{3,2},{4,5},{5,4},{6,7},{7,6},{8,9},{9,8},{10,11... | collective-permute-start | bytes 98312 | tf_op jit(solution)/shard_map/ppermute | solution.py:15
  98.9 2.8 %collective-permute-start.16 = (f32[128,64]{0,1:T(8,128)S(1)}, f32[128,64]{0,1:T(8,128)S(1)}, u32[]{:S(2)}, u32[]{:S(2)}) collective-permute-start(f32[128,64]{0,1:T(8,128)S(1)} %add.137), channel_id=1, source_target_pairs={{0,2},{1,3},{2,0},{3,1},{4,6},{5,7},{6,4},{7,5},{8,10},{9,11},{10,... | collective-permute-start | bytes 98312 | tf_op jit(solution)/shard_map/ppermute | solution.py:15
  101.7 4.3 %collective-permute-start.17 = (f32[128,64]{0,1:T(8,128)S(1)}, f32[128,64]{0,1:T(8,128)S(1)}, u32[]{:S(2)}, u32[]{:S(2)}) collective-permute-start(f32[128,64]{0,1:T(8,128)S(1)} %add.138), channel_id=1, source_target_pairs={{0,4},{1,5},{2,6},{3,7},{4,0},{5,1},{6,2},{7,3},{8,12},{9,13},{10,... | collective-permute-start | bytes 98312 | tf_op jit(solution)/shard_map/ppermute | solution.py:15
  106.0 2.8 %collective-permute-start.18 = (f32[128,64]{0,1:T(8,128)S(1)}, f32[128,64]{0,1:T(8,128)S(1)}, u32[]{:S(2)}, u32[]{:S(2)}) collective-permute-start(f32[128,64]{0,1:T(8,128)S(1)} %add.139), channel_id=1, source_target_pairs={{0,8},{1,9},{2,10},{3,11},{4,12},{5,13},{6,14},{7,15},{8,0},{9,1},... | collective-permute-start | bytes 98312 | tf_op jit(solution)/shard_map/ppermute | solution.py:15
  108.8 4.0 %collective-permute-start.19 = (f32[128,64]{0,1:T(8,128)S(1)}, f32[128,64]{0,1:T(8,128)S(1)}, u32[]{:S(2)}, u32[]{:S(2)}) collective-permute-start(f32[128,64]{0,1:T(8,128)S(1)} %add.140), channel_id=1, source_target_pairs={{0,16},{1,17},{2,18},{3,19},{4,20},{5,21},{6,22},{7,23},{8,24},{9,... | collective-permute-start | bytes 98312 | tf_op jit(solution)/shard_map/ppermute | solution.py:15
  112.8 7.2 %collective-permute-start.20 = (f32[128,64]{0,1:T(8,128)S(1)}, f32[128,64]{0,1:T(8,128)S(1)}, u32[]{:S(2)}, u32[]{:S(2)}) collective-permute-start(f32[128,64]{0,1:T(8,128)S(1)} %add.141), channel_id=1, source_target_pairs={{0,32},{1,33},{2,34},{3,35},{4,36},{5,37},{6,38},{7,39},{8,40},{9,... | collective-permute-start | bytes 98312 | tf_op jit(solution)/shard_map/ppermute | solution.py:15
  123.4 6.5 %collective-permute-start.21 = (f32[128,64]{0,1:T(8,128)S(1)}, f32[128,64]{0,1:T(8,128)S(1)}, u32[]{:S(2)}, u32[]{:S(2)}) collective-permute-start(f32[128,64]{0,1:T(8,128)S(1)} %convolution_bitcast_fusion.4), channel_id=1, source_target_pairs={{0,1},{1,0},{2,3},{3,2},{4,5},{5,4},{6,7},{7,6},{8,9},{9,8},{10,11... | collective-permute-start | bytes 98312 | tf_op jit(solution)/shard_map/ppermute | solution.py:15
  129.9 2.8 %collective-permute-start.22 = (f32[128,64]{0,1:T(8,128)S(1)}, f32[128,64]{0,1:T(8,128)S(1)}, u32[]{:S(2)}, u32[]{:S(2)}) collective-permute-start(f32[128,64]{0,1:T(8,128)S(1)} %add.144), channel_id=1, source_target_pairs={{0,2},{1,3},{2,0},{3,1},{4,6},{5,7},{6,4},{7,5},{8,10},{9,11},{10,... | collective-permute-start | bytes 98312 | tf_op jit(solution)/shard_map/ppermute | solution.py:15
  132.7 4.3 %collective-permute-start.23 = (f32[128,64]{0,1:T(8,128)S(1)}, f32[128,64]{0,1:T(8,128)S(1)}, u32[]{:S(2)}, u32[]{:S(2)}) collective-permute-start(f32[128,64]{0,1:T(8,128)S(1)} %add.145), channel_id=1, source_target_pairs={{0,4},{1,5},{2,6},{3,7},{4,0},{5,1},{6,2},{7,3},{8,12},{9,13},{10,... | collective-permute-start | bytes 98312 | tf_op jit(solution)/shard_map/ppermute | solution.py:15
  137.0 2.8 %collective-permute-start.24 = (f32[128,64]{0,1:T(8,128)S(1)}, f32[128,64]{0,1:T(8,128)S(1)}, u32[]{:S(2)}, u32[]{:S(2)}) collective-permute-start(f32[128,64]{0,1:T(8,128)S(1)} %add.146), channel_id=1, source_target_pairs={{0,8},{1,9},{2,10},{3,11},{4,12},{5,13},{6,14},{7,15},{8,0},{9,1},... | collective-permute-start | bytes 98312 | tf_op jit(solution)/shard_map/ppermute | solution.py:15
  139.7 4.0 %collective-permute-start.25 = (f32[128,64]{0,1:T(8,128)S(1)}, f32[128,64]{0,1:T(8,128)S(1)}, u32[]{:S(2)}, u32[]{:S(2)}) collective-permute-start(f32[128,64]{0,1:T(8,128)S(1)} %add.147), channel_id=1, source_target_pairs={{0,16},{1,17},{2,18},{3,19},{4,20},{5,21},{6,22},{7,23},{8,24},{9,... | collective-permute-start | bytes 98312 | tf_op jit(solution)/shard_map/ppermute | solution.py:15
  146.7 25.5 %copy-start = (f32[1024,64]{0,1:T(8,128)}, f32[1024,64]{0,1:T(8,128)S(1)}, u32[]{:S(2)}) copy-start(f32[1024,64]{0,1:T(8,128)S(1)} %fusion.3) | copy-start | bytes 786436
Sparse Core Ops, SparseCore 0:
  22.6 107.0 all-gather.1
where the time goes:
time: 241 us; the launch traced here: 240 us
  starting transfers between devices  67.3 us (28%)
  blocking collectives  48 us (20%)
  waiting for transfers between devices  42.9 us (18%)
  matrix products  42.8 us (18%)
  local copies, waits for them, and re-layouts  17.7 us (7%)
  between operations  14.3 us (6%)
  other arithmetic  7.57 us (3%)
    ppermute x26, starting transfers between devices, partner_2(): return lax.ppermute(value, axis, pairs)  67.3 us
    ppermute x26, waiting for transfers between devices, partner_2(): return lax.ppermute(value, axis, pairs)  42.8 us
    all_to_all x1, blocking collectives, sum_at_owner(): pieces = lax.all_to_all(split_up(shard, dim, count), axis, 0, 0, tiled=True)  28.7 us
    dot_general x4, matrix products, kernel_block(): lax.dot_general(rows_in, train_features, (((1,), (1,)), ((), ())), prefer...  19.8 us
    all_to_all x1, blocking collectives, summed_on_arrival(): lax.all_to_all(pieces, axis, split_axis=0, concat_axis=0, tiled=True)  19.3 us
    dot_general x1, matrix products, body(): terms = jnp.dot(stored, weights_bf, preferred_element_type=jnp.float32)  11 us
    slice x1, local copies, waits for them, and re-layouts, body(): left_factors[:, tree_level - 1, :]  6.64 us
    slice x1, local copies, waits for them, and re-layouts, body(): right_factors[:, tree_level - 1, :]  5.9 us
  transfers between devices with their start and end apart: 27, of which 25 were waited for; matrix products, arithmetic and copies ran while one was open for 9% of the time, Pallas kernels for 0%

commit v1 on v0

v1 whole, which is shorter than its diff:
```python
import math

import jax
import jax.numpy as jnp
from jax import lax
from jax.experimental import pallas as pl
from jax.experimental.pallas import tpu as pltpu
from jax.sharding import Mesh, PartitionSpec as P

LEVELS = 4
RANK = 128
FEAT = 128
TARGETS = 64
POINTS = 1024
SPREAD = 3.0
CUTS = (0, 8, 32, 72, 128)

f32 = jnp.float32
bf16 = jnp.bfloat16
NT = (((1,), (1,)), ((), ()))
NN = (((1,), (0,)), ((), ()))


def params(limit=48):
    return pltpu.CompilerParams(vmem_limit_bytes=limit * 1024 * 1024)


def split2(value):
    high = value.astype(bf16)
    return high, (value - high.astype(f32)).astype(bf16)


def dot3(a, b, dims):
    def one(p, q):
        return lax.dot_general(p, q, dims, preferred_element_type=f32)

    return one(a[0], b[0]) + (one(a[0], b[1]) + one(a[1], b[0]))


def gram_kernel(targets_ref, left_ref, right_ref, tests_ref, out_ref, upper, lower):
    step = pl.program_id(0)
    count = targets_ref.shape[1]

    def level(ref, index):
        return ref[pl.ds(index, count, stride=LEVELS), :]

    rows = jnp.concatenate([targets_ref[...]] + [level(left_ref, k).T for k in range(3)], axis=0)
    high, low = split2(rows)
    right = [split2(level(right_ref, k)) for k in range(4)]
    pair = lambda i, j: tuple(jnp.concatenate([right[i][p], right[j][p]], axis=1) for p in (0, 1))
    first = dot3((high[:192], low[:192]), pair(0, 1), NN)
    second = dot3((high, low), pair(2, 3), NN)

    @pl.when(step == 0)
    def _():
        upper[...] = first
        lower[...] = second

    @pl.when(step > 0)
    def _():
        upper[...] += first
        lower[...] += second

    @pl.when(step == pl.num_programs(0) - 1)
    def _():
        for n in range(8):
            block = jnp.concatenate(
                [
                    upper[8 * n : 8 * n + 8, :RANK],
                    upper[24 * n : 24 * n + 24, RANK:],
                    lower[40 * n : 40 * n + 40, :RANK],
                    lower[56 * n : 56 * n + 56, RANK:],
                ],
                axis=0,
            )
            out_ref[n, :128] = block.astype(bf16)
            out_ref[n, 128:] = tests_ref[...]


def gram(targets_t, left, right, tests):
    chunk = 256
    return pl.pallas_call(
        gram_kernel,
        grid=(POINTS // chunk,),
        in_specs=[
            pl.BlockSpec((TARGETS, chunk), lambda i: (0, i)),
            pl.BlockSpec((LEVELS * chunk, RANK), lambda i: (i, 0)),
            pl.BlockSpec((LEVELS * chunk, RANK), lambda i: (i, 0)),
            pl.BlockSpec((32, FEAT), lambda i: (0, 0)),
        ],
        out_specs=pl.BlockSpec((8, 160, RANK), lambda i: (0, 0, 0)),
        out_shape=jax.ShapeDtypeStruct((8, 160, RANK), bf16),
        scratch_shapes=[pltpu.VMEM((192, 256), f32), pltpu.VMEM((448, 256), f32)],
        compiler_params=params(),
        name="gram",
    )(targets_t, left, right, tests)


def block_sum_kernel(where, in_ref, out_ref):
    core = where[8]
    total = in_ref[0, :128].astype(f32)
    for n in range(1, 8):
        total += in_ref[n, :128].astype(f32)
    total = total.astype(bf16)
    tests = [in_ref[2 * x + core, 128:] for x in range(4)]
    for n in range(8):
        out_ref[n, :128] = total
        for x in range(4):
            out_ref[n, 128 + 32 * x : 160 + 32 * x] = tests[x]


def block_sum(where, arrived):
    return pl.pallas_call(
        block_sum_kernel,
        grid_spec=pltpu.PrefetchScalarGridSpec(
            num_scalar_prefetch=1,
            grid=(1,),
            in_specs=[pl.BlockSpec((8, 160, RANK), lambda i, w: (0, 0, 0))],
            out_specs=pl.BlockSpec((8, 256, RANK), lambda i, w: (0, 0, 0)),
        ),
        out_shape=jax.ShapeDtypeStruct((8, 256, RANK), bf16),
        compiler_params=params(),
        name="block_sum",
    )(where, arrived)


def plane_sum_kernel(where, in_ref, send_ref, near_ref, tests_ref):
    z = where[9]
    pair = jnp.right_shift(z, 1)

    def rows(index):
        return in_ref[index, :128].astype(f32)

    whole = [rows(k) for k in range(8)]
    below = (whole[0] + whole[1]) + (whole[2] + whole[3])
    above = (whole[4] + whole[5]) + (whole[6] + whole[7])
    send = (below + above)[:32].astype(bf16)
    for k in range(4):
        send_ref[k] = send
    odd, even = 2 * jnp.bitwise_or(pair, 1), 2 * jnp.bitwise_and(pair, 2)
    near_ref[0, :40] = above[32:72]
    near_ref[1, :40] = below[32:72]
    near_ref[0, 40:] = (rows(odd) + rows(odd + 1))[72:]
    near_ref[1, 40:] = (rows(even) + rows(even + 1))[72:]
    for k in range(8):
        tests_ref[128 * k : 128 * k + 128] = in_ref[k, 128:]


def plane_sum(where, arrived):
    return pl.pallas_call(
        plane_sum_kernel,
        grid_spec=pltpu.PrefetchScalarGridSpec(
            num_scalar_prefetch=1,
            grid=(1,),
            in_specs=[pl.BlockSpec((8, 256, RANK), lambda i, w: (0, 0, 0))],
            out_specs=[
                pl.BlockSpec((4, 32, RANK), lambda i, w: (0, 0, 0)),
                pl.BlockSpec((2, 96, RANK), lambda i, w: (0, 0, 0)),
                pl.BlockSpec((1024, FEAT), lambda i, w: (0, 0)),
            ],
        ),
        out_shape=[
            jax.ShapeDtypeStruct((4, 32, RANK), bf16),
            jax.ShapeDtypeStruct((2, 96, RANK), f32),
            jax.ShapeDtypeStruct((1024, FEAT), bf16),
        ],
        compiler_params=params(),
        name="plane_sum",
    )(where, arrived)


def node_kernel(where, far_ref, near_ref, *refs):
    caps, pivots, out_ref = refs[:4], refs[4:8], refs[8]
    y = where[10]

    def far(index):
        return far_ref[index].astype(f32)

    stacks = [
        ((far(2) + far(3))[:8], (far(0) + far(1))[:8]),
        (far(jnp.bitwise_or(y, 1))[8:], far(jnp.bitwise_and(y, 2))[8:]),
        (near_ref[0, :40], near_ref[1, :40]),
        (near_ref[0, 40:], near_ref[1, 40:]),
    ]
    solved = []
    for level in range(LEVELS):
        stacked = split2(jnp.concatenate(stacks[level], axis=1))
        source = lax.broadcasted_iota(jnp.int32, (256, 256), 0)
        picks = jnp.where(source == pivots[level][0], 1.0, 0.0).astype(bf16)
        moved = [
            lax.dot_general(piece, picks, NN, preferred_element_type=f32).astype(bf16)
            for piece in stacked
        ]
        solved.append(dot3(moved, split2(caps[level][0]), NT))
    block = jnp.concatenate(solved, axis=0).astype(bf16)
    for n in range(8):
        out_ref[n] = block


def node_solve(where, far, near, capacitance, pivots):
    cap_specs = [
        pl.BlockSpec((1, RANK, 2 * RANK), lambda i, w, k=k: (w[k], w[4 + k], 0)) for k in range(4)
    ]
    pivot_specs = [
        pl.BlockSpec((1, 1, 2 * RANK), lambda i, w, k=k: (w[k], 0, 0)) for k in range(4)
    ]
    return pl.pallas_call(
        node_kernel,
        grid_spec=pltpu.PrefetchScalarGridSpec(
            num_scalar_prefetch=1,
            grid=(1,),
            in_specs=[
                pl.BlockSpec((4, 32, RANK), lambda i, w: (0, 0, 0)),
                pl.BlockSpec((2, 96, RANK), lambda i, w: (0, 0, 0)),
            ]
            + cap_specs
            + pivot_specs,
            out_specs=pl.BlockSpec((8, 128, RANK), lambda i, w: (0, 0, 0)),
        ),
        out_shape=jax.ShapeDtypeStruct((8, 128, RANK), bf16),
        compiler_params=params(),
        name="node_solve",
    )(where, far, near, *([capacitance] * 4), *([pivots] * 4))


def update_kernel(pieces_ref, targets_ref, left_ref, out_ref, weights_ref, shares_high, shares_low):
    count = targets_ref.shape[1]

    @pl.when(pl.program_id(0) == 0)
    def _():
        pieces = [pieces_ref[n].astype(f32) for n in range(8)]
        shares = []
        for level in range(LEVELS):
            rows = jnp.concatenate([p[CUTS[level] : CUTS[level + 1]] for p in pieces], axis=0)
            share = rows[:TARGETS]
            for k in range(level):
                begin = TARGETS + RANK * k
                share -= dot3(shares[k], split2(rows[begin : begin + RANK]), NN)
            shares.append(split2(share))
        shares_high[...] = jnp.concatenate([s[0] for s in shares], axis=1)
        shares_low[...] = jnp.concatenate([s[1] for s in shares], axis=1)

    left = [split2(left_ref[pl.ds(k, count, stride=LEVELS), :]) for k in range(LEVELS)]
    joined = [jnp.concatenate([part[p] for part in left], axis=1) for p in (0, 1)]
    value = targets_ref[...] - dot3((shares_high[...], shares_low[...]), joined, NT)
    out_ref[...] = value
    weights_ref[...] = value.astype(bf16)


def update(pieces, targets_t, left):
    chunk = 256
    return pl.pallas_call(
        update_kernel,
        grid=(POINTS // chunk,),
        in_specs=[
            pl.BlockSpec((8, 128, RANK), lambda i: (0, 0, 0)),
            pl.BlockSpec((TARGETS, chunk), lambda i: (0, i)),
            pl.BlockSpec((LEVELS * chunk, RANK), lambda i: (i, 0)),
        ],
        out_specs=[
            pl.BlockSpec((TARGETS, chunk), lambda i: (0, i)),
            pl.BlockSpec((TARGETS, chunk), lambda i: (0, i)),
        ],
        out_shape=[
            jax.ShapeDtypeStruct((TARGETS, POINTS), f32),
            jax.ShapeDtypeStruct((TARGETS, POINTS), bf16),
        ],
        scratch_shapes=[
            pltpu.VMEM((TARGETS, LEVELS * RANK), bf16),
            pltpu.VMEM((TARGETS, LEVELS * RANK), bf16),
        ],
        compiler_params=params(),
        name="update",
    )(pieces, targets_t, left)


def widened(points, norm_at, one_at):
    value = points.astype(f32)
    norm = -0.5 * jnp.sum(value * value, axis=1, keepdims=True)
    high = norm.astype(bf16).astype(f32)
    middle = (norm - high).astype(bf16).astype(f32)
    low = norm - high - middle
    lane = lax.broadcasted_iota(jnp.int32, points.shape, 1)
    extra = jnp.where((lane >= one_at) & (lane < one_at + 3), 1.0, 0.0)
    for k, piece in enumerate((high, middle, low)):
        extra = jnp.where(lane == norm_at + k, piece, extra)
    return jnp.concatenate([points, extra.astype(bf16)], axis=1)


def predict_kernel(where, *refs):
    tests, own_ref, other_ref = refs[:4], refs[4], refs[5]
    own_w, other_w, out_ref, train, weights, block = refs[6:]
    turn, part = pl.program_id(0), pl.program_id(1)

    @pl.when((turn == 0) & (part == 0))
    def _():
        for k, (ref, w) in enumerate(((own_ref, own_w), (other_ref, other_w))):
            for j in range(4):
                at = 1024 * k + 256 * j
                train[at : at + 256] = widened(ref[256 * j : 256 * j + 256], 0, 3)
                weights[at : at + 256] = w[:, 256 * j : 256 * j + 256].astype(f32).T.astype(bf16)

    for k in range(4):

        @pl.when(turn == k)
        def _():
            block[...] = widened(tests[k][...], 3, 0)

    scale = 2.0 * SPREAD / FEAT * math.log2(math.e)
    total = jnp.zeros((256, TARGETS), f32)
    for j in range(8):
        at = 256 * j
        inner = lax.dot_general(block[...], train[at : at + 256], NT, preferred_element_type=f32)
        kernel = jnp.exp2(inner * scale).astype(bf16)
        total += lax.dot_general(kernel, weights[at : at + 256], NN, preferred_element_type=f32)
    for k in range(8):
        rows = [total[32 * k + 16 * h : 32 * k + 16 * h + 16] for h in (0, 1)]
        out_ref[k] = jnp.concatenate(rows, axis=1).astype(bf16)


def predict(where, tests, features, other_features, weights, other_weights):
    def test_spec(k):
        def at(i, j, w):
            return (jnp.where(i == k, j, jnp.where(i < k, 0, 3)), 0)

        return pl.BlockSpec((256, FEAT), at)

    whole = lambda shape: pl.BlockSpec(shape, lambda i, j, w: (0,) * len(shape))
    return pl.pallas_call(
        predict_kernel,
        grid_spec=pltpu.PrefetchScalarGridSpec(
            num_scalar_prefetch=1,
            grid=(4, 4),
            in_specs=[test_spec(k) for k in range(4)]
            + [whole((POINTS, FEAT))] * 2
            + [whole((TARGETS, POINTS))] * 2,
            out_specs=pl.BlockSpec(
                (8, 16, 128), lambda i, j, w: (4 * jnp.bitwise_xor(w[10], i) + j, 0, 0)
            ),
            scratch_shapes=[
                pltpu.VMEM((2 * POINTS, 2 * FEAT), bf16),
                pltpu.VMEM((2 * POINTS, TARGETS), bf16),
                pltpu.VMEM((256, 2 * FEAT), bf16),
            ],
        ),
        out_shape=jax.ShapeDtypeStruct((128, 16, 128), bf16),
        compiler_params=params(),
        name="predict",
    )(where, *tests, features, other_features, weights, other_weights)


def final_kernel(in_ref, out_ref):
    total = in_ref[0].astype(f32)
    for k in range(1, 128):
        total += in_ref[k].astype(f32)
    out_ref[:16] = total[:, :TARGETS]
    out_ref[16:] = total[:, TARGETS:]


def final_sum(arrived):
    return pl.pallas_call(
        final_kernel,
        out_shape=jax.ShapeDtypeStruct((32, TARGETS), f32),
        compiler_params=params(),
        name="final_sum",
    )(arrived)


def exchange(blocks, axes):
    return lax.all_to_all(blocks, axes, 0, 0, tiled=True)


def flipped(value, axis, mask):
    return lax.ppermute(value, axis, [(s, s ^ mask) for s in range(lax.axis_size(axis))])


def body(targets, train_features, test_features, left_factors, right_factors, capacitance, pivots):
    y, z, core = lax.axis_index("y"), lax.axis_index("z"), lax.axis_index("core")
    leaf = 4 * y + jnp.right_shift(z, 1)
    children = [jnp.right_shift(leaf, 3 - k) for k in range(LEVELS)]
    nodes = [(1 << k) - 1 + jnp.right_shift(children[k], 1) for k in range(LEVELS)]
    sides = [jnp.bitwise_and(child, 1) for child in children]
    where = jnp.stack([*nodes, *sides, core, z, y]).astype(jnp.int32)

    left = left_factors.reshape(LEVELS * POINTS, RANK)
    right = right_factors.reshape(LEVELS * POINTS, RANK)
    targets_t = targets.T

    other_features = flipped(train_features, "core", 1)
    sums = gram(targets_t, left, right, test_features)
    sums = block_sum(where, exchange(sums, ("x", "core")))
    send, near, tests = plane_sum(where, exchange(sums, "z"))
    all_tests = [tests] + [flipped(tests, "y", k) for k in (1, 2, 3)]
    far = exchange(send, "y")
    pieces = node_solve(where, far, near, capacitance, pivots.reshape(-1, 1, 2 * RANK))
    solved, weights = update(exchange(pieces, ("x", "core")), targets_t, left)
    other_weights = flipped(weights, "core", 1)
    terms = predict(where, all_tests, train_features, other_features, weights, other_weights)
    predictions = final_sum(exchange(terms, ("y", "z", "x")))
    return solved.T, predictions


def solution(mesh):
    axes = ("y", "z", "x", "core")
    fine = Mesh(mesh.devices.reshape(4, 8, 4, 2), axes)
    rows = P(axes, None)
    factors = P(axes, None, None)
    return jax.shard_map(
        body,
        mesh=fine,
        in_specs=(rows, rows, rows, factors, factors, P(), P()),
        out_specs=(rows, rows),
        check_vma=False,
    )
```

time: 241 us -> 130 us (0.54)
  starting transfers between devices: 67.3 us -> 22.8 us
  matrix products: 42.8 us -> 0 us
  Pallas kernels: 0 us -> 31.9 us
  waiting for transfers between devices: 42.9 us -> 19.4 us
  between operations: 14.3 us -> 0.68 us
  local copies, waits for them, and re-layouts: 17.7 us -> 7.05 us
  other arithmetic: 7.57 us -> 0 us
    ppermute x26 -> x5, starting transfers between devices: 67.3 us -> 4.09 us  [flipped(): lax.ppermute(value, axis, [(s, s ^ mask) for s in range(lax.axis_size(axi...]
    dot_general x17 -> x0, matrix products: 42.8 us -> none  [the longest x4 19.8 us: kernel_block(): lax.dot_general(rows_in, train_features, (((1,), (1,)), ((), ())), prefer...]
    ppermute x26 -> x5, waiting for transfers between devices: 42.8 us -> 4.58 us  [flipped(): lax.ppermute(value, axis, [(s, s ^ mask) for s in range(lax.axis_size(axi...]
    pallas_call x0 -> x7, Pallas kernels: none -> 31.9 us  [the longest x1 21.5 us: predict(): pl.pallas_call(predict_kernel, grid_spec=pltpu.PrefetchScalarGridSpec(num...]
    all_to_all x0 -> x3, starting transfers between devices: none -> 18.7 us  [exchange(): return lax.all_to_all(blocks, axes, 0, 0, tiled=True)]
    all_to_all x0 -> x3, waiting for transfers between devices: none -> 14.8 us  [exchange(): return lax.all_to_all(blocks, axes, 0, 0, tiled=True)]
    slice x2 -> x0, local copies, waits for them, and re-layouts: 12.5 us -> none  [the longest x1 6.64 us: body(): left_factors[:, tree_level - 1, :]]
    unnamed x6 -> x18, local copies, waits for them, and re-layouts: 0.23 us -> 6.95 us
  transfers between devices with their start and end apart: 27 -> 8, of which waited for: 25 -> 5; matrix products, arithmetic and copies ran while one was open for 9% -> 0% of each run, Pallas kernels for 0% -> 2%
where the time goes in v1:
time: 130 us; the launch traced here: 128 us
  blocking collectives  46 us (35%)
  Pallas kernels  31.9 us (25%)
  starting transfers between devices  22.8 us (18%)
  waiting for transfers between devices  19.4 us (15%)
  local copies, waits for them, and re-layouts  7.05 us (5%)
    all_to_all x2, blocking collectives, exchange(): return lax.all_to_all(blocks, axes, 0, 0, tiled=True)  46 us
    pallas_call x1, Pallas kernels, predict(): pl.pallas_call(predict_kernel, grid_spec=pltpu.PrefetchScalarGridSpec(num...  21.5 us
    all_to_all x3, starting transfers between devices, exchange(): return lax.all_to_all(blocks, axes, 0, 0, tiled=True)  18.7 us
    all_to_all x3, waiting for transfers between devices, exchange(): return lax.all_to_all(blocks, axes, 0, 0, tiled=True)  14.8 us
    unnamed x18, local copies, waits for them, and re-layouts  6.95 us
    ppermute x5, waiting for transfers between devices, flipped(): lax.ppermute(value, axis, [(s, s ^ mask) for s in range(lax.axis_size(axi...  4.58 us
    ppermute x5, starting transfers between devices, flipped(): lax.ppermute(value, axis, [(s, s ^ mask) for s in range(lax.axis_size(axi...  4.09 us
    pallas_call x1, Pallas kernels, gram(): pl.pallas_call(gram_kernel, grid=(POINTS // chunk,), in_specs=[pl.BlockSp...  2.95 us
  transfers between devices with their start and end apart: 8, of which 5 were waited for; matrix products, arithmetic and copies ran while one was open for 0% of the time, Pallas kernels for 2%

profile of v1, /device:TPU:1, one launch (start us, length us, event | category | flops | bytes accessed | tf_op | source)
XLA Modules:
  0.0 127.9 jit_solution(11050831286243124680)
XLA Ops:
  0.6 0.0 copy-start.1
  0.6 1.6 %copy-done.1 = f32[1024,4,128]{2,1,0:T(4,128)S(1)} copy-done((f32[1024,4,128]{2,1,0:T(4,128)S(1)}, f32[1024,4,128]{2,1,0:T(4,128)}, u32[]{:S(2)}) %copy-start.1) | copy-done | bytes 2097176
  2.2 0.0 copy-start.3
  2.2 1.6 %copy-done.3 = f32[1024,4,128]{2,1,0:T(4,128)S(1)} copy-done((f32[1024,4,128]{2,1,0:T(4,128)S(1)}, f32[1024,4,128]{2,1,0:T(4,128)}, u32[]{:S(2)}) %copy-start.3) | copy-done | bytes 2097176
  3.8 0.0 copy-start.4
  3.8 0.9 copy-done.4
  4.8 0.0 copy-start.7
  4.8 0.7 copy-done.7
  5.5 2.9 %gram.1 = bf16[8,160,128]{2,1,0:T(8,128)(2,1)} custom-call(f32[64,1024]{1,0:T(8,128)S(1)} %bitcast.18, f32[4096,128]{1,0:T(8,128)S(1)} %bitcast.15, f32[4096,128]{1,0:T(8,128)S(1)} %bitcast.17, bf16[32,128]{1,0:T(8,128)(2,1)S(1)} %copy-done.7), custom_call_target="tpu_custom_call" | custom-call | tf_op jit(solution)/shard_map/gram/pallas_call | solution.py:82
  8.4 0.0 copy-start.8
  8.4 6.7 %all-to-all-start = ((bf16[8,160,128]{2,1,0:T(8,128)(2,1)}), bf16[8,160,128]{2,1,0:T(8,128)(2,1)S(1)}, u32[]{:S(2)}, u32[]{:S(2)}) async-start(bf16[8,160,128]{2,1,0:T(8,128)(2,1)} %gram.1), calls=%async_computation | async-start | bytes 655360 | tf_op jit(solution)/shard_map/all_to_all | solution.py:370
  15.1 0.1 stack.47.where
  15.2 7.1 %all-to-all-done.in_ref = bf16[8,160,128]{2,1,0:T(8,128)(2,1)S(1)} async-done(((bf16[8,160,128]{2,1,0:T(8,128)(2,1)}), bf16[8,160,128]{2,1,0:T(8,128)(2,1)S(1)}, u32[]{:S(2)}, u32[]{:S(2)}) %all-to-all-start) | async-done | bytes 327712 | tf_op jit(solution)/shard_map/all_to_all | solution.py:370
  22.3 0.6 block_sum.1
  22.9 22.6 %all_to_all.25.in_ref = bf16[8,256,128]{2,1,0:T(8,128)(2,1)S(1)} all-to-all(bf16[8,256,128]{2,1,0:T(8,128)(2,1)S(1)} %block_sum.1), channel_id=1, replica_groups=mesh['y'=4,'z'=8,'x'=4,'core'=2] {'z'}, dimensions={0} | all-to-all | bytes 1048576 | tf_op jit(solution)/shard_map/all_to_all | solution.py:370
  45.5 1.2 plane_sum.1
  46.7 4.2 %all-to-all-start.2 = ((bf16[4,32,128]{2,1,0:T(8,128)(2,1)}), bf16[4,32,128]{2,1,0:T(8,128)(2,1)S(1)}, u32[]{:S(2)}, u32[]{:S(2)}) async-start(bf16[4,32,128]{2,1,0:T(8,128)(2,1)} %get-tuple-element.7), calls=%async_computation.2 | async-start | bytes 65536 | tf_op jit(solution)/shard_map/all_to_all | solution.py:370
  50.8 0.0 copy-done.8
  50.9 4.3 %all-to-all-done.2.far_ref = bf16[4,32,128]{2,1,0:T(8,128)(2,1)S(1)} async-done(((bf16[4,32,128]{2,1,0:T(8,128)(2,1)}), bf16[4,32,128]{2,1,0:T(8,128)(2,1)S(1)}, u32[]{:S(2)}, u32[]{:S(2)}) %all-to-all-start.2) | async-done | bytes 32800 | tf_op jit(solution)/shard_map/all_to_all | solution.py:370
  55.1 0.0 copy-start
  55.1 2.1 %copy-done = f32[15,256,256]{2,1,0:T(8,128)S(1)} copy-done((f32[15,256,256]{2,1,0:T(8,128)S(1)}, f32[15,256,256]{2,1,0:T(8,128)}, u32[]{:S(2)}) %copy-start) | copy-done | bytes 3932184
  57.3 0.0 copy-start.6
  57.3 0.0 copy-start.2
  57.3 0.0 copy-start.5
  57.3 2.0 %node_solve.1 = bf16[8,128,128]{2,1,0:T(8,128)(2,1)} custom-call(s32[11]{0:T(128)S(1)} %stack.47.where, bf16[4,32,128]{2,1,0:T(8,128)(2,1)S(1)} %all-to-all-done.2.far_ref, f32[2,96,128]{2,1,0:T(8,128)S(1)} %get-tuple-element.8.near_ref, f32[15,256,256]{2,1,0:T(8,128)S(1)} %copy-done, f32[15,256,256]{2,1,0:T(8,128)S(1)} %copy-done, ...), custom_call_target="tpu_custom_call" | custom-call | tf_op jit(solution)/shard_map/node_solve/pallas_call | solution.py:207
  59.2 7.8 %all-to-all-start.3 = ((bf16[8,128,128]{2,1,0:T(8,128)(2,1)}), bf16[8,128,128]{2,1,0:T(8,128)(2,1)S(1)}, u32[]{:S(2)}, u32[]{:S(2)}) async-start(bf16[8,128,128]{2,1,0:T(8,128)(2,1)} %node_solve.1), calls=%async_computation.3 | async-start | bytes 524288 | tf_op jit(solution)/shard_map/all_to_all | solution.py:370
  67.0 0.0 copy-done.6
  67.0 0.2 collective-permute-start.3
  67.2 0.9 collective-permute-start.2
  68.1 1.2 collective-permute-start.1
  69.3 1.2 collective-permute-start
  70.5 3.5 %all-to-all-done.3.pieces_ref = bf16[8,128,128]{2,1,0:T(8,128)(2,1)S(1)} async-done(((bf16[8,128,128]{2,1,0:T(8,128)(2,1)}), bf16[8,128,128]{2,1,0:T(8,128)(2,1)S(1)}, u32[]{:S(2)}, u32[]{:S(2)}) %all-to-all-start.3) | async-done | bytes 262176 | tf_op jit(solution)/shard_map/all_to_all | solution.py:370
  73.9 0.0 copy-done.2
  73.9 0.0 copy-done.5
  73.9 2.9 %update.1 = (f32[64,1024]{1,0:T(8,128)}, bf16[64,1024]{1,0:T(8,128)(2,1)S(1)}) custom-call(bf16[8,128,128]{2,1,0:T(8,128)(2,1)S(1)} %all-to-all-done.3.pieces_ref, f32[64,1024]{1,0:T(8,128)S(1)} %bitcast.19, f32[4096,128]{1,0:T(8,128)S(1)} %bitcast.16), custom_call_target="tpu_custom_call" | custom-call | tf_op jit(solution)/shard_map/update/pallas_call | solution.py:252
  76.9 0.6 collective-permute-start.4
  77.5 0.0 collective-permute-done.3.refs_5_
  77.5 4.2 %collective-permute-done.2.refs_3_ = bf16[1024,128]{1,0:T(8,128)(2,1)} collective-permute-done((bf16[1024,128]{1,0:T(8,128)(2,1)S(1)}, bf16[1024,128]{1,0:T(8,128)(2,1)}, u32[]{:S(2)}, u32[]{:S(2)}) %collective-permute-start.2) | collective-permute-done | bytes 262176 | tf_op jit(solution)/shard_map/ppermute | solution.py:374
  81.7 0.0 collective-permute-done.1.refs_2_
  81.7 0.3 collective-permute-done.refs_1_
  82.1 0.0 collective-permute-done.4.refs_7_
  82.1 21.5 %predict.1 = bf16[128,16,128]{2,1,0:T(8,128)(2,1)S(1)} custom-call(s32[11]{0:T(128)S(1)} %stack.47.where, bf16[1024,128]{1,0:T(8,128)(2,1)S(1)} %get-tuple-element.10.refs_0_, bf16[1024,128]{1,0:T(8,128)(2,1)} %collective-permute-done.refs_1_, bf16[1024,128]{1,0:T(8,128)(2,1)} %collective-permute-done.1.refs_2_, ...), custom_call_target="tpu_custom_call" | custom-call | tf_op jit(solution)/shard_map/predict/pallas_call | solution.py:329
  103.6 23.4 %all_to_all.26.in_ref = bf16[128,16,128]{2,1,0:T(8,128)(2,1)S(1)} all-to-all(bf16[128,16,128]{2,1,0:T(8,128)(2,1)S(1)} %predict.1), channel_id=1, replica_groups=mesh['y'=4,'z'=8,'x'=4,'core'=2] {'y','z','x'}, dimensions={0} | all-to-all | bytes 1048576 | tf_op jit(solution)/shard_map/all_to_all | solution.py:370
  127.0 0.8 final_sum.1
  (1 shorter events, 0.0 us)
Async XLA Ops:
  0.6 1.6 %copy-start.1 = (f32[1024,4,128]{2,1,0:T(4,128)S(1)}, f32[1024,4,128]{2,1,0:T(4,128)}, u32[]{:S(2)}) copy-start(f32[1024,4,128]{2,1,0:T(4,128)} %param.10) | copy-start | bytes 6291460
  2.2 1.6 %copy-start.3 = (f32[1024,4,128]{2,1,0:T(4,128)S(1)}, f32[1024,4,128]{2,1,0:T(4,128)}, u32[]{:S(2)}) copy-start(f32[1024,4,128]{2,1,0:T(4,128)} %param.11) | copy-start | bytes 6291460
  3.8 0.9 copy-start.4
  4.8 0.7 copy-start.7
  8.4 42.4 %copy-start.8 = (s32[15,256]{1,0:T(8,128)S(1)}, s32[15,256]{1,0:T(8,128)}, u32[]{:S(2)}) copy-start(s32[15,256]{1,0:T(8,128)} %param.13) | copy-start | bytes 46084
  8.4 13.8 %all-to-all-start = ((bf16[8,160,128]{2,1,0:T(8,128)(2,1)}), bf16[8,160,128]{2,1,0:T(8,128)(2,1)S(1)}, u32[]{:S(2)}, u32[]{:S(2)}) async-start(bf16[8,160,128]{2,1,0:T(8,128)(2,1)} %gram.1), calls=%async_computation | async-start | bytes 655360 | tf_op jit(solution)/shard_map/all_to_all | solution.py:370
  46.7 8.5 %all-to-all-start.2 = ((bf16[4,32,128]{2,1,0:T(8,128)(2,1)}), bf16[4,32,128]{2,1,0:T(8,128)(2,1)S(1)}, u32[]{:S(2)}, u32[]{:S(2)}) async-start(bf16[4,32,128]{2,1,0:T(8,128)(2,1)} %get-tuple-element.7), calls=%async_computation.2 | async-start | bytes 65536 | tf_op jit(solution)/shard_map/all_to_all | solution.py:370
  55.1 2.1 %copy-start = (f32[15,256,256]{2,1,0:T(8,128)S(1)}, f32[15,256,256]{2,1,0:T(8,128)}, u32[]{:S(2)}) copy-start(f32[15,256,256]{2,1,0:T(8,128)} %refs_3_.1) | copy-start | bytes 11796484
  57.3 9.8 %copy-start.6 = (bf16[1024,128]{1,0:T(8,128)(2,1)S(1)}, bf16[1024,128]{1,0:T(8,128)(2,1)}, u32[]{:S(2)}) copy-start(bf16[1024,128]{1,0:T(8,128)(2,1)} %refs_4_.1) | copy-start | bytes 786436
  57.3 16.7 %copy-start.2 = (f32[1024,4,128]{2,1,0:T(4,128)S(1)}, f32[1024,4,128]{2,1,0:T(4,128)}, u32[]{:S(2)}) copy-start(f32[1024,4,128]{2,1,0:T(4,128)} %param.10) | copy-start | bytes 6291460
  57.3 16.7 %copy-start.5 = (f32[1024,64]{0,1:T(8,128)S(1)}, f32[1024,64]{0,1:T(8,128)}, u32[]{:S(2)}) copy-start(f32[1024,64]{0,1:T(8,128)} %param.7) | copy-start | bytes 786436
  59.2 14.7 %all-to-all-start.3 = ((bf16[8,128,128]{2,1,0:T(8,128)(2,1)}), bf16[8,128,128]{2,1,0:T(8,128)(2,1)S(1)}, u32[]{:S(2)}, u32[]{:S(2)}) async-start(bf16[8,128,128]{2,1,0:T(8,128)(2,1)} %node_solve.1), calls=%async_computation.3 | async-start | bytes 524288 | tf_op jit(solution)/shard_map/all_to_all | solution.py:370
  67.0 10.5 %collective-permute-start.3 = (bf16[1024,128]{1,0:T(8,128)(2,1)S(1)}, bf16[1024,128]{1,0:T(8,128)(2,1)S(1)}, u32[]{:S(2)}, u32[]{:S(2)}) collective-permute-start(bf16[1024,128]{1,0:T(8,128)(2,1)S(1)} %copy-done.6), channel_id=1, source_target_pairs={{0,1},{1,0},{2,3},{3,2},{4,5},{5,4},{6,7},{7,6},{8,9},{9,8},{10,11... | collective-permute-start | bytes 786440 | tf_op jit(solution)/shard_map/ppermute | solution.py:374
  67.2 14.5 %collective-permute-start.2 = (bf16[1024,128]{1,0:T(8,128)(2,1)S(1)}, bf16[1024,128]{1,0:T(8,128)(2,1)}, u32[]{:S(2)}, u32[]{:S(2)}) collective-permute-start(bf16[1024,128]{1,0:T(8,128)(2,1)S(1)} %get-tuple-element.10.refs_0_), channel_id=1, source_target_pairs={{0,192},{64,128},{128,64},{192,0},{1,193},{65,129},{129,65},{193,1... | collective-permute-start | bytes 786440 | tf_op jit(solution)/shard_map/ppermute | solution.py:374
  68.1 13.6 %collective-permute-start.1 = (bf16[1024,128]{1,0:T(8,128)(2,1)S(1)}, bf16[1024,128]{1,0:T(8,128)(2,1)}, u32[]{:S(2)}, u32[]{:S(2)}) collective-permute-start(bf16[1024,128]{1,0:T(8,128)(2,1)S(1)} %get-tuple-element.10.refs_0_), channel_id=1, source_target_pairs={{0,128},{64,192},{128,0},{192,64},{1,129},{65,193},{129,1},{193,65... | collective-permute-start | bytes 786440 | tf_op jit(solution)/shard_map/ppermute | solution.py:374
  69.3 12.8 %collective-permute-start = (bf16[1024,128]{1,0:T(8,128)(2,1)S(1)}, bf16[1024,128]{1,0:T(8,128)(2,1)}, u32[]{:S(2)}, u32[]{:S(2)}) collective-permute-start(bf16[1024,128]{1,0:T(8,128)(2,1)S(1)} %get-tuple-element.10.refs_0_), channel_id=1, source_target_pairs={{0,64},{64,0},{128,192},{192,128},{1,65},{65,1},{129,193},{193,129... | collective-permute-start | bytes 786440 | tf_op jit(solution)/shard_map/ppermute | solution.py:374
  76.9 5.2 %collective-permute-start.4 = (bf16[64,1024]{1,0:T(8,128)(2,1)S(1)}, bf16[64,1024]{1,0:T(8,128)(2,1)S(1)}, u32[]{:S(2)}, u32[]{:S(2)}) collective-permute-start(bf16[64,1024]{1,0:T(8,128)(2,1)S(1)} %get-tuple-element.11.refs_6_), channel_id=1, source_target_pairs={{0,1},{1,0},{2,3},{3,2},{4,5},{5,4},{6,7},{7,6},{8,9},{9,8},{10,11... | collective-permute-start | bytes 393224 | tf_op jit(solution)/shard_map/ppermute | solution.py:374

commit v2 on v1

v2 whole, which is shorter than its diff:
```python
import functools
import math

import jax
import jax.numpy as jnp
from jax import lax
from jax.experimental import pallas as pl
from jax.experimental.pallas import tpu as pltpu
from jax.sharding import Mesh, PartitionSpec as P

LEVELS = 4
RANK = 128
FEAT = 128
TARGETS = 64
POINTS = 1024
SPREAD = 3.0
CUTS = (0, 8, 32, 72, 128)

f32 = jnp.float32
bf16 = jnp.bfloat16
NT = (((1,), (1,)), ((), ()))
NN = (((1,), (0,)), ((), ()))


def params(limit=12):
    return pltpu.CompilerParams(vmem_limit_bytes=limit * 1024 * 1024)


def split2(value):
    high = value.astype(bf16)
    return high, (value - high.astype(f32)).astype(bf16)


def dot3(a, b, dims):
    def one(p, q):
        return lax.dot_general(p, q, dims, preferred_element_type=f32)

    return one(a[0], b[0]) + (one(a[0], b[1]) + one(a[1], b[0]))


def gram_kernel(targets_hbm, left_hbm, right_hbm, out_ref, targets, left, right, upper, lower, sems):
    count = targets.shape[2]
    steps = targets.shape[0]
    loads = []
    for k in range(steps):
        rows = pl.ds(LEVELS * count * k, LEVELS * count)
        pairs = (
            (left_hbm.at[rows], left.at[k]),
            (right_hbm.at[rows], right.at[k]),
            (targets_hbm.at[:, pl.ds(count * k, count)], targets.at[k]),
        )
        loads.append([pltpu.make_async_copy(*p, sems.at[3 * k + n]) for n, p in enumerate(pairs)])
        for load in loads[k]:
            load.start()

    for k in range(steps):
        for load in loads[k]:
            load.wait()

        def level(ref, index):
            return ref[k, pl.ds(index, count, stride=LEVELS), :]

        rows = jnp.concatenate([targets[k]] + [level(left, n).T for n in range(3)], axis=0)
        high, low = split2(rows)
        parts = [split2(level(right, n)) for n in range(LEVELS)]
        pair = lambda i, j: tuple(jnp.concatenate([parts[i][p], parts[j][p]], axis=1) for p in (0, 1))
        first = dot3((high[:192], low[:192]), pair(0, 1), NN)
        second = dot3((high, low), pair(2, 3), NN)
        if k == 0:
            upper[...] = first
            lower[...] = second
        else:
            upper[...] += first
            lower[...] += second

    for n in range(8):
        block = jnp.concatenate(
            [
                upper[8 * n : 8 * n + 8, :RANK],
                upper[24 * n : 24 * n + 24, RANK:],
                lower[40 * n : 40 * n + 40, :RANK],
                lower[56 * n : 56 * n + 56, RANK:],
            ],
            axis=0,
        )
        out_ref[n] = block.astype(bf16)


def gram(targets_t, left, right):
    chunk = 256
    steps = POINTS // chunk
    return pl.pallas_call(
        gram_kernel,
        in_specs=[pl.BlockSpec(memory_space=pltpu.HBM)] * 3,
        out_specs=pl.BlockSpec(memory_space=pltpu.VMEM),
        out_shape=jax.ShapeDtypeStruct((8, 128, RANK), bf16),
        scratch_shapes=[
            pltpu.VMEM((steps, TARGETS, chunk), f32),
            pltpu.VMEM((steps, LEVELS * chunk, RANK), f32),
            pltpu.VMEM((steps, LEVELS * chunk, RANK), f32),
            pltpu.VMEM((192, 256), f32),
            pltpu.VMEM((448, 256), f32),
            pltpu.SemaphoreType.DMA((3 * steps,)),
        ],
        compiler_params=params(60),
        name="gram",
    )(targets_t, left, right)


def block_sum_kernel(in_ref, tests_ref, out_ref):
    total = in_ref[0].astype(f32)
    for n in range(1, 8):
        total += in_ref[n].astype(f32)
    total = total.astype(bf16)
    for n in range(8):
        out_ref[n, :128] = total
        out_ref[n, 128:] = tests_ref[...]


def block_sum(arrived, tests):
    return pl.pallas_call(
        block_sum_kernel,
        out_shape=jax.ShapeDtypeStruct((8, 160, RANK), bf16),
        compiler_params=params(),
        name="block_sum",
    )(arrived, tests)


def plane_sum_kernel(where, in_ref, send_ref, near_ref):
    z = where[8]
    pair = jnp.right_shift(z, 1)

    def rows(index):
        return in_ref[index, :128].astype(f32)

    whole = [rows(k) for k in range(8)]
    below = (whole[0] + whole[1]) + (whole[2] + whole[3])
    above = (whole[4] + whole[5]) + (whole[6] + whole[7])
    send = (below + above)[:32].astype(bf16)
    for k in range(4):
        send_ref[k, :32] = send
        for j in range(8):
            send_ref[k, 32 + 32 * j : 64 + 32 * j] = in_ref[j, 128:]
    odd, even = 2 * jnp.bitwise_or(pair, 1), 2 * jnp.bitwise_and(pair, 2)
    near_ref[0, :40] = above[32:72]
    near_ref[1, :40] = below[32:72]
    near_ref[0, 40:] = (rows(odd) + rows(odd + 1))[72:]
    near_ref[1, 40:] = (rows(even) + rows(even + 1))[72:]


def plane_sum(where, arrived):
    return pl.pallas_call(
        plane_sum_kernel,
        grid_spec=pltpu.PrefetchScalarGridSpec(
            num_scalar_prefetch=1,
            grid=(1,),
            in_specs=[pl.BlockSpec((8, 160, RANK), lambda i, w: (0, 0, 0))],
            out_specs=[
                pl.BlockSpec((4, 288, RANK), lambda i, w: (0, 0, 0)),
                pl.BlockSpec((2, 96, RANK), lambda i, w: (0, 0, 0)),
            ],
        ),
        out_shape=[
            jax.ShapeDtypeStruct((4, 288, RANK), bf16),
            jax.ShapeDtypeStruct((2, 96, RANK), f32),
        ],
        compiler_params=params(),
        name="plane_sum",
    )(where, arrived)


def node_kernel(where, far_ref, near_ref, capacitance, *refs):
    pivots, out_ref, caps, sems = refs
    loads = [
        pltpu.make_async_copy(
            capacitance.at[where[k], pl.ds(pl.multiple_of(RANK * where[4 + k], RANK), RANK)],
            caps.at[k],
            sems.at[k],
        )
        for k in range(LEVELS)
    ]
    for load in loads:
        load.start()
    y = where[9]

    def far(index):
        return far_ref[index, :32].astype(f32)

    stacks = [
        ((far(2) + far(3))[:8], (far(0) + far(1))[:8]),
        (far(jnp.bitwise_or(y, 1))[8:], far(jnp.bitwise_and(y, 2))[8:]),
        (near_ref[0, :40], near_ref[1, :40]),
        (near_ref[0, 40:], near_ref[1, 40:]),
    ]
    solved = []
    for level in range(LEVELS):
        stacked = split2(jnp.concatenate(stacks[level], axis=1))
        source = lax.broadcasted_iota(jnp.int32, (256, 256), 0)
        picks = jnp.where(source == pivots[pl.ds(where[level], 1), :], 1.0, 0.0).astype(bf16)
        moved = [
            lax.dot_general(piece, picks, NN, preferred_element_type=f32).astype(bf16)
            for piece in stacked
        ]
        loads[level].wait()
        solved.append(dot3(moved, split2(caps[level]), NT))
    block = jnp.concatenate(solved, axis=0).astype(bf16)
    for n in range(8):
        out_ref[n] = block


def node_solve(where, far, near, capacitance, pivots):
    return pl.pallas_call(
        node_kernel,
        grid_spec=pltpu.PrefetchScalarGridSpec(
            num_scalar_prefetch=1,
            grid=(1,),
            in_specs=[
                pl.BlockSpec((4, 288, RANK), lambda i, w: (0, 0, 0)),
                pl.BlockSpec((2, 96, RANK), lambda i, w: (0, 0, 0)),
                pl.BlockSpec(memory_space=pltpu.HBM),
                pl.BlockSpec((15, 2 * RANK), lambda i, w: (0, 0)),
            ],
            out_specs=pl.BlockSpec((8, 128, RANK), lambda i, w: (0, 0, 0)),
            scratch_shapes=[
                pltpu.VMEM((LEVELS, RANK, 2 * RANK), f32),
                pltpu.SemaphoreType.DMA((LEVELS,)),
            ],
        ),
        out_shape=jax.ShapeDtypeStruct((8, 128, RANK), bf16),
        compiler_params=params(52),
        name="node_solve",
    )(where, far, near, capacitance, pivots)


def update_kernel(
    pieces_ref, targets_ref, left_ref, mark, out_ref, weights_ref, shares_high, shares_low
):
    del mark
    count = targets_ref.shape[1]

    @pl.when(pl.program_id(0) == 0)
    def _():
        pieces = [pieces_ref[n].astype(f32) for n in range(8)]
        shares = []
        for level in range(LEVELS):
            rows = jnp.concatenate([p[CUTS[level] : CUTS[level + 1]] for p in pieces], axis=0)
            share = rows[:TARGETS]
            for k in range(level):
                begin = TARGETS + RANK * k
                share -= dot3(shares[k], split2(rows[begin : begin + RANK]), NN)
            shares.append(split2(share))
        shares_high[...] = jnp.concatenate([s[0] for s in shares], axis=1)
        shares_low[...] = jnp.concatenate([s[1] for s in shares], axis=1)

    left = [split2(left_ref[pl.ds(k, count, stride=LEVELS), :]) for k in range(LEVELS)]
    joined = [jnp.concatenate([part[p] for part in left], axis=1) for p in (0, 1)]
    value = targets_ref[...] - dot3((shares_high[...], shares_low[...]), joined, NT)
    out_ref[...] = value
    rounded = value.astype(bf16)
    for k in range(4):
        weights_ref[k] = rounded


def update(pieces, targets_t, left, mark):
    chunk = 512
    return pl.pallas_call(
        update_kernel,
        grid=(POINTS // chunk,),
        in_specs=[
            pl.BlockSpec((8, 128, RANK), lambda i: (0, 0, 0)),
            pl.BlockSpec((TARGETS, chunk), lambda i: (0, i)),
            pl.BlockSpec((LEVELS * chunk, RANK), lambda i: (i, 0)),
            pl.BlockSpec(memory_space=pl.ANY),
        ],
        out_specs=[
            pl.BlockSpec((TARGETS, chunk), lambda i: (0, i)),
            pl.BlockSpec((4, TARGETS, chunk), lambda i: (0, 0, i)),
        ],
        out_shape=[
            jax.ShapeDtypeStruct((TARGETS, POINTS), f32),
            jax.ShapeDtypeStruct((4, TARGETS, POINTS), bf16),
        ],
        scratch_shapes=[
            pltpu.VMEM((TARGETS, LEVELS * RANK), bf16),
            pltpu.VMEM((TARGETS, LEVELS * RANK), bf16),
        ],
        compiler_params=params(),
        name="update",
    )(pieces, targets_t, left, mark)


def widened(points, norm_at, one_at):
    value = points.astype(f32)
    norm = -0.5 * jnp.sum(value * value, axis=1, keepdims=True)
    high = norm.astype(bf16).astype(f32)
    middle = (norm - high).astype(bf16).astype(f32)
    low = norm - high - middle
    lane = lax.broadcasted_iota(jnp.int32, points.shape, 1)
    extra = jnp.where((lane >= one_at) & (lane < one_at + 3), 1.0, 0.0)
    for k, piece in enumerate((high, middle, low)):
        extra = jnp.where(lane == norm_at + k, piece, extra)
    return jnp.concatenate([points, extra.astype(bf16)], axis=1)


def block_kernel(tests_ref, *refs):
    features, (out, mark, tests, points, train, slots, sems) = refs[:4], refs[4:]
    mark[...] = jnp.zeros_like(mark)
    loads = [
        pltpu.make_async_copy(features[j], points.at[j], sems.at[j]) for j in range(4)
    ]
    for load in loads:
        load.start()
    for k in range(4):
        tests[256 * k : 256 * k + 256] = widened(tests_ref[k, 32:], 3, 0)
    scale = 2.0 * SPREAD / FEAT * math.log2(math.e)
    stores = []
    for j in range(4):
        loads[j].wait()
        for q in range(4):
            rows = slice(256 * q, 256 * q + 256)
            train[rows] = widened(points[j, rows], 0, 3)
            for i in range(2):
                columns = slice(512 * i, 512 * i + 512)
                inner = lax.dot_general(
                    train[rows], tests[columns], NT, preferred_element_type=f32
                )
                slots[j, rows, columns] = jnp.exp2(inner * scale).astype(bf16)
            part = pl.ds(256 * q, 256)
            stores.append(
                pltpu.make_async_copy(
                    slots.at[j, part], out.at[j, part], sems.at[4 + 4 * j + q]
                )
            )
            stores[-1].start()
    for store in stores:
        store.wait()


def kernel_block(tests, features):
    return pl.pallas_call(
        block_kernel,
        in_specs=[pl.BlockSpec(memory_space=pltpu.VMEM)]
        + [pl.BlockSpec(memory_space=pl.ANY)] * 4,
        out_specs=[pl.BlockSpec(memory_space=pl.ANY), pl.BlockSpec(memory_space=pltpu.VMEM)],
        out_shape=[jax.ShapeDtypeStruct((4, POINTS, 1024), bf16), jax.ShapeDtypeStruct((8, 128), f32)],
        scratch_shapes=[
            pltpu.VMEM((1024, 2 * FEAT), bf16),
            pltpu.VMEM((4, POINTS, FEAT), bf16),
            pltpu.VMEM((POINTS, 2 * FEAT), bf16),
            pltpu.VMEM((4, POINTS, 1024), bf16),
            pltpu.SemaphoreType.DMA((20,)),
        ],
        compiler_params=params(51),
        cost_estimate=pl.CostEstimate(
            flops=2 * 4 * POINTS * 1024 * 256, bytes_accessed=10 << 20, transcendentals=4 << 20
        ),
        name="kernel_block",
    )(tests, *features)


def apply_kernel(where, *refs, last):
    x = where[10]
    if last:
        block, weights_ref, before_ref, out_ref, total, slots, sems = refs
    else:
        block, weights_ref, _, total, slots, sems = refs
    loads = []
    for j in range(4):
        for q in range(4):
            part = pl.ds(256 * q, 256)
            loads.append(
                pltpu.make_async_copy(block.at[j, part], slots.at[j, part], sems.at[4 * j + q])
            )
            loads[-1].start()
    for j in range(4):
        for load in loads[4 * j : 4 * j + 4]:
            load.wait()
        for i in range(4):
            columns = slice(256 * i, 256 * i + 256)
            part = lax.dot_general(
                weights_ref[jnp.bitwise_xor(x, j)], slots[j, :, columns], NN, preferred_element_type=f32
            )
            if j == 0:
                total[:, columns] = part + before_ref[:, columns] if last else part
            else:
                total[:, columns] += part
    if last:
        for i in range(4):
            terms = total[:, 256 * i : 256 * i + 256].T
            for k in range(8):
                rows = [terms[32 * k + 16 * h : 32 * k + 16 * h + 16] for h in (0, 1)]
                out_ref[8 * i + k] = jnp.concatenate(rows, axis=1).astype(bf16)


def apply_block(where, block, weights, before=None, mark=None):
    vmem = pl.BlockSpec(memory_space=pltpu.VMEM)
    last = before is not None
    total = pltpu.VMEM((TARGETS, 1024), f32)
    return pl.pallas_call(
        functools.partial(apply_kernel, last=last),
        in_specs=[pl.BlockSpec(memory_space=pltpu.SMEM), pl.BlockSpec(memory_space=pl.ANY), vmem]
        + [vmem if last else pl.BlockSpec(memory_space=pl.ANY)],
        out_specs=vmem,
        out_shape=jax.ShapeDtypeStruct((32, 16, 128) if last else (TARGETS, 1024), bf16 if last else f32),
        scratch_shapes=[total] * last
        + [pltpu.VMEM((4, POINTS, 1024), bf16), pltpu.SemaphoreType.DMA((16,))],
        compiler_params=params(51),
        cost_estimate=pl.CostEstimate(
            flops=2 * 4 * POINTS * 1024 * 256, bytes_accessed=9 << 20, transcendentals=0
        ),
        name="apply_block",
    )(where, block, weights, before if last else mark)


def final_kernel(in_ref, out_ref):
    total = in_ref[0].astype(f32)
    for k in range(1, 32):
        total += in_ref[k].astype(f32)
    out_ref[:16] = total[:, :TARGETS]
    out_ref[16:] = total[:, TARGETS:]


def final_sum(arrived):
    return pl.pallas_call(
        final_kernel,
        out_shape=jax.ShapeDtypeStruct((32, TARGETS), f32),
        compiler_params=params(),
        name="final_sum",
    )(arrived)


def exchange(blocks, axes):
    return lax.all_to_all(blocks, axes, 0, 0, tiled=True)


def flipped(value, axis, mask):
    return lax.ppermute(value, axis, [(s, s ^ mask) for s in range(lax.axis_size(axis))])


def body(targets, train_features, test_features, left_factors, right_factors, capacitance, pivots):
    y, z = lax.axis_index("y"), lax.axis_index("z")
    leaf = 4 * y + jnp.right_shift(z, 1)
    children = [jnp.right_shift(leaf, 3 - k) for k in range(LEVELS)]
    nodes = [(1 << k) - 1 + jnp.right_shift(children[k], 1) for k in range(LEVELS)]
    sides = [jnp.bitwise_and(child, 1) for child in children]
    where = jnp.stack([*nodes, *sides, z, y, lax.axis_index("x")]).astype(jnp.int32)

    left = left_factors.reshape(LEVELS * POINTS, RANK)
    right = right_factors.reshape(LEVELS * POINTS, RANK)
    targets_t = targets.T

    arrived = exchange(gram(targets_t, left, right), ("x", "core"))
    arrived, own = lax.optimization_barrier((arrived, train_features))
    own = [own] + [flipped(own, "x", k) for k in (1, 2, 3)]
    other = [flipped(part, "core", 1) for part in own]
    planes = exchange(block_sum(arrived, test_features), "z")
    send, near = plane_sum(where, planes)
    far = exchange(send, "y")
    pieces = node_solve(where, far, near, capacitance, pivots)
    pieces = exchange(pieces, ("x", "core"))
    own_block, own_mark = kernel_block(far, own)
    solved, weights = update(pieces, targets_t, left, own_mark)
    weights = exchange(weights, "x")
    other_block, other_mark = kernel_block(far, other)
    weights, other_mark = lax.optimization_barrier((weights, other_mark))
    other_weights = flipped(weights, "core", 1)
    terms = apply_block(where, own_block, weights, mark=other_mark)
    terms = apply_block(where, other_block, other_weights, before=terms)
    predictions = final_sum(exchange(terms, ("y", "z")))
    return solved.T, predictions


def solution(mesh):
    axes = ("y", "z", "x", "core")
    fine = Mesh(mesh.devices.reshape(4, 8, 4, 2), axes)
    rows = P(axes, None)
    factors = P(axes, None, None)
    return jax.shard_map(
        body,
        mesh=fine,
        in_specs=(rows, rows, rows, factors, factors, P(), P()),
        out_specs=(rows, rows),
        check_vma=False,
    )
```

time: 130 us -> 105 us (0.81); the launches traced: 128 us -> 104 us
  blocking collectives: 46 us -> 35 us
  waiting for transfers between devices: 19.4 us -> 10.9 us
  local copies, waits for them, and re-layouts: 7.05 us -> 0.11 us
  starting transfers between devices: 22.8 us -> 25.6 us
    all_to_all x2 -> x3, blocking collectives: 46 us -> 35 us  [exchange(): return lax.all_to_all(blocks, axes, 0, 0, tiled=True)]
    unnamed x18 -> x10, local copies, waits for them, and re-layouts: 6.95 us -> 0.02 us
    ppermute x5 -> x8, waiting for transfers between devices: 4.58 us -> 0.02 us  [flipped(): lax.ppermute(value, axis, [(s, s ^ mask) for s in range(lax.axis_size(axi...]
    all_to_all x3, waiting for transfers between devices: 14.8 us -> 10.9 us  [exchange(): return lax.all_to_all(blocks, axes, 0, 0, tiled=True)]
    ppermute x5 -> x8, starting transfers between devices: 4.09 us -> 6.72 us  [flipped(): lax.ppermute(value, axis, [(s, s ^ mask) for s in range(lax.axis_size(axi...]
    pallas_call x3 -> x6, Pallas kernels: 25.1 us -> 24.8 us  [the longest x2 10.4 us: kernel_block(): pl.pallas_call(block_kernel, in_specs=[pl.BlockSpec(memory_space=pltpu.VM...]
  transfers between devices with their start and end apart: 8 -> 11, of which waited for: 5 -> 3; matrix products, arithmetic and copies ran while one was open for 0% -> 0% of each run, Pallas kernels for 2% -> 20%
where the time goes in v2:
time: 105 us; the launch traced here: 104 us
  blocking collectives  35 us (33%)
  Pallas kernels  31.8 us (30%)
  starting transfers between devices  25.6 us (24%)
  waiting for transfers between devices  10.9 us (10%)
    all_to_all x3, blocking collectives, exchange(): return lax.all_to_all(blocks, axes, 0, 0, tiled=True)  35 us
    all_to_all x3, starting transfers between devices, exchange(): return lax.all_to_all(blocks, axes, 0, 0, tiled=True)  18.9 us
    all_to_all x3, waiting for transfers between devices, exchange(): return lax.all_to_all(blocks, axes, 0, 0, tiled=True)  10.9 us
    pallas_call x2, Pallas kernels, kernel_block(): pl.pallas_call(block_kernel, in_specs=[pl.BlockSpec(memory_space=pltpu.VM...  10.4 us
    pallas_call x2, Pallas kernels, apply_block(): pl.pallas_call(functools.partial(apply_kernel, last=last), in_specs=[pl.B...  9.39 us
    ppermute x8, starting transfers between devices, flipped(): lax.ppermute(value, axis, [(s, s ^ mask) for s in range(lax.axis_size(axi...  6.72 us
    pallas_call x1, Pallas kernels, gram(): pl.pallas_call(gram_kernel, in_specs=[pl.BlockSpec(memory_space=pltpu.HBM...  4.23 us
    pallas_call x1, Pallas kernels, node_solve(): pl.pallas_call(node_kernel, grid_spec=pltpu.PrefetchScalarGridSpec(num_sc...  3.16 us
  transfers between devices with their start and end apart: 11, of which 3 were waited for; matrix products, arithmetic and copies ran while one was open for 0% of the time, Pallas kernels for 20%

profile of v2, /device:TPU:1, one launch (start us, length us, event | category | flops | bytes accessed | tf_op | source)
XLA Modules:
  0.0 104.2 jit_solution(17199361590936688986)
XLA Ops:
  0.6 0.0 copy-start.4
  0.6 0.0 copy-start.3
  0.7 0.0 copy-start.2
  0.7 4.2 %gram.1 = bf16[8,128,128]{2,1,0:T(8,128)(2,1)} custom-call(f32[64,1024]{1,0:T(8,128)} %bitcast.17, f32[4096,128]{1,0:T(8,128)} %bitcast.15, f32[4096,128]{1,0:T(8,128)} %bitcast.19), custom_call_target="tpu_custom_call" | custom-call | tf_op jit(solution)/shard_map/gram/pallas_call | solution.py:92
  4.9 13.1 %all_to_all.30.in_ref = bf16[8,128,128]{2,1,0:T(8,128)(2,1)S(1)} all-to-all(bf16[8,128,128]{2,1,0:T(8,128)(2,1)} %gram.1), channel_id=1, replica_groups=mesh['y'=4,'z'=8,'x'=4,'core'=2] {'x','core'}, dimensions={0} | all-to-all | bytes 524288 | tf_op jit(solution)/shard_map/all_to_all | solution.py:433
  18.0 0.0 copy-done.3
  18.0 0.8 block_sum.1
  18.7 7.4 %all-to-all-start.1 = ((bf16[8,160,128]{2,1,0:T(8,128)(2,1)}), bf16[8,160,128]{2,1,0:T(8,128)(2,1)S(1)}, u32[]{:S(2)}, u32[]{:S(2)}) async-start(bf16[8,160,128]{2,1,0:T(8,128)(2,1)} %block_sum.1), calls=%async_computation.1 | async-start | bytes 655360 | tf_op jit(solution)/shard_map/all_to_all | solution.py:433
  26.2 0.0 copy-done.4
  26.2 0.4 collective-permute-start
  26.5 1.8 %collective-permute-start.1 = (bf16[1024,128]{1,0:T(8,128)(2,1)S(1)}, bf16[1024,128]{1,0:T(8,128)(2,1)}, u32[]{:S(2)}, u32[]{:S(2)}) collective-permute-start(bf16[1024,128]{1,0:T(8,128)(2,1)S(1)} %copy-done.4), channel_id=1, source_target_pairs={{0,4},{2,6},{4,0},{6,2},{1,5},{3,7},{5,1},{7,3},{8,12},{10,14},{12... | collective-permute-start | bytes 786440 | tf_op jit(solution)/shard_map/ppermute | solution.py:437
  28.3 1.8 %collective-permute-start.2 = (bf16[1024,128]{1,0:T(8,128)(2,1)S(1)}, bf16[1024,128]{1,0:T(8,128)(2,1)}, u32[]{:S(2)}, u32[]{:S(2)}) collective-permute-start(bf16[1024,128]{1,0:T(8,128)(2,1)S(1)} %copy-done.4), channel_id=1, source_target_pairs={{0,6},{2,4},{4,2},{6,0},{1,7},{3,5},{5,3},{7,1},{8,14},{10,12},{12... | collective-permute-start | bytes 786440 | tf_op jit(solution)/shard_map/ppermute | solution.py:437
  30.1 0.1 stack.47.where
  30.2 7.2 %all-to-all-done.1.in_ref = bf16[8,160,128]{2,1,0:T(8,128)(2,1)S(1)} async-done(((bf16[8,160,128]{2,1,0:T(8,128)(2,1)}), bf16[8,160,128]{2,1,0:T(8,128)(2,1)S(1)}, u32[]{:S(2)}, u32[]{:S(2)}) %all-to-all-start.1) | async-done | bytes 327712 | tf_op jit(solution)/shard_map/all_to_all | solution.py:433
  37.4 0.6 plane_sum.1
  38.0 9.7 %all_to_all.31.far_ref.tests_ref = bf16[4,288,128]{2,1,0:T(8,128)(2,1)S(1)} all-to-all(bf16[4,288,128]{2,1,0:T(8,128)(2,1)S(1)} %get-tuple-element.15), channel_id=1, replica_groups=mesh['y'=4,'z'=8,'x'=4,'core'=2] {'y'}, dimensions={0} | all-to-all | bytes 589824 | tf_op jit(solution)/shard_map/all_to_all | solution.py:433
  47.7 0.0 copy-done.2
  47.7 3.2 %node_solve.1 = bf16[8,128,128]{2,1,0:T(8,128)(2,1)} custom-call(s32[11]{0:T(128)S(1)} %stack.47.where, bf16[4,288,128]{2,1,0:T(8,128)(2,1)S(1)} %all_to_all.31.far_ref.tests_ref, f32[2,96,128]{2,1,0:T(8,128)S(1)} %get-tuple-element.16.near_ref, f32[15,256,256]{2,1,0:T(8,128)} %capacitance.1, s32[15,256]{1,0:T(8,128)S(1)} %copy-done.2), custom_call_target="tpu_custom_call" | custom-call | tf_op jit(solution)/shard_map/node_solve/pallas_call | solution.py:212
  50.8 7.8 %all-to-all-start.3 = ((bf16[8,128,128]{2,1,0:T(8,128)(2,1)}), bf16[8,128,128]{2,1,0:T(8,128)(2,1)S(1)}, u32[]{:S(2)}, u32[]{:S(2)}) async-start(bf16[8,128,128]{2,1,0:T(8,128)(2,1)} %node_solve.1), calls=%async_computation.3 | async-start | bytes 524288 | tf_op jit(solution)/shard_map/all_to_all | solution.py:433
  58.6 0.0 copy-start
  58.6 0.0 copy-start.1
  58.6 0.2 collective-permute-start.3
  58.8 0.0 collective-permute-done.refs_1_
  58.8 0.3 collective-permute-start.4
  59.1 0.0 collective-permute-done.1.refs_2_
  59.1 0.2 collective-permute-start.5
  59.3 0.0 collective-permute-done.2.refs_3_
  59.3 0.3 collective-permute-start.6
  59.6 4.9 %kernel_block.2 = (bf16[4,1024,1024]{2,1,0:T(8,128)(2,1)}, f32[8,128]{1,0:T(8,128)S(1)}) custom-call(bf16[4,288,128]{2,1,0:T(8,128)(2,1)S(1)} %all_to_all.31.far_ref.tests_ref, bf16[1024,128]{1,0:T(8,128)(2,1)S(1)} %copy-done.4, bf16[1024,128]{1,0:T(8,128)(2,1)S(1)} %collective-permute-done.refs_1_, bf16[1024,128]{1,0:T(8,128)(2,1)} %collective-permute-done.1.refs_2_, ...), custom_call_target="tpu_custom_call" | custom-call | flops 2147483648 | bytes 10485760 | tf_op jit(solution)/shard_map/kernel_block/pallas_call | solution.py:340
  64.6 0.6 all-to-all-done.3.pieces_ref
  65.1 0.0 copy-done
  65.1 0.0 copy-done.1
  65.1 2.6 %update.1 = (f32[64,1024]{1,0:T(8,128)}, bf16[4,64,1024]{2,1,0:T(8,128)(2,1)}) custom-call(bf16[8,128,128]{2,1,0:T(8,128)(2,1)S(1)} %all-to-all-done.3.pieces_ref, f32[64,1024]{1,0:T(8,128)S(1)} %bitcast.18, f32[4096,128]{1,0:T(8,128)S(1)} %bitcast.16, f32[8,128]{1,0:T(8,128)S(1)} %get-tuple-element.18.mark), custom_call_target="tpu_custom_call" | custom-call | tf_op jit(solution)/shard_map/update/pallas_call | solution.py:266
  67.7 3.6 %all-to-all-start.4 = ((bf16[4,64,1024]{2,1,0:T(8,128)(2,1)}), bf16[4,64,1024]{2,1,0:T(8,128)(2,1)S(1)}, u32[]{:S(2)}, u32[]{:S(2)}) async-start(bf16[4,64,1024]{2,1,0:T(8,128)(2,1)} %get-tuple-element.21), calls=%async_computation.4 | async-start | bytes 1048576 | tf_op jit(solution)/shard_map/all_to_all | solution.py:433
  71.4 0.0 collective-permute-done.3.refs_0_
  71.4 0.0 collective-permute-done.4.refs_1_
  71.4 0.0 collective-permute-done.5.refs_2_
  71.4 0.0 collective-permute-done.6.refs_3_
  71.4 5.5 %kernel_block.3 = (bf16[4,1024,1024]{2,1,0:T(8,128)(2,1)}, f32[8,128]{1,0:T(8,128)S(1)}) custom-call(bf16[4,288,128]{2,1,0:T(8,128)(2,1)S(1)} %all_to_all.31.far_ref.tests_ref, bf16[1024,128]{1,0:T(8,128)(2,1)} %collective-permute-done.3.refs_0_, bf16[1024,128]{1,0:T(8,128)(2,1)} %collective-permute-done.4.refs_1_, ...), custom_call_target="tpu_custom_call" | custom-call | flops 2147483648 | bytes 10485760 | tf_op jit(solution)/shard_map/kernel_block/pallas_call | solution.py:340
  76.9 3.1 %all-to-all-done.4.refs_1_ = bf16[4,64,1024]{2,1,0:T(8,128)(2,1)S(1)} async-done(((bf16[4,64,1024]{2,1,0:T(8,128)(2,1)}), bf16[4,64,1024]{2,1,0:T(8,128)(2,1)S(1)}, u32[]{:S(2)}, u32[]{:S(2)}) %all-to-all-start.4) | async-done | bytes 524320 | tf_op jit(solution)/shard_map/all_to_all | solution.py:433
  80.0 1.8 %collective-permute-start.7 = (bf16[4,64,1024]{2,1,0:T(8,128)(2,1)S(1)}, bf16[4,64,1024]{2,1,0:T(8,128)(2,1)S(1)}, u32[]{:S(2)}, u32[]{:S(2)}) collective-permute-start(bf16[4,64,1024]{2,1,0:T(8,128)(2,1)S(1)} %all-to-all-done.4.refs_1_), channel_id=1, source_target_pairs={{0,1},{1,0},{2,3},{3,2},{4,5},{5,4},{6,7},{7,6},{8,9},{9,8},{10,11... | collective-permute-start | bytes 1572872 | tf_op jit(solution)/shard_map/ppermute | solution.py:437
  81.8 4.5 %apply_block.2.refs_2_ = f32[64,1024]{1,0:T(8,128)S(1)} custom-call(s32[11]{0:T(128)S(1)} %stack.47.where, bf16[4,1024,1024]{2,1,0:T(8,128)(2,1)} %get-tuple-element.24.refs_0_, bf16[4,64,1024]{2,1,0:T(8,128)(2,1)S(1)} %all-to-all-done.4.refs_1_, f32[8,128]{1,0:T(8,128)S(1)} %get-tuple-element.25.refs_2_), custom_call_target="tpu_custom_call" | custom-call | flops 2147483648 | bytes 9437184 | tf_op jit(solution)/shard_map/apply_block/pallas_call | solution.py:399
  86.3 0.0 collective-permute-done.7.refs_1_
  86.3 4.8 %apply_block.3 = bf16[32,16,128]{2,1,0:T(8,128)(2,1)S(1)} custom-call(s32[11]{0:T(128)S(1)} %stack.47.where, bf16[4,1024,1024]{2,1,0:T(8,128)(2,1)} %get-tuple-element.20.refs_0_, bf16[4,64,1024]{2,1,0:T(8,128)(2,1)S(1)} %collective-permute-done.7.refs_1_, f32[64,1024]{1,0:T(8,128)S(1)} %apply_block.2.refs_2_), custom_call_target="tpu_custom_call" | custom-call | flops 2147483648 | bytes 9437184 | tf_op jit(solution)/shard_map/apply_block/pallas_call | solution.py:399
  91.2 12.3 %all_to_all.32.in_ref = bf16[32,16,128]{2,1,0:T(8,128)(2,1)S(1)} all-to-all(bf16[32,16,128]{2,1,0:T(8,128)(2,1)S(1)} %apply_block.3), channel_id=1, replica_groups=mesh['y'=4,'z'=8,'x'=4,'core'=2] {'y','z'}, dimensions={0} | all-to-all | bytes 262144 | tf_op jit(solution)/shard_map/all_to_all | solution.py:433
  103.5 0.7 final_sum.1
Async XLA Ops:
  0.6 25.5 %copy-start.4 = (bf16[1024,128]{1,0:T(8,128)(2,1)S(1)}, bf16[1024,128]{1,0:T(8,128)(2,1)}, u32[]{:S(2)}) copy-start(bf16[1024,128]{1,0:T(8,128)(2,1)} %refs_0_.2) | copy-start | bytes 786436
  0.6 17.3 %copy-start.3 = (bf16[32,128]{1,0:T(8,128)(2,1)S(1)}, bf16[32,128]{1,0:T(8,128)(2,1)}, u32[]{:S(2)}) copy-start(bf16[32,128]{1,0:T(8,128)(2,1)} %tests_ref.1) | copy-start | bytes 24580
  0.7 47.0 %copy-start.2 = (s32[15,256]{1,0:T(8,128)S(1)}, s32[15,256]{1,0:T(8,128)}, u32[]{:S(2)}) copy-start(s32[15,256]{1,0:T(8,128)} %refs_0_.1) | copy-start | bytes 46084
  18.7 18.7 %all-to-all-start.1 = ((bf16[8,160,128]{2,1,0:T(8,128)(2,1)}), bf16[8,160,128]{2,1,0:T(8,128)(2,1)S(1)}, u32[]{:S(2)}, u32[]{:S(2)}) async-start(bf16[8,160,128]{2,1,0:T(8,128)(2,1)} %block_sum.1), calls=%async_computation.1 | async-start | bytes 655360 | tf_op jit(solution)/shard_map/all_to_all | solution.py:433
  26.2 32.7 %collective-permute-start = (bf16[1024,128]{1,0:T(8,128)(2,1)S(1)}, bf16[1024,128]{1,0:T(8,128)(2,1)S(1)}, u32[]{:S(2)}, u32[]{:S(2)}) collective-permute-start(bf16[1024,128]{1,0:T(8,128)(2,1)S(1)} %copy-done.4), channel_id=1, source_target_pairs={{0,2},{2,0},{4,6},{6,4},{1,3},{3,1},{5,7},{7,5},{8,10},{10,8},{12,... | collective-permute-start | bytes 786440 | tf_op jit(solution)/shard_map/ppermute | solution.py:437
  26.5 32.6 %collective-permute-start.1 = (bf16[1024,128]{1,0:T(8,128)(2,1)S(1)}, bf16[1024,128]{1,0:T(8,128)(2,1)}, u32[]{:S(2)}, u32[]{:S(2)}) collective-permute-start(bf16[1024,128]{1,0:T(8,128)(2,1)S(1)} %copy-done.4), channel_id=1, source_target_pairs={{0,4},{2,6},{4,0},{6,2},{1,5},{3,7},{5,1},{7,3},{8,12},{10,14},{12... | collective-permute-start | bytes 786440 | tf_op jit(solution)/shard_map/ppermute | solution.py:437
  28.3 31.0 %collective-permute-start.2 = (bf16[1024,128]{1,0:T(8,128)(2,1)S(1)}, bf16[1024,128]{1,0:T(8,128)(2,1)}, u32[]{:S(2)}, u32[]{:S(2)}) collective-permute-start(bf16[1024,128]{1,0:T(8,128)(2,1)S(1)} %copy-done.4), channel_id=1, source_target_pairs={{0,6},{2,4},{4,2},{6,0},{1,7},{3,5},{5,3},{7,1},{8,14},{10,12},{12... | collective-permute-start | bytes 786440 | tf_op jit(solution)/shard_map/ppermute | solution.py:437
  50.8 14.3 %all-to-all-start.3 = ((bf16[8,128,128]{2,1,0:T(8,128)(2,1)}), bf16[8,128,128]{2,1,0:T(8,128)(2,1)S(1)}, u32[]{:S(2)}, u32[]{:S(2)}) async-start(bf16[8,128,128]{2,1,0:T(8,128)(2,1)} %node_solve.1), calls=%async_computation.3 | async-start | bytes 524288 | tf_op jit(solution)/shard_map/all_to_all | solution.py:433
  58.6 6.5 %copy-start = (f32[1024,4,128]{2,1,0:T(4,128)S(1)}, f32[1024,4,128]{2,1,0:T(4,128)}, u32[]{:S(2)}) copy-start(f32[1024,4,128]{2,1,0:T(4,128)} %param.10) | copy-start | bytes 6291460
  58.6 6.5 %copy-start.1 = (f32[1024,64]{0,1:T(8,128)S(1)}, f32[1024,64]{0,1:T(8,128)}, u32[]{:S(2)}) copy-start(f32[1024,64]{0,1:T(8,128)} %param.7) | copy-start | bytes 786436
  58.6 12.7 %collective-permute-start.3 = (bf16[1024,128]{1,0:T(8,128)(2,1)S(1)}, bf16[1024,128]{1,0:T(8,128)(2,1)}, u32[]{:S(2)}, u32[]{:S(2)}) collective-permute-start(bf16[1024,128]{1,0:T(8,128)(2,1)S(1)} %copy-done.4), channel_id=1, source_target_pairs={{0,1},{1,0},{2,3},{3,2},{4,5},{5,4},{6,7},{7,6},{8,9},{9,8},{10,11... | collective-permute-start | bytes 786440 | tf_op jit(solution)/shard_map/ppermute | solution.py:437
  58.8 12.5 %collective-permute-start.4 = (bf16[1024,128]{1,0:T(8,128)(2,1)S(1)}, bf16[1024,128]{1,0:T(8,128)(2,1)}, u32[]{:S(2)}, u32[]{:S(2)}) collective-permute-start(bf16[1024,128]{1,0:T(8,128)(2,1)S(1)} %collective-permute-done.refs_1_), channel_id=1, source_target_pairs={{0,1},{1,0},{2,3},{3,2},{4,5},{5,4},{6,7},{7,6},{8,9},{9,8},{10,11... | collective-permute-start | bytes 786440 | tf_op jit(solution)/shard_map/ppermute | solution.py:437
  59.1 12.3 %collective-permute-start.5 = (bf16[1024,128]{1,0:T(8,128)(2,1)}, bf16[1024,128]{1,0:T(8,128)(2,1)}, u32[]{:S(2)}, u32[]{:S(2)}) collective-permute-start(bf16[1024,128]{1,0:T(8,128)(2,1)} %collective-permute-done.1.refs_2_), channel_id=1, source_target_pairs={{0,1},{1,0},{2,3},{3,2},{4,5},{5,4},{6,7},{7,6},{8,9},{9,8},{10,11... | collective-permute-start | bytes 786440 | tf_op jit(solution)/shard_map/ppermute | solution.py:437
  59.3 12.0 %collective-permute-start.6 = (bf16[1024,128]{1,0:T(8,128)(2,1)}, bf16[1024,128]{1,0:T(8,128)(2,1)}, u32[]{:S(2)}, u32[]{:S(2)}) collective-permute-start(bf16[1024,128]{1,0:T(8,128)(2,1)} %collective-permute-done.2.refs_3_), channel_id=1, source_target_pairs={{0,1},{1,0},{2,3},{3,2},{4,5},{5,4},{6,7},{7,6},{8,9},{9,8},{10,11... | collective-permute-start | bytes 786440 | tf_op jit(solution)/shard_map/ppermute | solution.py:437
  67.7 12.3 %all-to-all-start.4 = ((bf16[4,64,1024]{2,1,0:T(8,128)(2,1)}), bf16[4,64,1024]{2,1,0:T(8,128)(2,1)S(1)}, u32[]{:S(2)}, u32[]{:S(2)}) async-start(bf16[4,64,1024]{2,1,0:T(8,128)(2,1)} %get-tuple-element.21), calls=%async_computation.4 | async-start | bytes 1048576 | tf_op jit(solution)/shard_map/all_to_all | solution.py:433
  80.0 6.3 %collective-permute-start.7 = (bf16[4,64,1024]{2,1,0:T(8,128)(2,1)S(1)}, bf16[4,64,1024]{2,1,0:T(8,128)(2,1)S(1)}, u32[]{:S(2)}, u32[]{:S(2)}) collective-permute-start(bf16[4,64,1024]{2,1,0:T(8,128)(2,1)S(1)} %all-to-all-done.4.refs_1_), channel_id=1, source_target_pairs={{0,1},{1,0},{2,3},{3,2},{4,5},{5,4},{6,7},{7,6},{8,9},{9,8},{10,11... | collective-permute-start | bytes 1572872 | tf_op jit(solution)/shard_map/ppermute | solution.py:437

commit v3 on v2

--- a/solution.py
+++ b/solution.py
@@ -36,6 +36,11 @@
         return lax.dot_general(p, q, dims, preferred_element_type=f32)
 
     return one(a[0], b[0]) + (one(a[0], b[1]) + one(a[1], b[0]))
+
+
+def dot2(a, b):
+    high = lax.dot_general(a[0], b, NN, preferred_element_type=f32)
+    return high + lax.dot_general(a[1], b, NN, preferred_element_type=f32)
 
 
 def gram_kernel(targets_hbm, left_hbm, right_hbm, out_ref, targets, left, right, upper, lower, sems):
@@ -62,10 +67,9 @@
 
         rows = jnp.concatenate([targets[k]] + [level(left, n).T for n in range(3)], axis=0)
         high, low = split2(rows)
-        parts = [split2(level(right, n)) for n in range(LEVELS)]
-        pair = lambda i, j: tuple(jnp.concatenate([parts[i][p], parts[j][p]], axis=1) for p in (0, 1))
-        first = dot3((high[:192], low[:192]), pair(0, 1), NN)
-        second = dot3((high, low), pair(2, 3), NN)
+        parts = [level(right, n).astype(bf16) for n in range(LEVELS)]
+        first = dot2((high[:192], low[:192]), jnp.concatenate(parts[:2], axis=1))
+        second = dot2((high, low), jnp.concatenate(parts[2:], axis=1))
         if k == 0:
             upper[...] = first
             lower[...] = second
@@ -169,8 +173,7 @@
     )(where, arrived)
 
 
-def node_kernel(where, far_ref, near_ref, capacitance, *refs):
-    pivots, out_ref, caps, sems = refs
+def factor_kernel(where, capacitance, pivots, high, low, caps, sems):
     loads = [
         pltpu.make_async_copy(
             capacitance.at[where[k], pl.ds(pl.multiple_of(RANK * where[4 + k], RANK), RANK)],
@@ -181,6 +184,35 @@
     ]
     for load in loads:
         load.start()
+    source = lax.broadcasted_iota(jnp.int32, (256, 256), 0)
+    for k in range(LEVELS):
+        picks = jnp.where(source == pivots[pl.ds(where[k], 1), :], 1.0, 0.0).astype(bf16)
+        loads[k].wait()
+        for ref, piece in zip((high, low), split2(caps[k])):
+            ref[k] = lax.dot_general(picks, piece, NT, preferred_element_type=f32).astype(bf16)
+
+
+def node_factors(where, capacitance, pivots):
+    vmem = pl.BlockSpec(memory_space=pltpu.VMEM)
+    return pl.pallas_call(
+        factor_kernel,
+        in_specs=[
+            pl.BlockSpec(memory_space=pltpu.SMEM),
+            pl.BlockSpec(memory_space=pltpu.HBM),
+            vmem,
+        ],
+        out_specs=[vmem] * 2,
+        out_shape=[jax.ShapeDtypeStruct((LEVELS, 2 * RANK, RANK), bf16)] * 2,
+        scratch_shapes=[
+            pltpu.VMEM((LEVELS, RANK, 2 * RANK), f32),
+            pltpu.SemaphoreType.DMA((LEVELS,)),
+        ],
+        compiler_params=params(52),
+        name="node_factors",
+    )(where, capacitance, pivots)
+
+
+def node_kernel(where, far_ref, near_ref, high, low, out_ref):
     y = where[9]
 
     def far(index):
@@ -192,44 +224,25 @@
         (near_ref[0, :40], near_ref[1, :40]),
         (near_ref[0, 40:], near_ref[1, 40:]),
     ]
-    solved = []
-    for level in range(LEVELS):
-        stacked = split2(jnp.concatenate(stacks[level], axis=1))
-        source = lax.broadcasted_iota(jnp.int32, (256, 256), 0)
-        picks = jnp.where(source == pivots[pl.ds(where[level], 1), :], 1.0, 0.0).astype(bf16)
-        moved = [
-            lax.dot_general(piece, picks, NN, preferred_element_type=f32).astype(bf16)
-            for piece in stacked
-        ]
-        loads[level].wait()
-        solved.append(dot3(moved, split2(caps[level]), NT))
+    solved = [
+        dot3(split2(jnp.concatenate(stacks[k], axis=1)), (high[k], low[k]), NN)
+        for k in range(LEVELS)
+    ]
     block = jnp.concatenate(solved, axis=0).astype(bf16)
     for n in range(8):
         out_ref[n] = block
 
 
-def node_solve(where, far, near, capacitance, pivots):
+def node_solve(where, far, near, factors):
+    vmem = pl.BlockSpec(memory_space=pltpu.VMEM)
     return pl.pallas_call(
         node_kernel,
-        grid_spec=pltpu.PrefetchScalarGridSpec(
-            num_scalar_prefetch=1,
-            grid=(1,),
-            in_specs=[
-                pl.BlockSpec((4, 288, RANK), lambda i, w: (0, 0, 0)),
-                pl.BlockSpec((2, 96, RANK), lambda i, w: (0, 0, 0)),
-                pl.BlockSpec(memory_space=pltpu.HBM),
-                pl.BlockSpec((15, 2 * RANK), lambda i, w: (0, 0)),
-            ],
-            out_specs=pl.BlockSpec((8, 128, RANK), lambda i, w: (0, 0, 0)),
-            scratch_shapes=[
-                pltpu.VMEM((LEVELS, RANK, 2 * RANK), f32),
-                pltpu.SemaphoreType.DMA((LEVELS,)),
-            ],
-        ),
+        in_specs=[pl.BlockSpec(memory_space=pltpu.SMEM)] + [vmem] * 4,
+        out_specs=vmem,
         out_shape=jax.ShapeDtypeStruct((8, 128, RANK), bf16),
-        compiler_params=params(52),
+        compiler_params=params(),
         name="node_solve",
-    )(where, far, near, capacitance, pivots)
+    )(where, far, near, *factors)
 
 
 def update_kernel(
@@ -247,7 +260,9 @@
             share = rows[:TARGETS]
             for k in range(level):
                 begin = TARGETS + RANK * k
-                share -= dot3(shares[k], split2(rows[begin : begin + RANK]), NN)
+                factor = rows[begin : begin + RANK].astype(bf16)
+                for part in shares[k]:
+                    share -= lax.dot_general(part, factor, NN, preferred_element_type=f32)
             shares.append(split2(share))
         shares_high[...] = jnp.concatenate([s[0] for s in shares], axis=1)
         shares_low[...] = jnp.concatenate([s[1] for s in shares], axis=1)
@@ -256,9 +271,7 @@
     joined = [jnp.concatenate([part[p] for part in left], axis=1) for p in (0, 1)]
     value = targets_ref[...] - dot3((shares_high[...], shares_low[...]), joined, NT)
     out_ref[...] = value
-    rounded = value.astype(bf16)
-    for k in range(4):
-        weights_ref[k] = rounded
+    weights_ref[...] = value.astype(bf16)
 
 
 def update(pieces, targets_t, left, mark):
@@ -274,11 +287,11 @@
         ],
         out_specs=[
             pl.BlockSpec((TARGETS, chunk), lambda i: (0, i)),
-            pl.BlockSpec((4, TARGETS, chunk), lambda i: (0, 0, i)),
+            pl.BlockSpec((TARGETS, chunk), lambda i: (0, i)),
         ],
         out_shape=[
             jax.ShapeDtypeStruct((TARGETS, POINTS), f32),
-            jax.ShapeDtypeStruct((4, TARGETS, POINTS), bf16),
+            jax.ShapeDtypeStruct((TARGETS, POINTS), bf16),
         ],
         scratch_shapes=[
             pltpu.VMEM((TARGETS, LEVELS * RANK), bf16),
@@ -302,68 +315,87 @@
     return jnp.concatenate([points, extra.astype(bf16)], axis=1)
 
 
-def block_kernel(tests_ref, *refs):
-    features, (out, mark, tests, points, train, slots, sems) = refs[:4], refs[4:]
+def tests_kernel(in_ref, out_ref):
+    for k in range(4):
+        out_ref[256 * k : 256 * k + 256] = widened(in_ref[k, 32:], 3, 0)
+
+
+def widen_tests(far):
+    return pl.pallas_call(
+        tests_kernel,
+        out_shape=jax.ShapeDtypeStruct((1024, 2 * FEAT), bf16),
+        compiler_params=params(),
+        name="widen_tests",
+    )(far)
+
+
+SCALE = 2.0 * SPREAD / FEAT * math.log2(math.e)
+
+
+def block_kernel(tests, *refs, whole):
+    features, (out, mark, points, train, slots, sems) = refs[:4], refs[4:]
     mark[...] = jnp.zeros_like(mark)
     loads = [
         pltpu.make_async_copy(features[j], points.at[j], sems.at[j]) for j in range(4)
     ]
     for load in loads:
         load.start()
-    for k in range(4):
-        tests[256 * k : 256 * k + 256] = widened(tests_ref[k, 32:], 3, 0)
-    scale = 2.0 * SPREAD / FEAT * math.log2(math.e)
     stores = []
     for j in range(4):
         loads[j].wait()
         for q in range(4):
             rows = slice(256 * q, 256 * q + 256)
-            train[rows] = widened(points[j, rows], 0, 3)
+            train[j % 2, rows] = widened(points[j, rows], 0, 3)
             for i in range(2):
                 columns = slice(512 * i, 512 * i + 512)
                 inner = lax.dot_general(
-                    train[rows], tests[columns], NT, preferred_element_type=f32
+                    train[j % 2, rows], tests[columns], NT, preferred_element_type=f32
                 )
-                slots[j, rows, columns] = jnp.exp2(inner * scale).astype(bf16)
-            part = pl.ds(256 * q, 256)
-            stores.append(
-                pltpu.make_async_copy(
-                    slots.at[j, part], out.at[j, part], sems.at[4 + 4 * j + q]
+                slots[j, rows, columns] = jnp.exp2(inner * SCALE).astype(bf16)
+            part = pl.ds(0, POINTS) if whole else pl.ds(256 * q, 256)
+            if q == 3 or not whole:
+                stores.append(
+                    pltpu.make_async_copy(
+                        slots.at[j, part], out.at[j, part], sems.at[4 + 4 * j + q]
+                    )
                 )
-            )
-            stores[-1].start()
+                stores[-1].start()
     for store in stores:
         store.wait()
 
 
-def kernel_block(tests, features):
-    return pl.pallas_call(
-        block_kernel,
-        in_specs=[pl.BlockSpec(memory_space=pltpu.VMEM)]
-        + [pl.BlockSpec(memory_space=pl.ANY)] * 4,
-        out_specs=[pl.BlockSpec(memory_space=pl.ANY), pl.BlockSpec(memory_space=pltpu.VMEM)],
-        out_shape=[jax.ShapeDtypeStruct((4, POINTS, 1024), bf16), jax.ShapeDtypeStruct((8, 128), f32)],
+def kernel_block(tests, features, limit, whole):
+    vmem = pl.BlockSpec(memory_space=pltpu.VMEM)
+    return pl.pallas_call(
+        functools.partial(block_kernel, whole=whole),
+        in_specs=[vmem] + [pl.BlockSpec(memory_space=pl.ANY)] * 4,
+        out_specs=[pl.BlockSpec(memory_space=pl.ANY), vmem],
+        out_shape=[
+            jax.ShapeDtypeStruct((4, POINTS, 1024), bf16),
+            jax.ShapeDtypeStruct((8, 128), f32),
+        ],
         scratch_shapes=[
-            pltpu.VMEM((1024, 2 * FEAT), bf16),
             pltpu.VMEM((4, POINTS, FEAT), bf16),
-            pltpu.VMEM((POINTS, 2 * FEAT), bf16),
+            pltpu.VMEM((2, POINTS, 2 * FEAT), bf16),
             pltpu.VMEM((4, POINTS, 1024), bf16),
             pltpu.SemaphoreType.DMA((20,)),
         ],
-        compiler_params=params(51),
+        compiler_params=params(limit),
         cost_estimate=pl.CostEstimate(
-            flops=2 * 4 * POINTS * 1024 * 256, bytes_accessed=10 << 20, transcendentals=4 << 20
+            flops=2 * 4 * POINTS * 1024 * 256,
+            bytes_accessed=10 << 20,
+            transcendentals=4 << 20,
         ),
         name="kernel_block",
     )(tests, *features)
 
 
-def apply_kernel(where, *refs, last):
-    x = where[10]
+def apply_kernel(block, *refs, last):
+    weights, refs = refs[:4], refs[4:]
     if last:
-        block, weights_ref, before_ref, out_ref, total, slots, sems = refs
+        before_ref, out_ref, total, slots, sems = refs
     else:
-        block, weights_ref, _, total, slots, sems = refs
+        _, total, slots, sems = refs
     loads = []
     for j in range(4):
         for q in range(4):
@@ -378,7 +410,7 @@
         for i in range(4):
             columns = slice(256 * i, 256 * i + 256)
             part = lax.dot_general(
-                weights_ref[jnp.bitwise_xor(x, j)], slots[j, :, columns], NN, preferred_element_type=f32
+                weights[j][...], slots[j, :, columns], NN, preferred_element_type=f32
             )
             if j == 0:
                 total[:, columns] = part + before_ref[:, columns] if last else part
@@ -392,24 +424,25 @@
                 out_ref[8 * i + k] = jnp.concatenate(rows, axis=1).astype(bf16)
 
 
-def apply_block(where, block, weights, before=None, mark=None):
+def apply_block(block, weights, before=None, mark=None):
     vmem = pl.BlockSpec(memory_space=pltpu.VMEM)
     last = before is not None
     total = pltpu.VMEM((TARGETS, 1024), f32)
     return pl.pallas_call(
         functools.partial(apply_kernel, last=last),
-        in_specs=[pl.BlockSpec(memory_space=pltpu.SMEM), pl.BlockSpec(memory_space=pl.ANY), vmem]
+        in_specs=[pl.BlockSpec(memory_space=pl.ANY)]
+        + [vmem] * 4
         + [vmem if last else pl.BlockSpec(memory_space=pl.ANY)],
         out_specs=vmem,
         out_shape=jax.ShapeDtypeStruct((32, 16, 128) if last else (TARGETS, 1024), bf16 if last else f32),
         scratch_shapes=[total] * last
         + [pltpu.VMEM((4, POINTS, 1024), bf16), pltpu.SemaphoreType.DMA((16,))],
-        compiler_params=params(51),
+        compiler_params=params(32 if last else 44),
         cost_estimate=pl.CostEstimate(
             flops=2 * 4 * POINTS * 1024 * 256, bytes_accessed=9 << 20, transcendentals=0
         ),
         name="apply_block",
-    )(where, block, weights, before if last else mark)
+    )(block, *weights, before if last else mark)
 
 
 def final_kernel(in_ref, out_ref):
@@ -443,7 +476,7 @@
     children = [jnp.right_shift(leaf, 3 - k) for k in range(LEVELS)]
     nodes = [(1 << k) - 1 + jnp.right_shift(children[k], 1) for k in range(LEVELS)]
     sides = [jnp.bitwise_and(child, 1) for child in children]
-    where = jnp.stack([*nodes, *sides, z, y, lax.axis_index("x")]).astype(jnp.int32)
+    where = jnp.stack([*nodes, *sides, z, y]).astype(jnp.int32)
 
     left = left_factors.reshape(LEVELS * POINTS, RANK)
     right = right_factors.reshape(LEVELS * POINTS, RANK)
@@ -456,16 +489,17 @@
     planes = exchange(block_sum(arrived, test_features), "z")
     send, near = plane_sum(where, planes)
     far = exchange(send, "y")
-    pieces = node_solve(where, far, near, capacitance, pivots)
+    pieces = node_solve(where, far, near, node_factors(where, capacitance, pivots))
     pieces = exchange(pieces, ("x", "core"))
-    own_block, own_mark = kernel_block(far, own)
+    tests = widen_tests(far)
+    own_block, own_mark = kernel_block(tests, own, 51, False)
     solved, weights = update(pieces, targets_t, left, own_mark)
-    weights = exchange(weights, "x")
-    other_block, other_mark = kernel_block(far, other)
-    weights, other_mark = lax.optimization_barrier((weights, other_mark))
-    other_weights = flipped(weights, "core", 1)
-    terms = apply_block(where, own_block, weights, mark=other_mark)
-    terms = apply_block(where, other_block, other_weights, before=terms)
+    weights = [weights] + [flipped(weights, "x", k) for k in (1, 2, 3)]
+    other_block, other_mark = kernel_block(tests, other, 32, True)
+    *weights[1:], other_mark = lax.optimization_barrier((*weights[1:], other_mark))
+    other_weights = [flipped(part, "core", 1) for part in weights]
+    terms = apply_block(own_block, weights, mark=other_mark)
+    terms = apply_block(other_block, other_weights, before=terms)
     predictions = final_sum(exchange(terms, ("y", "z")))
     return solved.T, predictions
 

time: 105 us -> 95.8 us (0.912)
  blocking collectives: 35 us -> 25.2 us
  starting transfers between devices: 25.6 us -> 31.8 us
  Pallas kernels: 31.8 us -> 28.2 us
  waiting for transfers between devices: 10.9 us -> 9.24 us
    all_to_all x3 -> x2, blocking collectives: 35 us -> 25.2 us  [exchange(): return lax.all_to_all(blocks, axes, 0, 0, tiled=True)]
    ppermute x8 -> x14, starting transfers between devices: 6.72 us -> 13.2 us  [flipped(): lax.ppermute(value, axis, [(s, s ^ mask) for s in range(lax.axis_size(axi...]
    pallas_call x2, Pallas kernels: 9.39 us -> 5.05 us  [apply_block(): pl.pallas_call(functools.partial(apply_kernel, last=last), in_specs=[pl.B...]
    all_to_all x3, waiting for transfers between devices: 10.9 us -> 9.2 us  [exchange(): return lax.all_to_all(blocks, axes, 0, 0, tiled=True)]
    pallas_call x3 -> x5, Pallas kernels: 13.5 us -> 14.3 us  [the longest x2 10.1 us: kernel_block(): pl.pallas_call(functools.partial(block_kernel, whole=whole), in_specs=[vm...]
  transfers between devices with their start and end apart: 11 -> 17, of which waited for: 3 -> 2; matrix products, arithmetic and copies ran while one was open for 0% -> 0% of each run, Pallas kernels for 20% -> 21%
where the time goes in v3:
time: 95.8 us; the launch traced here: 95.3 us
  starting transfers between devices  31.8 us (33%)
  Pallas kernels  28.2 us (29%)
  blocking collectives  25.2 us (26%)
  waiting for transfers between devices  9.24 us (10%)
    all_to_all x2, blocking collectives, exchange(): return lax.all_to_all(blocks, axes, 0, 0, tiled=True)  25.2 us
    all_to_all x3, starting transfers between devices, exchange(): return lax.all_to_all(blocks, axes, 0, 0, tiled=True)  18.6 us
    ppermute x14, starting transfers between devices, flipped(): lax.ppermute(value, axis, [(s, s ^ mask) for s in range(lax.axis_size(axi...  13.2 us
    pallas_call x2, Pallas kernels, kernel_block(): pl.pallas_call(functools.partial(block_kernel, whole=whole), in_specs=[vm...  10.1 us
    all_to_all x3, waiting for transfers between devices, exchange(): return lax.all_to_all(blocks, axes, 0, 0, tiled=True)  9.2 us
    pallas_call x2, Pallas kernels, apply_block(): pl.pallas_call(functools.partial(apply_kernel, last=last), in_specs=[pl.B...  5.05 us
    pallas_call x1, Pallas kernels, gram(): pl.pallas_call(gram_kernel, in_specs=[pl.BlockSpec(memory_space=pltpu.HBM...  3.69 us
    pallas_call x1, Pallas kernels, node_factors(): pl.pallas_call(factor_kernel, in_specs=[pl.BlockSpec(memory_space=pltpu.S...  2.52 us
  transfers between devices with their start and end apart: 17, of which 2 were waited for; matrix products, arithmetic and copies ran while one was open for 0% of the time, Pallas kernels for 21%

profile of v3, /device:TPU:1, one launch (start us, length us, event | category | flops | bytes accessed | tf_op | source)
XLA Modules:
  0.0 95.3 jit_solution(12238796480802008262)
XLA Ops:
  0.6 0.0 copy-start.5
  0.6 0.0 copy-start.4
  0.7 0.0 copy-start.3
  0.7 3.7 %gram.1 = bf16[8,128,128]{2,1,0:T(8,128)(2,1)} custom-call(f32[64,1024]{1,0:T(8,128)} %bitcast.16, f32[4096,128]{1,0:T(8,128)} %bitcast.14, f32[4096,128]{1,0:T(8,128)} %bitcast.18), custom_call_target="tpu_custom_call" | custom-call | tf_op jit(solution)/shard_map/gram/pallas_call | solution.py:96
  4.4 13.1 %all_to_all.25.in_ref = bf16[8,128,128]{2,1,0:T(8,128)(2,1)S(1)} all-to-all(bf16[8,128,128]{2,1,0:T(8,128)(2,1)} %gram.1), channel_id=1, replica_groups=mesh['y'=4,'z'=8,'x'=4,'core'=2] {'x','core'}, dimensions={0} | all-to-all | bytes 524288 | tf_op jit(solution)/shard_map/all_to_all | solution.py:466
  17.4 0.0 copy-done.4
  17.4 0.8 block_sum.1
  18.2 7.4 %all-to-all-start.1 = ((bf16[8,160,128]{2,1,0:T(8,128)(2,1)}), bf16[8,160,128]{2,1,0:T(8,128)(2,1)S(1)}, u32[]{:S(2)}, u32[]{:S(2)}) async-start(bf16[8,160,128]{2,1,0:T(8,128)(2,1)} %block_sum.1), calls=%async_computation.1 | async-start | bytes 655360 | tf_op jit(solution)/shard_map/all_to_all | solution.py:466
  25.6 0.0 copy-done.5
  25.6 1.0 %collective-permute-start.2 = (bf16[1024,128]{1,0:T(8,128)(2,1)S(1)}, bf16[1024,128]{1,0:T(8,128)(2,1)}, u32[]{:S(2)}, u32[]{:S(2)}) collective-permute-start(bf16[1024,128]{1,0:T(8,128)(2,1)S(1)} %copy-done.5), channel_id=1, source_target_pairs={{0,6},{2,4},{4,2},{6,0},{1,7},{3,5},{5,3},{7,1},{8,14},{10,12},{12... | collective-permute-start | bytes 786440 | tf_op jit(solution)/shard_map/ppermute | solution.py:470
  26.6 1.2 %collective-permute-start.1 = (bf16[1024,128]{1,0:T(8,128)(2,1)S(1)}, bf16[1024,128]{1,0:T(8,128)(2,1)}, u32[]{:S(2)}, u32[]{:S(2)}) collective-permute-start(bf16[1024,128]{1,0:T(8,128)(2,1)S(1)} %copy-done.5), channel_id=1, source_target_pairs={{0,4},{2,6},{4,0},{6,2},{1,5},{3,7},{5,1},{7,3},{8,12},{10,14},{12... | collective-permute-start | bytes 786440 | tf_op jit(solution)/shard_map/ppermute | solution.py:470
  27.8 1.2 %collective-permute-start = (bf16[1024,128]{1,0:T(8,128)(2,1)S(1)}, bf16[1024,128]{1,0:T(8,128)(2,1)}, u32[]{:S(2)}, u32[]{:S(2)}) collective-permute-start(bf16[1024,128]{1,0:T(8,128)(2,1)S(1)} %copy-done.5), channel_id=1, source_target_pairs={{0,2},{2,0},{4,6},{6,4},{1,3},{3,1},{5,7},{7,5},{8,10},{10,8},{12,... | collective-permute-start | bytes 786440 | tf_op jit(solution)/shard_map/ppermute | solution.py:470
  29.0 0.1 stack.43.where
  29.1 7.8 %all-to-all-done.1.in_ref = bf16[8,160,128]{2,1,0:T(8,128)(2,1)S(1)} async-done(((bf16[8,160,128]{2,1,0:T(8,128)(2,1)}), bf16[8,160,128]{2,1,0:T(8,128)(2,1)S(1)}, u32[]{:S(2)}, u32[]{:S(2)}) %all-to-all-start.1) | async-done | bytes 327712 | tf_op jit(solution)/shard_map/all_to_all | solution.py:466
  36.8 1.3 %plane_sum.1 = (bf16[4,288,128]{2,1,0:T(8,128)(2,1)}, f32[2,96,128]{2,1,0:T(8,128)S(1)}) custom-call(s32[10]{0:T(128)S(1)} %stack.43.where, bf16[8,160,128]{2,1,0:T(8,128)(2,1)S(1)} %all-to-all-done.1.in_ref), custom_call_target="tpu_custom_call" | custom-call | tf_op jit(solution)/shard_map/plane_sum/pallas_call | solution.py:156
  38.1 4.2 %all-to-all-start.2 = ((bf16[4,288,128]{2,1,0:T(8,128)(2,1)}), bf16[4,288,128]{2,1,0:T(8,128)(2,1)S(1)}, u32[]{:S(2)}, u32[]{:S(2)}) async-start(bf16[4,288,128]{2,1,0:T(8,128)(2,1)} %get-tuple-element.19), calls=%async_computation.2 | async-start | bytes 589824 | tf_op jit(solution)/shard_map/all_to_all | solution.py:466
  42.3 3.3 %collective-permute-start.3 = (bf16[1024,128]{1,0:T(8,128)(2,1)S(1)}, bf16[1024,128]{1,0:T(8,128)(2,1)}, u32[]{:S(2)}, u32[]{:S(2)}) collective-permute-start(bf16[1024,128]{1,0:T(8,128)(2,1)S(1)} %copy-done.5), channel_id=1, source_target_pairs={{0,1},{1,0},{2,3},{3,2},{4,5},{5,4},{6,7},{7,6},{8,9},{9,8},{10,11... | collective-permute-start | bytes 786440 | tf_op jit(solution)/shard_map/ppermute | solution.py:470
  45.6 0.0 collective-permute-done.2.refs_3_
  45.6 0.1 collective-permute-start.6
  45.7 0.0 collective-permute-done.1.refs_2_
  45.7 0.4 collective-permute-start.5
  46.1 0.0 collective-permute-done.refs_1_
  46.1 0.1 collective-permute-start.4
  46.2 0.0 copy-done.3
  46.2 2.5 %node_factors.1 = (bf16[4,256,128]{2,1,0:T(8,128)(2,1)S(1)}, bf16[4,256,128]{2,1,0:T(8,128)(2,1)S(1)}) custom-call(s32[10]{0:T(128)S(1)} %stack.43.where, f32[15,256,256]{2,1,0:T(8,128)} %capacitance.1, s32[15,256]{1,0:T(8,128)S(1)} %copy-done.3), custom_call_target="tpu_custom_call" | custom-call | tf_op jit(solution)/shard_map/node_factors/pallas_call | solution.py:197
  48.8 0.0 all-to-all-done.2.far_ref.in_ref
  48.8 1.5 %node_solve.1 = bf16[8,128,128]{2,1,0:T(8,128)(2,1)} custom-call(s32[10]{0:T(128)S(1)} %stack.43.where, bf16[4,288,128]{2,1,0:T(8,128)(2,1)S(1)} %all-to-all-done.2.far_ref.in_ref, f32[2,96,128]{2,1,0:T(8,128)S(1)} %get-tuple-element.20.near_ref, bf16[4,256,128]{2,1,0:T(8,128)(2,1)S(1)} %get-tuple-element.21.high, bf16[4,256,128]{2,1,0:T(8,128)(2,1)S(1)} %get-tuple-element.22.low), custom_call_target="tpu_custom_call" | custom-call | tf_op jit(solution)/shard_map/node_solve/pallas_call | solution.py:238
  50.3 7.0 %all-to-all-start.3 = ((bf16[8,128,128]{2,1,0:T(8,128)(2,1)}), bf16[8,128,128]{2,1,0:T(8,128)(2,1)S(1)}, u32[]{:S(2)}, u32[]{:S(2)}) async-start(bf16[8,128,128]{2,1,0:T(8,128)(2,1)} %node_solve.1), calls=%async_computation.3 | async-start | bytes 524288 | tf_op jit(solution)/shard_map/all_to_all | solution.py:466
  57.3 0.3 widen_tests.1.tests
  57.5 0.0 copy-start
  57.5 0.0 copy-start.2
  57.6 4.8 %kernel_block.2 = (bf16[4,1024,1024]{2,1,0:T(8,128)(2,1)}, f32[8,128]{1,0:T(8,128)S(1)}) custom-call(bf16[1024,256]{1,0:T(8,128)(2,1)S(1)} %widen_tests.1.tests, bf16[1024,128]{1,0:T(8,128)(2,1)S(1)} %copy-done.5, bf16[1024,128]{1,0:T(8,128)(2,1)} %collective-permute-done.refs_1_, bf16[1024,128]{1,0:T(8,128)(2,1)} %collective-permute-done.1.refs_2_, ...), custom_call_target="tpu_custom_call" | custom-call | flops 2147483648 | bytes 10485760 | tf_op jit(solution)/shard_map/kernel_block/pallas_call | solution.py:369
  62.4 1.4 %all-to-all-done.3.pieces_ref = bf16[8,128,128]{2,1,0:T(8,128)(2,1)S(1)} async-done(((bf16[8,128,128]{2,1,0:T(8,128)(2,1)}), bf16[8,128,128]{2,1,0:T(8,128)(2,1)S(1)}, u32[]{:S(2)}, u32[]{:S(2)}) %all-to-all-start.3) | async-done | bytes 262176 | tf_op jit(solution)/shard_map/all_to_all | solution.py:466
  63.8 0.0 copy-done
  63.8 0.0 copy-done.2
  63.8 0.0 copy-start.1
  63.8 2.3 %update.1 = (f32[64,1024]{1,0:T(8,128)}, bf16[64,1024]{1,0:T(8,128)(2,1)S(1)}) custom-call(bf16[8,128,128]{2,1,0:T(8,128)(2,1)S(1)} %all-to-all-done.3.pieces_ref, f32[64,1024]{1,0:T(8,128)S(1)} %bitcast.17, f32[4096,128]{1,0:T(8,128)S(1)} %bitcast.15, f32[8,128]{1,0:T(8,128)S(1)} %get-tuple-element.24.mark), custom_call_target="tpu_custom_call" | custom-call | tf_op jit(solution)/shard_map/update/pallas_call | solution.py:279
  66.1 1.3 %collective-permute-start.10 = (bf16[64,1024]{1,0:T(8,128)(2,1)S(1)}, bf16[64,1024]{1,0:T(8,128)(2,1)S(1)}, u32[]{:S(2)}, u32[]{:S(2)}) collective-permute-start(bf16[64,1024]{1,0:T(8,128)(2,1)S(1)} %get-tuple-element.27.refs_0_), channel_id=1, source_target_pairs={{0,6},{2,4},{4,2},{6,0},{1,7},{3,5},{5,3},{7,1},{8,14},{10,12},{12... | collective-permute-start | bytes 393224 | tf_op jit(solution)/shard_map/ppermute | solution.py:470
  67.4 0.0 collective-permute-done.3.refs_0_
  67.4 0.8 collective-permute-start.9
  68.2 0.0 collective-permute-done.6.refs_3_
  68.2 1.2 %collective-permute-start.8 = (bf16[64,1024]{1,0:T(8,128)(2,1)S(1)}, bf16[64,1024]{1,0:T(8,128)(2,1)S(1)}, u32[]{:S(2)}, u32[]{:S(2)}) collective-permute-start(bf16[64,1024]{1,0:T(8,128)(2,1)S(1)} %get-tuple-element.27.refs_0_), channel_id=1, source_target_pairs={{0,2},{2,0},{4,6},{6,4},{1,3},{3,1},{5,7},{7,5},{8,10},{10,8},{12,... | collective-permute-start | bytes 393224 | tf_op jit(solution)/shard_map/ppermute | solution.py:470
  69.4 0.0 collective-permute-done.5.refs_2_
  69.4 0.0 collective-permute-done.4.refs_1_
  69.4 5.3 %kernel_block.3 = (bf16[4,1024,1024]{2,1,0:T(8,128)(2,1)S(1)}, f32[8,128]{1,0:T(8,128)S(1)}) custom-call(bf16[1024,256]{1,0:T(8,128)(2,1)S(1)} %widen_tests.1.tests, bf16[1024,128]{1,0:T(8,128)(2,1)} %collective-permute-done.3.refs_0_, bf16[1024,128]{1,0:T(8,128)(2,1)} %collective-permute-done.4.refs_1_, bf16[1024,128]{1,0:T(8,128)(2,1)} %collective-permute-done.5.refs_2_, ...), custom_call_target="tpu_custom_call" | custom-call | flops 2147483648 | bytes 10485760 | tf_op jit(solution)/shard_map/kernel_block/pallas_call | solution.py:369
  74.6 2.0 %collective-permute-start.7 = (bf16[64,1024]{1,0:T(8,128)(2,1)S(1)}, bf16[64,1024]{1,0:T(8,128)(2,1)S(1)}, u32[]{:S(2)}, u32[]{:S(2)}) collective-permute-start(bf16[64,1024]{1,0:T(8,128)(2,1)S(1)} %get-tuple-element.27.refs_0_), channel_id=1, source_target_pairs={{0,1},{1,0},{2,3},{3,2},{4,5},{5,4},{6,7},{7,6},{8,9},{9,8},{10,11... | collective-permute-start | bytes 393224 | tf_op jit(solution)/shard_map/ppermute | solution.py:470
  76.6 0.0 collective-permute-done.10.refs_3_
  76.6 0.0 collective-permute-done.9.refs_2_
  76.6 0.0 collective-permute-done.8.refs_1_
  76.6 0.1 collective-permute-start.11
  76.8 0.5 collective-permute-start.12
  77.2 0.1 collective-permute-start.13
  77.3 0.0 copy-done.1
  77.3 2.4 %apply_block.2.refs_4_ = f32[64,1024]{1,0:T(8,128)S(1)} custom-call(bf16[4,1024,1024]{2,1,0:T(8,128)(2,1)S(1)} %copy-done.1, bf16[64,1024]{1,0:T(8,128)(2,1)S(1)} %get-tuple-element.27.refs_0_, bf16[64,1024]{1,0:T(8,128)(2,1)S(1)} %collective-permute-done.8.refs_1_, bf16[64,1024]{1,0:T(8,128)(2,1)S(1)} %collective-permute-done.9.refs_2_, ...), custom_call_target="tpu_custom_call" | custom-call | flops 2147483648 | bytes 9437184 | tf_op jit(solution)/shard_map/apply_block/pallas_call | solution.py:431
  79.7 0.0 collective-permute-done.7.refs_0_
  79.7 0.0 collective-permute-done.11.refs_1_
  79.7 0.0 collective-permute-done.12.refs_2_
  79.7 0.0 collective-permute-done.13.refs_3_
  79.7 2.7 %apply_block.3 = bf16[32,16,128]{2,1,0:T(8,128)(2,1)S(1)} custom-call(bf16[4,1024,1024]{2,1,0:T(8,128)(2,1)S(1)} %get-tuple-element.26.block, bf16[64,1024]{1,0:T(8,128)(2,1)S(1)} %collective-permute-done.7.refs_0_, bf16[64,1024]{1,0:T(8,128)(2,1)S(1)} %collective-permute-done.11.refs_1_, bf16[64,1024]{1,0:T(8,128)(2,1)S(1)} %collective-permute-done.12.refs_2_, ...), custom_call_target="tpu_custom_call" | custom-call | flops 2147483648 | bytes 9437184 | tf_op jit(solution)/shard_map/apply_block/pallas_call | solution.py:431
  82.4 12.1 %all_to_all.26.in_ref = bf16[32,16,128]{2,1,0:T(8,128)(2,1)S(1)} all-to-all(bf16[32,16,128]{2,1,0:T(8,128)(2,1)S(1)} %apply_block.3), channel_id=1, replica_groups=mesh['y'=4,'z'=8,'x'=4,'core'=2] {'y','z'}, dimensions={0} | all-to-all | bytes 262144 | tf_op jit(solution)/shard_map/all_to_all | solution.py:466
  94.6 0.7 final_sum.1
Async XLA Ops:
  0.6 25.0 %copy-start.5 = (bf16[1024,128]{1,0:T(8,128)(2,1)S(1)}, bf16[1024,128]{1,0:T(8,128)(2,1)}, u32[]{:S(2)}) copy-start(bf16[1024,128]{1,0:T(8,128)(2,1)} %refs_0_) | copy-start | bytes 786436
  0.6 16.8 %copy-start.4 = (bf16[32,128]{1,0:T(8,128)(2,1)S(1)}, bf16[32,128]{1,0:T(8,128)(2,1)}, u32[]{:S(2)}) copy-start(bf16[32,128]{1,0:T(8,128)(2,1)} %tests_ref.1) | copy-start | bytes 24580
  0.7 45.6 %copy-start.3 = (s32[15,256]{1,0:T(8,128)S(1)}, s32[15,256]{1,0:T(8,128)}, u32[]{:S(2)}) copy-start(s32[15,256]{1,0:T(8,128)} %pivots.1) | copy-start | bytes 46084
  18.2 18.7 %all-to-all-start.1 = ((bf16[8,160,128]{2,1,0:T(8,128)(2,1)}), bf16[8,160,128]{2,1,0:T(8,128)(2,1)S(1)}, u32[]{:S(2)}, u32[]{:S(2)}) async-start(bf16[8,160,128]{2,1,0:T(8,128)(2,1)} %block_sum.1), calls=%async_computation.1 | async-start | bytes 655360 | tf_op jit(solution)/shard_map/all_to_all | solution.py:466
  25.6 20.0 %collective-permute-start.2 = (bf16[1024,128]{1,0:T(8,128)(2,1)S(1)}, bf16[1024,128]{1,0:T(8,128)(2,1)}, u32[]{:S(2)}, u32[]{:S(2)}) collective-permute-start(bf16[1024,128]{1,0:T(8,128)(2,1)S(1)} %copy-done.5), channel_id=1, source_target_pairs={{0,6},{2,4},{4,2},{6,0},{1,7},{3,5},{5,3},{7,1},{8,14},{10,12},{12... | collective-permute-start | bytes 786440 | tf_op jit(solution)/shard_map/ppermute | solution.py:470
  26.6 19.1 %collective-permute-start.1 = (bf16[1024,128]{1,0:T(8,128)(2,1)S(1)}, bf16[1024,128]{1,0:T(8,128)(2,1)}, u32[]{:S(2)}, u32[]{:S(2)}) collective-permute-start(bf16[1024,128]{1,0:T(8,128)(2,1)S(1)} %copy-done.5), channel_id=1, source_target_pairs={{0,4},{2,6},{4,0},{6,2},{1,5},{3,7},{5,1},{7,3},{8,12},{10,14},{12... | collective-permute-start | bytes 786440 | tf_op jit(solution)/shard_map/ppermute | solution.py:470
  27.8 18.3 %collective-permute-start = (bf16[1024,128]{1,0:T(8,128)(2,1)S(1)}, bf16[1024,128]{1,0:T(8,128)(2,1)}, u32[]{:S(2)}, u32[]{:S(2)}) collective-permute-start(bf16[1024,128]{1,0:T(8,128)(2,1)S(1)} %copy-done.5), channel_id=1, source_target_pairs={{0,2},{2,0},{4,6},{6,4},{1,3},{3,1},{5,7},{7,5},{8,10},{10,8},{12,... | collective-permute-start | bytes 786440 | tf_op jit(solution)/shard_map/ppermute | solution.py:470
  38.1 10.6 %all-to-all-start.2 = ((bf16[4,288,128]{2,1,0:T(8,128)(2,1)}), bf16[4,288,128]{2,1,0:T(8,128)(2,1)S(1)}, u32[]{:S(2)}, u32[]{:S(2)}) async-start(bf16[4,288,128]{2,1,0:T(8,128)(2,1)} %get-tuple-element.19), calls=%async_computation.2 | async-start | bytes 589824 | tf_op jit(solution)/shard_map/all_to_all | solution.py:466
  42.3 25.1 %collective-permute-start.3 = (bf16[1024,128]{1,0:T(8,128)(2,1)S(1)}, bf16[1024,128]{1,0:T(8,128)(2,1)}, u32[]{:S(2)}, u32[]{:S(2)}) collective-permute-start(bf16[1024,128]{1,0:T(8,128)(2,1)S(1)} %copy-done.5), channel_id=1, source_target_pairs={{0,1},{1,0},{2,3},{3,2},{4,5},{5,4},{6,7},{7,6},{8,9},{9,8},{10,11... | collective-permute-start | bytes 786440 | tf_op jit(solution)/shard_map/ppermute | solution.py:470
  45.6 22.6 %collective-permute-start.6 = (bf16[1024,128]{1,0:T(8,128)(2,1)}, bf16[1024,128]{1,0:T(8,128)(2,1)}, u32[]{:S(2)}, u32[]{:S(2)}) collective-permute-start(bf16[1024,128]{1,0:T(8,128)(2,1)} %collective-permute-done.2.refs_3_), channel_id=1, source_target_pairs={{0,1},{1,0},{2,3},{3,2},{4,5},{5,4},{6,7},{7,6},{8,9},{9,8},{10,11... | collective-permute-start | bytes 786440 | tf_op jit(solution)/shard_map/ppermute | solution.py:470
  45.7 23.7 %collective-permute-start.5 = (bf16[1024,128]{1,0:T(8,128)(2,1)}, bf16[1024,128]{1,0:T(8,128)(2,1)}, u32[]{:S(2)}, u32[]{:S(2)}) collective-permute-start(bf16[1024,128]{1,0:T(8,128)(2,1)} %collective-permute-done.1.refs_2_), channel_id=1, source_target_pairs={{0,1},{1,0},{2,3},{3,2},{4,5},{5,4},{6,7},{7,6},{8,9},{9,8},{10,11... | collective-permute-start | bytes 786440 | tf_op jit(solution)/shard_map/ppermute | solution.py:470
  46.1 23.2 %collective-permute-start.4 = (bf16[1024,128]{1,0:T(8,128)(2,1)}, bf16[1024,128]{1,0:T(8,128)(2,1)}, u32[]{:S(2)}, u32[]{:S(2)}) collective-permute-start(bf16[1024,128]{1,0:T(8,128)(2,1)} %collective-permute-done.refs_1_), channel_id=1, source_target_pairs={{0,1},{1,0},{2,3},{3,2},{4,5},{5,4},{6,7},{7,6},{8,9},{9,8},{10,11... | collective-permute-start | bytes 786440 | tf_op jit(solution)/shard_map/ppermute | solution.py:470
  50.3 13.5 %all-to-all-start.3 = ((bf16[8,128,128]{2,1,0:T(8,128)(2,1)}), bf16[8,128,128]{2,1,0:T(8,128)(2,1)S(1)}, u32[]{:S(2)}, u32[]{:S(2)}) async-start(bf16[8,128,128]{2,1,0:T(8,128)(2,1)} %node_solve.1), calls=%async_computation.3 | async-start | bytes 524288 | tf_op jit(solution)/shard_map/all_to_all | solution.py:466
  57.5 6.3 %copy-start = (f32[1024,4,128]{2,1,0:T(4,128)S(1)}, f32[1024,4,128]{2,1,0:T(4,128)}, u32[]{:S(2)}) copy-start(f32[1024,4,128]{2,1,0:T(4,128)} %param.10) | copy-start | bytes 6291460
  57.5 6.2 %copy-start.2 = (f32[1024,64]{0,1:T(8,128)S(1)}, f32[1024,64]{0,1:T(8,128)}, u32[]{:S(2)}) copy-start(f32[1024,64]{0,1:T(8,128)} %param.7) | copy-start | bytes 786436
  63.8 13.5 %copy-start.1 = (bf16[4,1024,1024]{2,1,0:T(8,128)(2,1)S(1)}, bf16[4,1024,1024]{2,1,0:T(8,128)(2,1)}, u32[]{:S(2)}) copy-start(bf16[4,1024,1024]{2,1,0:T(8,128)(2,1)} %get-tuple-element.32.block) | copy-start | bytes 25165828
  66.1 10.5 %collective-permute-start.10 = (bf16[64,1024]{1,0:T(8,128)(2,1)S(1)}, bf16[64,1024]{1,0:T(8,128)(2,1)S(1)}, u32[]{:S(2)}, u32[]{:S(2)}) collective-permute-start(bf16[64,1024]{1,0:T(8,128)(2,1)S(1)} %get-tuple-element.27.refs_0_), channel_id=1, source_target_pairs={{0,6},{2,4},{4,2},{6,0},{1,7},{3,5},{5,3},{7,1},{8,14},{10,12},{12... | collective-permute-start | bytes 393224 | tf_op jit(solution)/shard_map/ppermute | solution.py:470
  67.4 9.3 %collective-permute-start.9 = (bf16[64,1024]{1,0:T(8,128)(2,1)S(1)}, bf16[64,1024]{1,0:T(8,128)(2,1)S(1)}, u32[]{:S(2)}, u32[]{:S(2)}) collective-permute-start(bf16[64,1024]{1,0:T(8,128)(2,1)S(1)} %get-tuple-element.27.refs_0_), channel_id=1, source_target_pairs={{0,4},{2,6},{4,0},{6,2},{1,5},{3,7},{5,1},{7,3},{8,12},{10,14},{12... | collective-permute-start | bytes 393224 | tf_op jit(solution)/shard_map/ppermute | solution.py:470
  68.2 8.4 %collective-permute-start.8 = (bf16[64,1024]{1,0:T(8,128)(2,1)S(1)}, bf16[64,1024]{1,0:T(8,128)(2,1)S(1)}, u32[]{:S(2)}, u32[]{:S(2)}) collective-permute-start(bf16[64,1024]{1,0:T(8,128)(2,1)S(1)} %get-tuple-element.27.refs_0_), channel_id=1, source_target_pairs={{0,2},{2,0},{4,6},{6,4},{1,3},{3,1},{5,7},{7,5},{8,10},{10,8},{12,... | collective-permute-start | bytes 393224 | tf_op jit(solution)/shard_map/ppermute | solution.py:470
  74.6 5.0 %collective-permute-start.7 = (bf16[64,1024]{1,0:T(8,128)(2,1)S(1)}, bf16[64,1024]{1,0:T(8,128)(2,1)S(1)}, u32[]{:S(2)}, u32[]{:S(2)}) collective-permute-start(bf16[64,1024]{1,0:T(8,128)(2,1)S(1)} %get-tuple-element.27.refs_0_), channel_id=1, source_target_pairs={{0,1},{1,0},{2,3},{3,2},{4,5},{5,4},{6,7},{7,6},{8,9},{9,8},{10,11... | collective-permute-start | bytes 393224 | tf_op jit(solution)/shard_map/ppermute | solution.py:470
  76.6 3.1 %collective-permute-start.11 = (bf16[64,1024]{1,0:T(8,128)(2,1)S(1)}, bf16[64,1024]{1,0:T(8,128)(2,1)S(1)}, u32[]{:S(2)}, u32[]{:S(2)}) collective-permute-start(bf16[64,1024]{1,0:T(8,128)(2,1)S(1)} %collective-permute-done.8.refs_1_), channel_id=1, source_target_pairs={{0,1},{1,0},{2,3},{3,2},{4,5},{5,4},{6,7},{7,6},{8,9},{9,8},{10,11... | collective-permute-start | bytes 393224 | tf_op jit(solution)/shard_map/ppermute | solution.py:470
  76.8 3.0 %collective-permute-start.12 = (bf16[64,1024]{1,0:T(8,128)(2,1)S(1)}, bf16[64,1024]{1,0:T(8,128)(2,1)S(1)}, u32[]{:S(2)}, u32[]{:S(2)}) collective-permute-start(bf16[64,1024]{1,0:T(8,128)(2,1)S(1)} %collective-permute-done.9.refs_2_), channel_id=1, source_target_pairs={{0,1},{1,0},{2,3},{3,2},{4,5},{5,4},{6,7},{7,6},{8,9},{9,8},{10,11... | collective-permute-start | bytes 393224 | tf_op jit(solution)/shard_map/ppermute | solution.py:470
  77.2 2.5 %collective-permute-start.13 = (bf16[64,1024]{1,0:T(8,128)(2,1)S(1)}, bf16[64,1024]{1,0:T(8,128)(2,1)S(1)}, u32[]{:S(2)}, u32[]{:S(2)}) collective-permute-start(bf16[64,1024]{1,0:T(8,128)(2,1)S(1)} %collective-permute-done.10.refs_3_), channel_id=1, source_target_pairs={{0,1},{1,0},{2,3},{3,2},{4,5},{5,4},{6,7},{7,6},{8,9},{9,8},{10,11... | collective-permute-start | bytes 393224 | tf_op jit(solution)/shard_map/ppermute | solution.py:470

commit v4 on v3

--- a/solution.py
+++ b/solution.py
@@ -130,7 +130,8 @@
     )(arrived, tests)
 
 
-def plane_sum_kernel(where, in_ref, send_ref, near_ref):
+def plane_sum_kernel(where, in_ref, ready, send_ref, near_ref):
+    del ready
     z = where[8]
     pair = jnp.right_shift(z, 1)
 
@@ -141,10 +142,9 @@
     below = (whole[0] + whole[1]) + (whole[2] + whole[3])
     above = (whole[4] + whole[5]) + (whole[6] + whole[7])
     send = (below + above)[:32].astype(bf16)
-    for k in range(4):
-        send_ref[k, :32] = send
-        for j in range(8):
-            send_ref[k, 32 + 32 * j : 64 + 32 * j] = in_ref[j, 128:]
+    send_ref[:32] = send
+    for j in range(8):
+        send_ref[32 + 32 * j : 64 + 32 * j] = in_ref[j, 128:]
     odd, even = 2 * jnp.bitwise_or(pair, 1), 2 * jnp.bitwise_and(pair, 2)
     near_ref[0, :40] = above[32:72]
     near_ref[1, :40] = below[32:72]
@@ -152,25 +152,28 @@
     near_ref[1, 40:] = (rows(even) + rows(even + 1))[72:]
 
 
-def plane_sum(where, arrived):
+def plane_sum(where, arrived, ready):
     return pl.pallas_call(
         plane_sum_kernel,
         grid_spec=pltpu.PrefetchScalarGridSpec(
             num_scalar_prefetch=1,
             grid=(1,),
-            in_specs=[pl.BlockSpec((8, 160, RANK), lambda i, w: (0, 0, 0))],
+            in_specs=[
+                pl.BlockSpec((8, 160, RANK), lambda i, w: (0, 0, 0)),
+                pl.BlockSpec(memory_space=pl.ANY),
+            ],
             out_specs=[
-                pl.BlockSpec((4, 288, RANK), lambda i, w: (0, 0, 0)),
+                pl.BlockSpec((288, RANK), lambda i, w: (0, 0)),
                 pl.BlockSpec((2, 96, RANK), lambda i, w: (0, 0, 0)),
             ],
         ),
         out_shape=[
-            jax.ShapeDtypeStruct((4, 288, RANK), bf16),
+            jax.ShapeDtypeStruct((288, RANK), bf16),
             jax.ShapeDtypeStruct((2, 96, RANK), f32),
         ],
         compiler_params=params(),
         name="plane_sum",
-    )(where, arrived)
+    )(where, arrived, ready)
 
 
 def factor_kernel(where, capacitance, pivots, high, low, caps, sems):
@@ -212,15 +215,16 @@
     )(where, capacitance, pivots)
 
 
-def node_kernel(where, far_ref, near_ref, high, low, out_ref):
+def node_kernel(where, near_ref, high, low, *refs):
+    far, out_ref = [ref[:32].astype(f32) for ref in refs[:4]], refs[4]
     y = where[9]
 
-    def far(index):
-        return far_ref[index, :32].astype(f32)
+    def ordered(own, other, odd):
+        return jnp.where(odd == 1, own, other), jnp.where(odd == 1, other, own)
 
     stacks = [
-        ((far(2) + far(3))[:8], (far(0) + far(1))[:8]),
-        (far(jnp.bitwise_or(y, 1))[8:], far(jnp.bitwise_and(y, 2))[8:]),
+        ordered((far[0] + far[1])[:8], (far[2] + far[3])[:8], jnp.right_shift(y, 1)),
+        ordered(far[0][8:], far[1][8:], jnp.bitwise_and(y, 1)),
         (near_ref[0, :40], near_ref[1, :40]),
         (near_ref[0, 40:], near_ref[1, 40:]),
     ]
@@ -237,12 +241,12 @@
     vmem = pl.BlockSpec(memory_space=pltpu.VMEM)
     return pl.pallas_call(
         node_kernel,
-        in_specs=[pl.BlockSpec(memory_space=pltpu.SMEM)] + [vmem] * 4,
+        in_specs=[pl.BlockSpec(memory_space=pltpu.SMEM)] + [vmem] * 7,
         out_specs=vmem,
         out_shape=jax.ShapeDtypeStruct((8, 128, RANK), bf16),
         compiler_params=params(),
         name="node_solve",
-    )(where, far, near, *factors)
+    )(where, near, *factors, *far)
 
 
 def update_kernel(
@@ -315,18 +319,22 @@
     return jnp.concatenate([points, extra.astype(bf16)], axis=1)
 
 
-def tests_kernel(in_ref, out_ref):
+def tests_kernel(where, *refs):
     for k in range(4):
-        out_ref[256 * k : 256 * k + 256] = widened(in_ref[k, 32:], 3, 0)
-
-
-def widen_tests(far):
+        at = pl.multiple_of(256 * jnp.bitwise_xor(where[9], k), 256)
+        refs[4][pl.ds(at, 256)] = widened(refs[k][32:], 3, 0)
+
+
+def widen_tests(where, far):
     return pl.pallas_call(
         tests_kernel,
+        in_specs=[pl.BlockSpec(memory_space=pltpu.SMEM)]
+        + [pl.BlockSpec(memory_space=pltpu.VMEM)] * 4,
+        out_specs=pl.BlockSpec(memory_space=pltpu.VMEM),
         out_shape=jax.ShapeDtypeStruct((1024, 2 * FEAT), bf16),
         compiler_params=params(),
         name="widen_tests",
-    )(far)
+    )(where, *far)
 
 
 SCALE = 2.0 * SPREAD / FEAT * math.log2(math.e)
@@ -487,11 +495,12 @@
     own = [own] + [flipped(own, "x", k) for k in (1, 2, 3)]
     other = [flipped(part, "core", 1) for part in own]
     planes = exchange(block_sum(arrived, test_features), "z")
-    send, near = plane_sum(where, planes)
-    far = exchange(send, "y")
-    pieces = node_solve(where, far, near, node_factors(where, capacitance, pivots))
+    factors = node_factors(where, capacitance, pivots)
+    send, near = plane_sum(where, planes, factors[0])
+    far = [send] + [flipped(send, "y", k) for k in (1, 2, 3)]
+    pieces = node_solve(where, far, near, factors)
     pieces = exchange(pieces, ("x", "core"))
-    tests = widen_tests(far)
+    tests = widen_tests(where, far)
     own_block, own_mark = kernel_block(tests, own, 51, False)
     solved, weights = update(pieces, targets_t, left, own_mark)
     weights = [weights] + [flipped(weights, "x", k) for k in (1, 2, 3)]

time: 95.8 us -> 95.4 us (level)
  waiting for transfers between devices: 9.24 us -> 5.91 us
  blocking collectives: 25.2 us -> 27.9 us
    ppermute x14 -> x17, starting transfers between devices: 13.2 us -> 21.2 us  [flipped(): lax.ppermute(value, axis, [(s, s ^ mask) for s in range(lax.axis_size(axi...]
    all_to_all x3 -> x2, starting transfers between devices: 18.6 us -> 11 us  [exchange(): return lax.all_to_all(blocks, axes, 0, 0, tiled=True)]
    all_to_all x3 -> x2, waiting for transfers between devices: 9.2 us -> 5.86 us  [exchange(): return lax.all_to_all(blocks, axes, 0, 0, tiled=True)]
    all_to_all x2, blocking collectives: 25.2 us -> 27.9 us  [exchange(): return lax.all_to_all(blocks, axes, 0, 0, tiled=True)]
  transfers between devices with their start and end apart: 17 -> 19, of which waited for: 2 -> 2; matrix products, arithmetic and copies ran while one was open for 0% -> 0% of each run, Pallas kernels for 21% -> 21%
where the time goes in v4:
time: 95.4 us; the launch traced here: 95 us
  starting transfers between devices  32.2 us (34%)
  Pallas kernels  28 us (29%)
  blocking collectives  27.9 us (29%)
  waiting for transfers between devices  5.91 us (6%)
    all_to_all x2, blocking collectives, exchange(): return lax.all_to_all(blocks, axes, 0, 0, tiled=True)  27.9 us
    ppermute x17, starting transfers between devices, flipped(): lax.ppermute(value, axis, [(s, s ^ mask) for s in range(lax.axis_size(axi...  21.2 us
    all_to_all x2, starting transfers between devices, exchange(): return lax.all_to_all(blocks, axes, 0, 0, tiled=True)  11 us
    pallas_call x2, Pallas kernels, kernel_block(): pl.pallas_call(functools.partial(block_kernel, whole=whole), in_specs=[vm...  10.1 us
    all_to_all x2, waiting for transfers between devices, exchange(): return lax.all_to_all(blocks, axes, 0, 0, tiled=True)  5.86 us
    pallas_call x2, Pallas kernels, apply_block(): pl.pallas_call(functools.partial(apply_kernel, last=last), in_specs=[pl.B...  5.06 us
    pallas_call x1, Pallas kernels, gram(): pl.pallas_call(gram_kernel, in_specs=[pl.BlockSpec(memory_space=pltpu.HBM...  3.69 us
    pallas_call x1, Pallas kernels, node_factors(): pl.pallas_call(factor_kernel, in_specs=[pl.BlockSpec(memory_space=pltpu.S...  2.53 us
  transfers between devices with their start and end apart: 19, of which 2 were waited for; matrix products, arithmetic and copies ran while one was open for 0% of the time, Pallas kernels for 21%

profile of v4, /device:TPU:1, one launch (start us, length us, event | category | flops | bytes accessed | tf_op | source)
XLA Modules:
  0.0 95.0 jit_solution(5244789369802732274)
XLA Ops:
  0.6 0.0 copy-start.5
  0.6 0.0 copy-start.4
  0.7 0.0 copy-start.3
  0.7 3.7 %gram.1 = bf16[8,128,128]{2,1,0:T(8,128)(2,1)} custom-call(f32[64,1024]{1,0:T(8,128)} %bitcast.16, f32[4096,128]{1,0:T(8,128)} %bitcast.14, f32[4096,128]{1,0:T(8,128)} %bitcast.18), custom_call_target="tpu_custom_call" | custom-call | tf_op jit(solution)/shard_map/gram/pallas_call | solution.py:96
  4.4 13.1 %all_to_all.20.in_ref = bf16[8,128,128]{2,1,0:T(8,128)(2,1)S(1)} all-to-all(bf16[8,128,128]{2,1,0:T(8,128)(2,1)} %gram.1), channel_id=1, replica_groups=mesh['y'=4,'z'=8,'x'=4,'core'=2] {'x','core'}, dimensions={0} | all-to-all | bytes 524288 | tf_op jit(solution)/shard_map/all_to_all | solution.py:474
  17.4 0.0 copy-done.4
  17.4 0.8 block_sum.1
  18.2 7.4 %all-to-all-start.1 = ((bf16[8,160,128]{2,1,0:T(8,128)(2,1)}), bf16[8,160,128]{2,1,0:T(8,128)(2,1)S(1)}, u32[]{:S(2)}, u32[]{:S(2)}) async-start(bf16[8,160,128]{2,1,0:T(8,128)(2,1)} %block_sum.1), calls=%async_computation.1 | async-start | bytes 655360 | tf_op jit(solution)/shard_map/all_to_all | solution.py:474
  25.6 0.0 copy-done.5
  25.6 1.0 %collective-permute-start.5 = (bf16[1024,128]{1,0:T(8,128)(2,1)S(1)}, bf16[1024,128]{1,0:T(8,128)(2,1)}, u32[]{:S(2)}, u32[]{:S(2)}) collective-permute-start(bf16[1024,128]{1,0:T(8,128)(2,1)S(1)} %copy-done.5), channel_id=1, source_target_pairs={{0,6},{2,4},{4,2},{6,0},{1,7},{3,5},{5,3},{7,1},{8,14},{10,12},{12... | collective-permute-start | bytes 786440 | tf_op jit(solution)/shard_map/ppermute | solution.py:478
  26.6 1.2 %collective-permute-start.4 = (bf16[1024,128]{1,0:T(8,128)(2,1)S(1)}, bf16[1024,128]{1,0:T(8,128)(2,1)}, u32[]{:S(2)}, u32[]{:S(2)}) collective-permute-start(bf16[1024,128]{1,0:T(8,128)(2,1)S(1)} %copy-done.5), channel_id=1, source_target_pairs={{0,4},{2,6},{4,0},{6,2},{1,5},{3,7},{5,1},{7,3},{8,12},{10,14},{12... | collective-permute-start | bytes 786440 | tf_op jit(solution)/shard_map/ppermute | solution.py:478
  27.8 1.2 %collective-permute-start.3 = (bf16[1024,128]{1,0:T(8,128)(2,1)S(1)}, bf16[1024,128]{1,0:T(8,128)(2,1)}, u32[]{:S(2)}, u32[]{:S(2)}) collective-permute-start(bf16[1024,128]{1,0:T(8,128)(2,1)S(1)} %copy-done.5), channel_id=1, source_target_pairs={{0,2},{2,0},{4,6},{6,4},{1,3},{3,1},{5,7},{7,5},{8,10},{10,8},{12,... | collective-permute-start | bytes 786440 | tf_op jit(solution)/shard_map/ppermute | solution.py:478
  29.0 0.1 stack.43.where
  29.1 0.0 copy-done.3
  29.1 2.5 %node_factors.1 = (bf16[4,256,128]{2,1,0:T(8,128)(2,1)S(1)}, bf16[4,256,128]{2,1,0:T(8,128)(2,1)S(1)}) custom-call(s32[10]{0:T(128)S(1)} %stack.43.where, f32[15,256,256]{2,1,0:T(8,128)} %capacitance.1, s32[15,256]{1,0:T(8,128)S(1)} %copy-done.3), custom_call_target="tpu_custom_call" | custom-call | tf_op jit(solution)/shard_map/node_factors/pallas_call | solution.py:200
  31.6 5.2 %all-to-all-done.1.in_ref = bf16[8,160,128]{2,1,0:T(8,128)(2,1)S(1)} async-done(((bf16[8,160,128]{2,1,0:T(8,128)(2,1)}), bf16[8,160,128]{2,1,0:T(8,128)(2,1)S(1)}, u32[]{:S(2)}, u32[]{:S(2)}) %all-to-all-start.1) | async-done | bytes 327712 | tf_op jit(solution)/shard_map/all_to_all | solution.py:474
  36.8 0.6 plane_sum.1
  37.4 2.8 %collective-permute-start.2 = (bf16[288,128]{1,0:T(8,128)(2,1)S(1)}, bf16[288,128]{1,0:T(8,128)(2,1)S(1)}, u32[]{:S(2)}, u32[]{:S(2)}) collective-permute-start(bf16[288,128]{1,0:T(8,128)(2,1)S(1)} %get-tuple-element.22.refs_0_), channel_id=1, source_target_pairs={{0,192},{64,128},{128,64},{192,0},{1,193},{65,129},{129,65},{193,1... | collective-permute-start | bytes 221192 | tf_op jit(solution)/shard_map/ppermute | solution.py:478
  40.2 0.3 collective-permute-start.1
  40.6 0.0 collective-permute-done.5.refs_3_
  40.6 0.3 collective-permute-start
  40.9 0.0 collective-permute-done.4.refs_2_
  40.9 3.7 %collective-permute-start.6 = (bf16[1024,128]{1,0:T(8,128)(2,1)S(1)}, bf16[1024,128]{1,0:T(8,128)(2,1)}, u32[]{:S(2)}, u32[]{:S(2)}) collective-permute-start(bf16[1024,128]{1,0:T(8,128)(2,1)S(1)} %copy-done.5), channel_id=1, source_target_pairs={{0,1},{1,0},{2,3},{3,2},{4,5},{5,4},{6,7},{7,6},{8,9},{9,8},{10,11... | collective-permute-start | bytes 786440 | tf_op jit(solution)/shard_map/ppermute | solution.py:478
  44.6 0.0 collective-permute-done.3.refs_1_
  44.6 0.1 collective-permute-start.9
  44.7 0.0 collective-permute-done.2.refs_3_
  44.7 1.7 %collective-permute-start.8 = (bf16[1024,128]{1,0:T(8,128)(2,1)}, bf16[1024,128]{1,0:T(8,128)(2,1)}, u32[]{:S(2)}, u32[]{:S(2)}) collective-permute-start(bf16[1024,128]{1,0:T(8,128)(2,1)} %collective-permute-done.4.refs_2_), channel_id=1, source_target_pairs={{0,1},{1,0},{2,3},{3,2},{4,5},{5,4},{6,7},{7,6},{8,9},{9,8},{10,11... | collective-permute-start | bytes 786440 | tf_op jit(solution)/shard_map/ppermute | solution.py:478
  46.4 0.0 collective-permute-done.1.refs_2_
  46.4 3.0 %collective-permute-start.7 = (bf16[1024,128]{1,0:T(8,128)(2,1)}, bf16[1024,128]{1,0:T(8,128)(2,1)}, u32[]{:S(2)}, u32[]{:S(2)}) collective-permute-start(bf16[1024,128]{1,0:T(8,128)(2,1)} %collective-permute-done.3.refs_1_), channel_id=1, source_target_pairs={{0,1},{1,0},{2,3},{3,2},{4,5},{5,4},{6,7},{7,6},{8,9},{9,8},{10,11... | collective-permute-start | bytes 786440 | tf_op jit(solution)/shard_map/ppermute | solution.py:478
  49.4 0.0 collective-permute-done.refs_1_
  49.4 1.5 %node_solve.1 = bf16[8,128,128]{2,1,0:T(8,128)(2,1)} custom-call(s32[10]{0:T(128)S(1)} %stack.43.where, f32[2,96,128]{2,1,0:T(8,128)S(1)} %get-tuple-element.20.near_ref, bf16[4,256,128]{2,1,0:T(8,128)(2,1)S(1)} %get-tuple-element.19.ready.high, bf16[4,256,128]{2,1,0:T(8,128)(2,1)S(1)} %get-tuple-element.21.low, ...), custom_call_target="tpu_custom_call" | custom-call | tf_op jit(solution)/shard_map/node_solve/pallas_call | solution.py:242
  50.9 3.5 %all-to-all-start.2 = ((bf16[8,128,128]{2,1,0:T(8,128)(2,1)}), bf16[8,128,128]{2,1,0:T(8,128)(2,1)S(1)}, u32[]{:S(2)}, u32[]{:S(2)}) async-start(bf16[8,128,128]{2,1,0:T(8,128)(2,1)} %node_solve.1), calls=%async_computation.2 | async-start | bytes 524288 | tf_op jit(solution)/shard_map/all_to_all | solution.py:474
  54.4 0.8 widen_tests.1.tests
  55.2 0.0 copy-start
  55.3 0.0 copy-start.2
  55.3 4.8 %kernel_block.2 = (bf16[4,1024,1024]{2,1,0:T(8,128)(2,1)}, f32[8,128]{1,0:T(8,128)S(1)}) custom-call(bf16[1024,256]{1,0:T(8,128)(2,1)S(1)} %widen_tests.1.tests, bf16[1024,128]{1,0:T(8,128)(2,1)S(1)} %copy-done.5, bf16[1024,128]{1,0:T(8,128)(2,1)} %collective-permute-done.3.refs_1_, bf16[1024,128]{1,0:T(8,128)(2,1)} %collective-permute-done.4.refs_2_, ...), custom_call_target="tpu_custom_call" | custom-call | flops 2147483648 | bytes 10485760 | tf_op jit(solution)/shard_map/kernel_block/pallas_call | solution.py:377
  60.1 0.6 all-to-all-done.2.pieces_ref
  60.7 0.0 copy-done
  60.7 0.0 copy-done.2
  60.7 2.3 %update.1 = (f32[64,1024]{1,0:T(8,128)}, bf16[64,1024]{1,0:T(8,128)(2,1)S(1)}) custom-call(bf16[8,128,128]{2,1,0:T(8,128)(2,1)S(1)} %all-to-all-done.2.pieces_ref, f32[64,1024]{1,0:T(8,128)S(1)} %bitcast.17, f32[4096,128]{1,0:T(8,128)S(1)} %bitcast.15, f32[8,128]{1,0:T(8,128)S(1)} %get-tuple-element.24.mark), custom_call_target="tpu_custom_call" | custom-call | tf_op jit(solution)/shard_map/update/pallas_call | solution.py:283
  63.1 1.8 %collective-permute-start.13 = (bf16[64,1024]{1,0:T(8,128)(2,1)S(1)}, bf16[64,1024]{1,0:T(8,128)(2,1)S(1)}, u32[]{:S(2)}, u32[]{:S(2)}) collective-permute-start(bf16[64,1024]{1,0:T(8,128)(2,1)S(1)} %get-tuple-element.27.refs_0_), channel_id=1, source_target_pairs={{0,6},{2,4},{4,2},{6,0},{1,7},{3,5},{5,3},{7,1},{8,14},{10,12},{12... | collective-permute-start | bytes 393224 | tf_op jit(solution)/shard_map/ppermute | solution.py:478
  64.9 0.0 collective-permute-done.6.refs_0_
  64.9 0.5 collective-permute-start.12
  65.4 0.0 collective-permute-done.9.refs_3_
  65.4 0.9 collective-permute-start.11
  66.3 0.0 collective-permute-done.8.refs_2_
  66.3 0.0 collective-permute-done.7.refs_1_
  66.3 5.3 %kernel_block.3 = (bf16[4,1024,1024]{2,1,0:T(8,128)(2,1)S(1)}, f32[8,128]{1,0:T(8,128)S(1)}) custom-call(bf16[1024,256]{1,0:T(8,128)(2,1)S(1)} %widen_tests.1.tests, bf16[1024,128]{1,0:T(8,128)(2,1)} %collective-permute-done.6.refs_0_, bf16[1024,128]{1,0:T(8,128)(2,1)} %collective-permute-done.7.refs_1_, bf16[1024,128]{1,0:T(8,128)(2,1)} %collective-permute-done.8.refs_2_, ...), custom_call_target="tpu_custom_call" | custom-call | flops 2147483648 | bytes 10485760 | tf_op jit(solution)/shard_map/kernel_block/pallas_call | solution.py:377
  71.6 1.9 %collective-permute-start.10 = (bf16[64,1024]{1,0:T(8,128)(2,1)S(1)}, bf16[64,1024]{1,0:T(8,128)(2,1)S(1)}, u32[]{:S(2)}, u32[]{:S(2)}) collective-permute-start(bf16[64,1024]{1,0:T(8,128)(2,1)S(1)} %get-tuple-element.27.refs_0_), channel_id=1, source_target_pairs={{0,1},{1,0},{2,3},{3,2},{4,5},{5,4},{6,7},{7,6},{8,9},{9,8},{10,11... | collective-permute-start | bytes 393224 | tf_op jit(solution)/shard_map/ppermute | solution.py:478
  73.5 0.0 collective-permute-done.13.refs_3_
  73.6 0.0 collective-permute-done.12.refs_2_
  73.6 0.0 collective-permute-done.11.refs_1_
  73.6 0.1 collective-permute-start.14
  73.7 0.5 collective-permute-start.15
  74.2 0.1 collective-permute-start.16
  74.3 0.0 copy-done.1
  74.3 2.4 %apply_block.2.refs_4_ = f32[64,1024]{1,0:T(8,128)S(1)} custom-call(bf16[4,1024,1024]{2,1,0:T(8,128)(2,1)S(1)} %copy-done.1, bf16[64,1024]{1,0:T(8,128)(2,1)S(1)} %get-tuple-element.27.refs_0_, bf16[64,1024]{1,0:T(8,128)(2,1)S(1)} %collective-permute-done.11.refs_1_, bf16[64,1024]{1,0:T(8,128)(2,1)S(1)} %collective-permute-done.12.refs_2_, ...), custom_call_target="tpu_custom_call" | custom-call | flops 2147483648 | bytes 9437184 | tf_op jit(solution)/shard_map/apply_block/pallas_call | solution.py:439
  76.6 0.0 collective-permute-done.10.refs_0_
  76.6 0.0 collective-permute-done.14.refs_1_
  76.7 0.0 collective-permute-done.15.refs_2_
  76.7 0.0 collective-permute-done.16.refs_3_
  76.7 2.7 %apply_block.3 = bf16[32,16,128]{2,1,0:T(8,128)(2,1)S(1)} custom-call(bf16[4,1024,1024]{2,1,0:T(8,128)(2,1)S(1)} %get-tuple-element.26.block, bf16[64,1024]{1,0:T(8,128)(2,1)S(1)} %collective-permute-done.10.refs_0_, bf16[64,1024]{1,0:T(8,128)(2,1)S(1)} %collective-permute-done.14.refs_1_, bf16[64,1024]{1,0:T(8,128)(2,1)S(1)} %collective-permute-done.15.refs_2_, ...), custom_call_target="tpu_custom_call" | custom-call | flops 2147483648 | bytes 9437184 | tf_op jit(solution)/shard_map/apply_block/pallas_call | solution.py:439
  79.4 14.9 %all_to_all.21.in_ref = bf16[32,16,128]{2,1,0:T(8,128)(2,1)S(1)} all-to-all(bf16[32,16,128]{2,1,0:T(8,128)(2,1)S(1)} %apply_block.3), channel_id=1, replica_groups=mesh['y'=4,'z'=8,'x'=4,'core'=2] {'y','z'}, dimensions={0} | all-to-all | bytes 262144 | tf_op jit(solution)/shard_map/all_to_all | solution.py:474
  94.3 0.7 final_sum.1
  (1 shorter events, 0.0 us)
Async XLA Ops:
  0.6 25.0 %copy-start.5 = (bf16[1024,128]{1,0:T(8,128)(2,1)S(1)}, bf16[1024,128]{1,0:T(8,128)(2,1)}, u32[]{:S(2)}) copy-start(bf16[1024,128]{1,0:T(8,128)(2,1)} %refs_0_) | copy-start | bytes 786436
  0.6 16.8 %copy-start.4 = (bf16[32,128]{1,0:T(8,128)(2,1)S(1)}, bf16[32,128]{1,0:T(8,128)(2,1)}, u32[]{:S(2)}) copy-start(bf16[32,128]{1,0:T(8,128)(2,1)} %tests_ref.1) | copy-start | bytes 24580
  0.7 28.4 %copy-start.3 = (s32[15,256]{1,0:T(8,128)S(1)}, s32[15,256]{1,0:T(8,128)}, u32[]{:S(2)}) copy-start(s32[15,256]{1,0:T(8,128)} %pivots.1) | copy-start | bytes 46084
  18.2 18.7 %all-to-all-start.1 = ((bf16[8,160,128]{2,1,0:T(8,128)(2,1)}), bf16[8,160,128]{2,1,0:T(8,128)(2,1)S(1)}, u32[]{:S(2)}, u32[]{:S(2)}) async-start(bf16[8,160,128]{2,1,0:T(8,128)(2,1)} %block_sum.1), calls=%async_computation.1 | async-start | bytes 655360 | tf_op jit(solution)/shard_map/all_to_all | solution.py:474
  25.6 15.0 %collective-permute-start.5 = (bf16[1024,128]{1,0:T(8,128)(2,1)S(1)}, bf16[1024,128]{1,0:T(8,128)(2,1)}, u32[]{:S(2)}, u32[]{:S(2)}) collective-permute-start(bf16[1024,128]{1,0:T(8,128)(2,1)S(1)} %copy-done.5), channel_id=1, source_target_pairs={{0,6},{2,4},{4,2},{6,0},{1,7},{3,5},{5,3},{7,1},{8,14},{10,12},{12... | collective-permute-start | bytes 786440 | tf_op jit(solution)/shard_map/ppermute | solution.py:478
  26.6 14.3 %collective-permute-start.4 = (bf16[1024,128]{1,0:T(8,128)(2,1)S(1)}, bf16[1024,128]{1,0:T(8,128)(2,1)}, u32[]{:S(2)}, u32[]{:S(2)}) collective-permute-start(bf16[1024,128]{1,0:T(8,128)(2,1)S(1)} %copy-done.5), channel_id=1, source_target_pairs={{0,4},{2,6},{4,0},{6,2},{1,5},{3,7},{5,1},{7,3},{8,12},{10,14},{12... | collective-permute-start | bytes 786440 | tf_op jit(solution)/shard_map/ppermute | solution.py:478
  27.8 16.8 %collective-permute-start.3 = (bf16[1024,128]{1,0:T(8,128)(2,1)S(1)}, bf16[1024,128]{1,0:T(8,128)(2,1)}, u32[]{:S(2)}, u32[]{:S(2)}) collective-permute-start(bf16[1024,128]{1,0:T(8,128)(2,1)S(1)} %copy-done.5), channel_id=1, source_target_pairs={{0,2},{2,0},{4,6},{6,4},{1,3},{3,1},{5,7},{7,5},{8,10},{10,8},{12,... | collective-permute-start | bytes 786440 | tf_op jit(solution)/shard_map/ppermute | solution.py:478
  37.4 7.3 %collective-permute-start.2 = (bf16[288,128]{1,0:T(8,128)(2,1)S(1)}, bf16[288,128]{1,0:T(8,128)(2,1)S(1)}, u32[]{:S(2)}, u32[]{:S(2)}) collective-permute-start(bf16[288,128]{1,0:T(8,128)(2,1)S(1)} %get-tuple-element.22.refs_0_), channel_id=1, source_target_pairs={{0,192},{64,128},{128,64},{192,0},{1,193},{65,129},{129,65},{193,1... | collective-permute-start | bytes 221192 | tf_op jit(solution)/shard_map/ppermute | solution.py:478
  40.2 6.2 %collective-permute-start.1 = (bf16[288,128]{1,0:T(8,128)(2,1)S(1)}, bf16[288,128]{1,0:T(8,128)(2,1)S(1)}, u32[]{:S(2)}, u32[]{:S(2)}) collective-permute-start(bf16[288,128]{1,0:T(8,128)(2,1)S(1)} %get-tuple-element.22.refs_0_), channel_id=1, source_target_pairs={{0,128},{64,192},{128,0},{192,64},{1,129},{65,193},{129,1},{193,65... | collective-permute-start | bytes 221192 | tf_op jit(solution)/shard_map/ppermute | solution.py:478
  40.6 8.8 %collective-permute-start = (bf16[288,128]{1,0:T(8,128)(2,1)S(1)}, bf16[288,128]{1,0:T(8,128)(2,1)S(1)}, u32[]{:S(2)}, u32[]{:S(2)}) collective-permute-start(bf16[288,128]{1,0:T(8,128)(2,1)S(1)} %get-tuple-element.22.refs_0_), channel_id=1, source_target_pairs={{0,64},{64,0},{128,192},{192,128},{1,65},{65,1},{129,193},{193,129... | collective-permute-start | bytes 221192 | tf_op jit(solution)/shard_map/ppermute | solution.py:478
  40.9 23.9 %collective-permute-start.6 = (bf16[1024,128]{1,0:T(8,128)(2,1)S(1)}, bf16[1024,128]{1,0:T(8,128)(2,1)}, u32[]{:S(2)}, u32[]{:S(2)}) collective-permute-start(bf16[1024,128]{1,0:T(8,128)(2,1)S(1)} %copy-done.5), channel_id=1, source_target_pairs={{0,1},{1,0},{2,3},{3,2},{4,5},{5,4},{6,7},{7,6},{8,9},{9,8},{10,11... | collective-permute-start | bytes 786440 | tf_op jit(solution)/shard_map/ppermute | solution.py:478
  44.6 20.8 %collective-permute-start.9 = (bf16[1024,128]{1,0:T(8,128)(2,1)}, bf16[1024,128]{1,0:T(8,128)(2,1)}, u32[]{:S(2)}, u32[]{:S(2)}) collective-permute-start(bf16[1024,128]{1,0:T(8,128)(2,1)} %collective-permute-done.5.refs_3_), channel_id=1, source_target_pairs={{0,1},{1,0},{2,3},{3,2},{4,5},{5,4},{6,7},{7,6},{8,9},{9,8},{10,11... | collective-permute-start | bytes 786440 | tf_op jit(solution)/shard_map/ppermute | solution.py:478
  44.7 21.6 %collective-permute-start.8 = (bf16[1024,128]{1,0:T(8,128)(2,1)}, bf16[1024,128]{1,0:T(8,128)(2,1)}, u32[]{:S(2)}, u32[]{:S(2)}) collective-permute-start(bf16[1024,128]{1,0:T(8,128)(2,1)} %collective-permute-done.4.refs_2_), channel_id=1, source_target_pairs={{0,1},{1,0},{2,3},{3,2},{4,5},{5,4},{6,7},{7,6},{8,9},{9,8},{10,11... | collective-permute-start | bytes 786440 | tf_op jit(solution)/shard_map/ppermute | solution.py:478
  46.4 19.9 %collective-permute-start.7 = (bf16[1024,128]{1,0:T(8,128)(2,1)}, bf16[1024,128]{1,0:T(8,128)(2,1)}, u32[]{:S(2)}, u32[]{:S(2)}) collective-permute-start(bf16[1024,128]{1,0:T(8,128)(2,1)} %collective-permute-done.3.refs_1_), channel_id=1, source_target_pairs={{0,1},{1,0},{2,3},{3,2},{4,5},{5,4},{6,7},{7,6},{8,9},{9,8},{10,11... | collective-permute-start | bytes 786440 | tf_op jit(solution)/shard_map/ppermute | solution.py:478
  50.9 9.8 %all-to-all-start.2 = ((bf16[8,128,128]{2,1,0:T(8,128)(2,1)}), bf16[8,128,128]{2,1,0:T(8,128)(2,1)S(1)}, u32[]{:S(2)}, u32[]{:S(2)}) async-start(bf16[8,128,128]{2,1,0:T(8,128)(2,1)} %node_solve.1), calls=%async_computation.2 | async-start | bytes 524288 | tf_op jit(solution)/shard_map/all_to_all | solution.py:474
  55.2 5.5 %copy-start = (f32[1024,4,128]{2,1,0:T(4,128)S(1)}, f32[1024,4,128]{2,1,0:T(4,128)}, u32[]{:S(2)}) copy-start(f32[1024,4,128]{2,1,0:T(4,128)} %param.10) | copy-start | bytes 6291460
  55.3 5.5 %copy-start.2 = (f32[1024,64]{0,1:T(8,128)S(1)}, f32[1024,64]{0,1:T(8,128)}, u32[]{:S(2)}) copy-start(f32[1024,64]{0,1:T(8,128)} %param.7) | copy-start | bytes 786436
  60.7 13.5 %copy-start.1 = (bf16[4,1024,1024]{2,1,0:T(8,128)(2,1)S(1)}, bf16[4,1024,1024]{2,1,0:T(8,128)(2,1)}, u32[]{:S(2)}) copy-start(bf16[4,1024,1024]{2,1,0:T(8,128)(2,1)} %get-tuple-element.32.block) | copy-start | bytes 25165828
  63.1 10.5 %collective-permute-start.13 = (bf16[64,1024]{1,0:T(8,128)(2,1)S(1)}, bf16[64,1024]{1,0:T(8,128)(2,1)S(1)}, u32[]{:S(2)}, u32[]{:S(2)}) collective-permute-start(bf16[64,1024]{1,0:T(8,128)(2,1)S(1)} %get-tuple-element.27.refs_0_), channel_id=1, source_target_pairs={{0,6},{2,4},{4,2},{6,0},{1,7},{3,5},{5,3},{7,1},{8,14},{10,12},{12... | collective-permute-start | bytes 393224 | tf_op jit(solution)/shard_map/ppermute | solution.py:478
  64.9 8.7 %collective-permute-start.12 = (bf16[64,1024]{1,0:T(8,128)(2,1)S(1)}, bf16[64,1024]{1,0:T(8,128)(2,1)S(1)}, u32[]{:S(2)}, u32[]{:S(2)}) collective-permute-start(bf16[64,1024]{1,0:T(8,128)(2,1)S(1)} %get-tuple-element.27.refs_0_), channel_id=1, source_target_pairs={{0,4},{2,6},{4,0},{6,2},{1,5},{3,7},{5,1},{7,3},{8,12},{10,14},{12... | collective-permute-start | bytes 393224 | tf_op jit(solution)/shard_map/ppermute | solution.py:478
  65.4 8.2 %collective-permute-start.11 = (bf16[64,1024]{1,0:T(8,128)(2,1)S(1)}, bf16[64,1024]{1,0:T(8,128)(2,1)S(1)}, u32[]{:S(2)}, u32[]{:S(2)}) collective-permute-start(bf16[64,1024]{1,0:T(8,128)(2,1)S(1)} %get-tuple-element.27.refs_0_), channel_id=1, source_target_pairs={{0,2},{2,0},{4,6},{6,4},{1,3},{3,1},{5,7},{7,5},{8,10},{10,8},{12,... | collective-permute-start | bytes 393224 | tf_op jit(solution)/shard_map/ppermute | solution.py:478
  71.6 5.0 %collective-permute-start.10 = (bf16[64,1024]{1,0:T(8,128)(2,1)S(1)}, bf16[64,1024]{1,0:T(8,128)(2,1)S(1)}, u32[]{:S(2)}, u32[]{:S(2)}) collective-permute-start(bf16[64,1024]{1,0:T(8,128)(2,1)S(1)} %get-tuple-element.27.refs_0_), channel_id=1, source_target_pairs={{0,1},{1,0},{2,3},{3,2},{4,5},{5,4},{6,7},{7,6},{8,9},{9,8},{10,11... | collective-permute-start | bytes 393224 | tf_op jit(solution)/shard_map/ppermute | solution.py:478
  73.6 3.1 %collective-permute-start.14 = (bf16[64,1024]{1,0:T(8,128)(2,1)S(1)}, bf16[64,1024]{1,0:T(8,128)(2,1)S(1)}, u32[]{:S(2)}, u32[]{:S(2)}) collective-permute-start(bf16[64,1024]{1,0:T(8,128)(2,1)S(1)} %collective-permute-done.11.refs_1_), channel_id=1, source_target_pairs={{0,1},{1,0},{2,3},{3,2},{4,5},{5,4},{6,7},{7,6},{8,9},{9,8},{10,11... | collective-permute-start | bytes 393224 | tf_op jit(solution)/shard_map/ppermute | solution.py:478
  73.7 3.0 %collective-permute-start.15 = (bf16[64,1024]{1,0:T(8,128)(2,1)S(1)}, bf16[64,1024]{1,0:T(8,128)(2,1)S(1)}, u32[]{:S(2)}, u32[]{:S(2)}) collective-permute-start(bf16[64,1024]{1,0:T(8,128)(2,1)S(1)} %collective-permute-done.12.refs_2_), channel_id=1, source_target_pairs={{0,1},{1,0},{2,3},{3,2},{4,5},{5,4},{6,7},{7,6},{8,9},{9,8},{10,11... | collective-permute-start | bytes 393224 | tf_op jit(solution)/shard_map/ppermute | solution.py:478
  74.2 2.5 %collective-permute-start.16 = (bf16[64,1024]{1,0:T(8,128)(2,1)S(1)}, bf16[64,1024]{1,0:T(8,128)(2,1)S(1)}, u32[]{:S(2)}, u32[]{:S(2)}) collective-permute-start(bf16[64,1024]{1,0:T(8,128)(2,1)S(1)} %collective-permute-done.13.refs_3_), channel_id=1, source_target_pairs={{0,1},{1,0},{2,3},{3,2},{4,5},{5,4},{6,7},{7,6},{8,9},{9,8},{10,11... | collective-permute-start | bytes 393224 | tf_op jit(solution)/shard_map/ppermute | solution.py:478
